TPU v7x, 32 devices: a whole 2x2x4 slice. The times are simulated.
32 devices in a mesh: path: 2 (over core), dp: 16 (over z, y, x).
Axes of the slice: x: 2, y: 2, z: 4, core: 2. Of those that a mesh axis runs over, the one named last changes fastest.
Arguments:
- acts: bfloat16 [2, 16, 16, 16, 4096], P('path', 'dp'), may hold values from -12 to 12
- cotangent: bfloat16 [2, 16, 16, 16, 4096], P('path', 'dp'), may hold values from -6 to 6
- clip_res: int32 [16], P('dp'), may hold values from 0 to 3, as said below
- w_slow_a: bfloat16 [1280, 256], replicated, may hold values from -0.15625 to 0.15625
- w_slow_b: bfloat16 [9, 256, 256], replicated, may hold values from -0.125 to 0.125
- w_slow_c: bfloat16 [256, 1024], replicated, may hold values from -0.375 to 0.375
- w_slow_proj: bfloat16 [1280, 1024], replicated, may hold values from -0.15625 to 0.15625
- slow_gain: float32 [2560], replicated, may hold values from 0.1 to 1.9
- slow_bias: float32 [2560], replicated, may hold values from -3 to 3
- w_fast_a: bfloat16 [3, 128, 32], replicated, may hold values from -0.3125 to 0.3125
- w_fast_b: bfloat16 [9, 32, 32], replicated, may hold values from -0.375 to 0.375
- w_fast_c: bfloat16 [32, 128], replicated, may hold values from -1 to 1
- w_lateral: bfloat16 [5, 128, 256], replicated, may hold values from -0.25 to 0.25
- fast_gain: float32 [192], replicated, may hold values from 0.1 to 1.9
- fast_bias: float32 [192], replicated, may hold values from -3 to 3
Outputs:
- out: bfloat16 [2, 16, 16, 16, 4096], P('path', 'dp')
- in_grad: bfloat16 [2, 16, 16, 16, 4096], P('path', 'dp')
- param_grads: float32 [2685312], P(('path', 'dp'))
Inputs may be any that keep to these rules, and one draw needn't show every extreme that they name: `clip_res`: level of each clip slot: 0 an empty slot; 1, 2, 3 a clip whose valid pixels are the top-left square of side 16 * 5 // 8, 14 or 16.
All inputs are finite; a program needn't handle non-finite values.
Results may differ from a plain program's by a relative error of at most 0.0085.
Values may be sent and summed in bfloat16 or wider, within the bound.
No kernel may reach another device: no remote copies, remote signals or barrier semaphores. Data moves between devices by JAX's collectives and lax.ppermute only.
A program may use at most 256 MiB of HBM per device.

v0:
```python
import jax
import jax.numpy as jnp
from jax import lax
from jax.sharding import PartitionSpec as P

TS = 4
ALPHA = 8
CS = 1024
CS_MID = 256
CF = 128
CF_MID = 32
TF = 32


epsilon = 1e-05


def shifted(block, axis, distance):
    devices = range(lax.axis_size(axis))
    route = [(i - distance, i) for i in devices if i - distance in devices]
    return lax.ppermute(block, axis, route)


def region_mask(levels, grid):
    sides = jnp.where(
        levels == 1,
        grid * 5 // 8,
        jnp.where(levels == 2, grid * 7 // 8, jnp.where(levels == 3, grid, 0)),
    )
    rows = lax.broadcasted_iota(jnp.int32, (levels.shape[0], grid, grid), 1)
    columns = lax.broadcasted_iota(jnp.int32, (levels.shape[0], grid, grid), 2)
    inside = jnp.logical_and(rows < sides[:, None, None], columns < sides[:, None, None])
    return jnp.where(inside, 1.0, 0.0).astype(jnp.float32)


def gelu_tanh(values):
    return jax.nn.gelu(values, approximate=True)


def activation_slope(values):
    pullback = jax.vjp(gelu_tanh, values)[1]
    return pullback(jnp.ones_like(values))[0]


def on_path(active, work, operands):

    def skipped(inner):
        return jax.tree.map(jnp.zeros_like, work(inner))

    return lax.cond(active, work, skipped, operands)


def product(features, kernel):
    return jnp.einsum("chwti,io->chwto", features, kernel, preferred_element_type=jnp.float32)


def product_grads(features, gradient, kernel):
    d_features = jnp.einsum("chwto,io->chwti", gradient, kernel, preferred_element_type=jnp.float32)
    d_kernel = jnp.einsum("chwti,chwto->io", features, gradient, preferred_element_type=jnp.float32)
    return (d_features, d_kernel)


def pair_forward(operands):
    joined, kernel_main, kernel_short = operands
    return (product(joined, kernel_main), product(joined, kernel_short))


def pair_backward(operands):
    joined, grad_main, grad_short, kernel_main, kernel_short = operands
    d_main, k_main = product_grads(joined, grad_main, kernel_main)
    d_short, k_short = product_grads(joined, grad_short, kernel_short)
    return (d_main + d_short, k_main, k_short)


def time_forward(operands):
    features, kernel = operands
    frames = features.shape[3]
    padded = jnp.pad(features, ((0, 0), (0, 0), (0, 0), (1, 1), (0, 0)))
    running_total = product(padded[:, :, :, 0:frames], kernel[0])
    for offset in range(1, 3):
        running_total = running_total + product(
            padded[:, :, :, offset : offset + frames], kernel[offset]
        )
    return running_total


def time_backward(operands):
    features, gradient, kernel = operands
    frames = features.shape[3]
    pad_spec = ((0, 0), (0, 0), (0, 0), (1, 1), (0, 0))
    padded = jnp.pad(features, pad_spec)
    grad_pad = jnp.pad(gradient, pad_spec)
    d_features = jnp.zeros(features.shape, jnp.float32)
    kernels = []
    for offset in range(3):
        d_features = d_features + jnp.einsum(
            "chwto,io->chwti",
            grad_pad[:, :, :, 2 - offset : 2 - offset + frames],
            kernel[offset],
            preferred_element_type=jnp.float32,
        )
        kernels.append(
            jnp.einsum(
                "chwti,chwto->io",
                padded[:, :, :, offset : offset + frames],
                gradient,
                preferred_element_type=jnp.float32,
            )
        )
    return (d_features, jnp.stack(kernels))


def space_forward(operands):
    features, kernel = operands
    height = features.shape[1]
    width = features.shape[2]
    padded = jnp.pad(features, ((0, 0), (1, 1), (1, 1), (0, 0), (0, 0)))
    running_total = product(padded[:, 0:height, 0:width], kernel[0])
    for offset in range(1, 9):
        shift_rows = offset // 3
        shift_cols = offset % 3
        running_total = running_total + product(
            padded[:, shift_rows : shift_rows + height, shift_cols : shift_cols + width],
            kernel[offset],
        )
    return running_total


def space_backward(operands):
    features, gradient, kernel = operands
    height = features.shape[1]
    width = features.shape[2]
    pad_spec = ((0, 0), (1, 1), (1, 1), (0, 0), (0, 0))
    padded = jnp.pad(features, pad_spec)
    grad_pad = jnp.pad(gradient, pad_spec)
    d_features = jnp.zeros(features.shape, jnp.float32)
    kernels = []
    for offset in range(9):
        shift_rows = offset // 3
        shift_cols = offset % 3
        moved = grad_pad[
            :, 2 - shift_rows : 2 - shift_rows + height, 2 - shift_cols : 2 - shift_cols + width
        ]
        d_features = d_features + jnp.einsum(
            "chwto,io->chwti", moved, kernel[offset], preferred_element_type=jnp.float32
        )
        kernels.append(
            jnp.einsum(
                "chwti,chwto->io",
                padded[:, shift_rows : shift_rows + height, shift_cols : shift_cols + width],
                gradient,
                preferred_element_type=jnp.float32,
            )
        )
    return (d_features, jnp.stack(kernels))


def lateral_stack(features):
    padded = jnp.pad(features, ((0, 0), (0, 0), (0, 0), (2, 2), (0, 0)))
    return jnp.stack(
        [padded[:, :, :, offset : offset + ALPHA * TS : ALPHA] for offset in range(5)], axis=4
    )


def lateral_forward(operands):
    stacked, kernel = operands
    return jnp.einsum("chwtki,kio->chwto", stacked, kernel, preferred_element_type=jnp.float32)


def lateral_backward(operands):
    stacked, gradient, kernel = operands
    d_stacked = jnp.einsum(
        "chwto,kio->chwtki", gradient, kernel, preferred_element_type=jnp.float32
    )
    d_kernel = jnp.einsum(
        "chwtki,chwto->kio", stacked, gradient, preferred_element_type=jnp.float32
    )
    return (d_stacked, d_kernel)


def lateral_spread(d_stacked):
    shape = d_stacked.shape
    filled = jnp.pad(d_stacked, ((0, 0), (0, 0), (0, 0), (0, 0), (0, ALPHA - 5), (0, 0)))
    merged = filled.reshape(shape[0], shape[1], shape[2], TS * ALPHA, shape[5])
    return jnp.pad(merged[:, :, :, 2:], ((0, 0), (0, 0), (0, 0), (0, 2), (0, 0)))


def partial_sums(values, valid_region):
    return jnp.sum(values * valid_region, axis=(0, 1, 2, 3))


def split_parts(vector, widths):
    pieces = []
    start = 0
    for width in widths:
        pieces.append(vector[start : start + width])
        start = start + width
    return pieces


def normalized_output(value, mean, inverse_scale):
    return (value - mean) * inverse_scale


def activate(value, mean, inverse_scale, norm_gain, shift, valid_region):
    return (
        gelu_tanh(normalized_output(value, mean, inverse_scale) * norm_gain + shift) * valid_region
    ).astype(jnp.bfloat16)


def moments(active, values, valid_region, valid_count):
    widths = [value.shape[-1] for value in values]

    def plain_sums(inner):
        return jnp.concatenate([partial_sums(value, valid_region) for value in inner])

    sums = on_path(active, plain_sums, tuple(values))
    means = lax.psum(sums, "dp") / valid_count

    def deviation_sums(inner):
        inner_values, inner_means = inner
        parts = []
        for value, mean in zip(inner_values, inner_means):
            centered = value - mean
            parts.append(partial_sums(centered * centered, valid_region))
        return jnp.concatenate(parts)

    deviations = on_path(active, deviation_sums, (tuple(values), tuple(split_parts(means, widths))))
    spreads = lax.psum(deviations, "dp") / valid_count
    scales = lax.rsqrt(spreads + epsilon)
    return (split_parts(means, widths), split_parts(scales, widths))


def backward_sum_pair(gradient_list, standardized_list, valid_region):
    bias_gradient_terms = jnp.concatenate(
        [partial_sums(item_gradient, valid_region) for item_gradient in gradient_list]
    )
    gain_gradient_terms = jnp.concatenate(
        [
            partial_sums(item_gradient * standardized, valid_region)
            for item_gradient, standardized in zip(gradient_list, standardized_list)
        ]
    )
    return (bias_gradient_terms, gain_gradient_terms)


def global_terms(bias_gradient_terms, gain_gradient_terms):
    return lax.psum((bias_gradient_terms, gain_gradient_terms), "dp")


def norm_gradient(
    result_gradient,
    standardized,
    norm_gain,
    inverse_scale,
    bias_gradient_sum,
    gain_gradient_sum,
    valid_region,
    valid_count,
):
    return (
        norm_gain
        * inverse_scale
        * (
            result_gradient
            - valid_region * (bias_gradient_sum + standardized * gain_gradient_sum) / valid_count
        )
    ).astype(jnp.bfloat16)


def local(
    acts,
    cotangent,
    clip_res,
    w_slow_a,
    w_slow_b,
    w_slow_c,
    w_slow_proj,
    slow_gain,
    slow_bias,
    w_fast_a,
    w_fast_b,
    w_fast_c,
    w_lateral,
    fast_gain,
    fast_bias,
):
    clips = acts.shape[1]
    grid = acts.shape[2]
    flat_shape = (clips, grid, grid, TS * CS)
    is_fast = lax.axis_index("path") == 1
    is_slow = jnp.logical_not(is_fast)
    valid_region = region_mask(clip_res, grid)[:, :, :, None, None]
    pixels = lax.psum(jnp.sum(valid_region), "dp")
    slow_count = pixels * TS
    fast_count = pixels * TF
    fast_in = acts[0].reshape(clips, grid, grid, TF, CF)
    slow_in = acts[0].reshape(clips, grid, grid, TS, CS)
    fast_first_gain, fast_second_gain, fast_third_gain = split_parts(
        fast_gain, [CF_MID, CF_MID, CF]
    )
    fast_first_bias, fast_second_bias, fast_third_bias = split_parts(
        fast_bias, [CF_MID, CF_MID, CF]
    )
    slow_first_gain, slow_second_gain, slow_third_gain, slow_projection_gain = split_parts(
        slow_gain, [CS_MID, CS_MID, CS, CS]
    )
    slow_first_bias, slow_second_bias, slow_third_bias, slow_projection_bias = split_parts(
        slow_bias, [CS_MID, CS_MID, CS, CS]
    )
    fast_a = on_path(is_fast, time_forward, (fast_in, w_fast_a))
    (fast_first_mean,), (fast_first_scale,) = moments(is_fast, [fast_a], valid_region, fast_count)

    def fast_second(inner):
        value, kernel = inner
        hidden = activate(
            value, fast_first_mean, fast_first_scale, fast_first_gain, fast_first_bias, valid_region
        )
        return (hidden, space_forward((hidden, kernel)))

    hid_f1, fast_b = on_path(is_fast, fast_second, (fast_a, w_fast_b))
    (fast_second_mean,), (fast_second_scale,) = moments(is_fast, [fast_b], valid_region, fast_count)

    def fast_third(inner):
        value, kernel = inner
        hidden = activate(
            value,
            fast_second_mean,
            fast_second_scale,
            fast_second_gain,
            fast_second_bias,
            valid_region,
        )
        return (hidden, product(hidden, kernel))

    hid_f2, fast_c = on_path(is_fast, fast_third, (fast_b, w_fast_c))
    (fast_third_mean,), (fast_third_scale,) = moments(is_fast, [fast_c], valid_region, fast_count)

    def fast_finish(inner):
        value, input_list, kernel = inner
        running_total = (
            normalized_output(value, fast_third_mean, fast_third_scale) * fast_third_gain
            + fast_third_bias
            + input_list.astype(jnp.float32)
        )
        rounded = (gelu_tanh(running_total) * valid_region).astype(jnp.bfloat16)
        stacked = lateral_stack(rounded)
        return (rounded.reshape(flat_shape), stacked.reshape(clips, grid, grid, TS * 5 * CF))

    fast_flat, handed = on_path(is_fast, fast_finish, (fast_c, fast_in, w_lateral))
    received = shifted(handed, "path", -1).reshape(clips, grid, grid, TS, 5, CF)
    lateral_in = on_path(is_slow, lateral_forward, (received, w_lateral)).astype(jnp.bfloat16)

    def slow_first(inner):
        input_list, lateral, kernel_main, kernel_short = inner
        return pair_forward(
            (jnp.concatenate([input_list, lateral], axis=4), kernel_main, kernel_short)
        )

    slow_a, slow_p = on_path(is_slow, slow_first, (slow_in, lateral_in, w_slow_a, w_slow_proj))
    (slow_first_mean, slow_projection_mean), (slow_first_scale, slow_projection_scale) = moments(
        is_slow, [slow_a, slow_p], valid_region, slow_count
    )

    def slow_second(inner):
        value, kernel = inner
        hidden = activate(
            value, slow_first_mean, slow_first_scale, slow_first_gain, slow_first_bias, valid_region
        )
        return (hidden, space_forward((hidden, kernel)))

    hid_s1, slow_b = on_path(is_slow, slow_second, (slow_a, w_slow_b))
    (slow_second_mean,), (slow_second_scale,) = moments(is_slow, [slow_b], valid_region, slow_count)

    def slow_third(inner):
        value, kernel = inner
        hidden = activate(
            value,
            slow_second_mean,
            slow_second_scale,
            slow_second_gain,
            slow_second_bias,
            valid_region,
        )
        return (hidden, product(hidden, kernel))

    hid_s2, slow_c = on_path(is_slow, slow_third, (slow_b, w_slow_c))
    (slow_third_mean,), (slow_third_scale,) = moments(is_slow, [slow_c], valid_region, slow_count)

    def slow_top(inner):
        third_value, projection_value, cot = inner
        third_standardized = normalized_output(third_value, slow_third_mean, slow_third_scale)
        projection_standardized = normalized_output(
            projection_value, slow_projection_mean, slow_projection_scale
        )
        running_total = (
            third_standardized * slow_third_gain
            + slow_third_bias
            + projection_standardized * slow_projection_gain
            + slow_projection_bias
        )
        result = (gelu_tanh(running_total) * valid_region).astype(jnp.bfloat16).reshape(flat_shape)
        total_gradient = (
            cot.reshape(clips, grid, grid, TS, CS).astype(jnp.float32)
            * valid_region
            * activation_slope(running_total)
        )
        bias_gradient_terms, gain_gradient_terms = backward_sum_pair(
            [total_gradient, total_gradient],
            [third_standardized, projection_standardized],
            valid_region,
        )
        return (result, total_gradient, bias_gradient_terms, gain_gradient_terms)

    slow_flat, d_sum_s, bias_t3, gain_t3 = on_path(
        is_slow, slow_top, (slow_c, slow_p, cotangent[0])
    )
    bias_all3, gain_all3 = global_terms(bias_t3, gain_t3)
    bias_c3, bias_p3 = split_parts(bias_all3, [CS, CS])
    gain_c3, gain_p3 = split_parts(gain_all3, [CS, CS])

    def slow_down_c(inner):
        total_gradient, third_value, projection_value, hidden, kernel, second_value = inner
        d_c = norm_gradient(
            total_gradient,
            normalized_output(third_value, slow_third_mean, slow_third_scale),
            slow_third_gain,
            slow_third_scale,
            bias_c3,
            gain_c3,
            valid_region,
            slow_count,
        )
        d_p = norm_gradient(
            total_gradient,
            normalized_output(projection_value, slow_projection_mean, slow_projection_scale),
            slow_projection_gain,
            slow_projection_scale,
            bias_p3,
            gain_p3,
            valid_region,
            slow_count,
        )
        hidden_gradient, k_grad = product_grads(hidden, d_c, kernel)
        second_standardized = normalized_output(second_value, slow_second_mean, slow_second_scale)
        preactivation_gradient = (
            hidden_gradient
            * valid_region
            * activation_slope(second_standardized * slow_second_gain + slow_second_bias)
        )
        bias_gradient_terms, gain_gradient_terms = backward_sum_pair(
            [preactivation_gradient], [second_standardized], valid_region
        )
        return (d_p, k_grad, preactivation_gradient, bias_gradient_terms, gain_gradient_terms)

    d_slow_p, grad_w_sc, d_pre_s2, bias_t2, gain_t2 = on_path(
        is_slow, slow_down_c, (d_sum_s, slow_c, slow_p, hid_s2, w_slow_c, slow_b)
    )
    bias_all2, gain_all2 = global_terms(bias_t2, gain_t2)

    def slow_down_b(inner):
        preactivation_gradient, second_value, hidden, kernel, first_value = inner
        d_b = norm_gradient(
            preactivation_gradient,
            normalized_output(second_value, slow_second_mean, slow_second_scale),
            slow_second_gain,
            slow_second_scale,
            bias_all2,
            gain_all2,
            valid_region,
            slow_count,
        )
        hidden_gradient, k_grad = space_backward((hidden, d_b, kernel))
        first_standardized = normalized_output(first_value, slow_first_mean, slow_first_scale)
        next_gradient = (
            hidden_gradient
            * valid_region
            * activation_slope(first_standardized * slow_first_gain + slow_first_bias)
        )
        bias_gradient_terms, gain_gradient_terms = backward_sum_pair(
            [next_gradient], [first_standardized], valid_region
        )
        return (k_grad, next_gradient, bias_gradient_terms, gain_gradient_terms)

    grad_w_sb, d_pre_s1, bias_t1, gain_t1 = on_path(
        is_slow, slow_down_b, (d_pre_s2, slow_b, hid_s1, w_slow_b, slow_a)
    )
    bias_all1, gain_all1 = global_terms(bias_t1, gain_t1)

    def slow_down_a(inner):
        preactivation_gradient, first_value, input_list, lateral, d_p, kernel_main, kernel_short = (
            inner
        )
        d_a = norm_gradient(
            preactivation_gradient,
            normalized_output(first_value, slow_first_mean, slow_first_scale),
            slow_first_gain,
            slow_first_scale,
            bias_all1,
            gain_all1,
            valid_region,
            slow_count,
        )
        joined = jnp.concatenate([input_list, lateral], axis=4)
        d_joined, k_main, k_short = pair_backward((joined, d_a, d_p, kernel_main, kernel_short))
        d_input = d_joined[:, :, :, :, 0:CS].astype(jnp.bfloat16).reshape(flat_shape)
        return (d_input, d_joined[:, :, :, :, CS:].astype(jnp.bfloat16), k_main, k_short)

    slow_grad_flat, d_lateral, grad_w_sa, grad_w_sp = on_path(
        is_slow,
        slow_down_a,
        (d_pre_s1, slow_a, slow_in, lateral_in, d_slow_p, w_slow_a, w_slow_proj),
    )
    d_taps, grad_w_lat = on_path(is_slow, lateral_backward, (received, d_lateral, w_lateral))
    d_flat = shifted(
        d_taps.reshape(clips, grid, grid, TS * 5 * CF).astype(jnp.bfloat16), "path", 1
    ).astype(jnp.float32)
    d_stacked = d_flat.reshape(clips, grid, grid, TS, 5, CF)

    def fast_top(inner):
        d_taps_in, third_value, input_list, cot = inner
        third_standardized = normalized_output(third_value, fast_third_mean, fast_third_scale)
        running_total = (
            third_standardized * fast_third_gain + fast_third_bias + input_list.astype(jnp.float32)
        )
        d_out = cot.reshape(clips, grid, grid, TF, CF).astype(jnp.float32) + lateral_spread(
            d_taps_in
        )
        total_gradient = d_out * valid_region * activation_slope(running_total)
        bias_gradient_terms, gain_gradient_terms = backward_sum_pair(
            [total_gradient], [third_standardized], valid_region
        )
        return (total_gradient, bias_gradient_terms, gain_gradient_terms)

    d_sum_f, bias_tf3, gain_tf3 = on_path(
        is_fast, fast_top, (d_stacked, fast_c, fast_in, cotangent[0])
    )
    bias_allf3, gain_allf3 = global_terms(bias_tf3, gain_tf3)

    def fast_down_c(inner):
        total_gradient, third_value, hidden, kernel, second_value = inner
        d_c = norm_gradient(
            total_gradient,
            normalized_output(third_value, fast_third_mean, fast_third_scale),
            fast_third_gain,
            fast_third_scale,
            bias_allf3,
            gain_allf3,
            valid_region,
            fast_count,
        )
        hidden_gradient, k_grad = product_grads(hidden, d_c, kernel)
        second_standardized = normalized_output(second_value, fast_second_mean, fast_second_scale)
        preactivation_gradient = (
            hidden_gradient
            * valid_region
            * activation_slope(second_standardized * fast_second_gain + fast_second_bias)
        )
        bias_gradient_terms, gain_gradient_terms = backward_sum_pair(
            [preactivation_gradient], [second_standardized], valid_region
        )
        return (k_grad, preactivation_gradient, bias_gradient_terms, gain_gradient_terms)

    grad_w_fc, d_pre_f2, bias_tf2, gain_tf2 = on_path(
        is_fast, fast_down_c, (d_sum_f, fast_c, hid_f2, w_fast_c, fast_b)
    )
    bias_allf2, gain_allf2 = global_terms(bias_tf2, gain_tf2)

    def fast_down_b(inner):
        preactivation_gradient, second_value, hidden, kernel, first_value = inner
        d_b = norm_gradient(
            preactivation_gradient,
            normalized_output(second_value, fast_second_mean, fast_second_scale),
            fast_second_gain,
            fast_second_scale,
            bias_allf2,
            gain_allf2,
            valid_region,
            fast_count,
        )
        hidden_gradient, k_grad = space_backward((hidden, d_b, kernel))
        first_standardized = normalized_output(first_value, fast_first_mean, fast_first_scale)
        next_gradient = (
            hidden_gradient
            * valid_region
            * activation_slope(first_standardized * fast_first_gain + fast_first_bias)
        )
        bias_gradient_terms, gain_gradient_terms = backward_sum_pair(
            [next_gradient], [first_standardized], valid_region
        )
        return (k_grad, next_gradient, bias_gradient_terms, gain_gradient_terms)

    grad_w_fb, d_pre_f1, bias_tf1, gain_tf1 = on_path(
        is_fast, fast_down_b, (d_pre_f2, fast_b, hid_f1, w_fast_b, fast_a)
    )
    bias_allf1, gain_allf1 = global_terms(bias_tf1, gain_tf1)

    def fast_down_a(inner):
        preactivation_gradient, first_value, input_list, kernel, total_gradient = inner
        d_a = norm_gradient(
            preactivation_gradient,
            normalized_output(first_value, fast_first_mean, fast_first_scale),
            fast_first_gain,
            fast_first_scale,
            bias_allf1,
            gain_allf1,
            valid_region,
            fast_count,
        )
        d_conv, k_grad = time_backward((input_list, d_a, kernel))
        return ((total_gradient + d_conv).astype(jnp.bfloat16).reshape(flat_shape), k_grad)

    fast_grad_flat, grad_w_fa = on_path(
        is_fast, fast_down_a, (d_pre_f1, fast_a, fast_in, w_fast_a, d_sum_f)
    )
    out = jnp.where(is_fast, fast_flat, slow_flat)
    in_grad = jnp.where(is_fast, fast_grad_flat, slow_grad_flat)
    slow_gains = jnp.concatenate([gain_t1, gain_t2, gain_t3])
    slow_biases = jnp.concatenate([bias_t1, bias_t2, bias_t3])
    fast_gains = jnp.concatenate([gain_tf1, gain_tf2, gain_tf3])
    fast_biases = jnp.concatenate([bias_tf1, bias_tf2, bias_tf3])
    terms = jnp.concatenate(
        [
            grad_w_sa.reshape(-1),
            grad_w_sb.reshape(-1),
            grad_w_sc.reshape(-1),
            grad_w_sp.reshape(-1),
            slow_gains,
            slow_biases,
            grad_w_fa.reshape(-1),
            grad_w_fb.reshape(-1),
            grad_w_fc.reshape(-1),
            grad_w_lat.reshape(-1),
            fast_gains,
            fast_biases,
        ]
    )
    param_grads = lax.psum_scatter(terms, ("path", "dp"), scatter_dimension=0, tiled=True)
    return (out[None], in_grad[None], param_grads)


def solution(mesh):
    in_specs = (
        P("path", "dp", None, None, None),
        P("path", "dp", None, None, None),
        P("dp"),
        P(),
        P(),
        P(),
        P(),
        P(),
        P(),
        P(),
        P(),
        P(),
        P(),
        P(),
        P(),
    )
    out_specs = (
        P("path", "dp", None, None, None),
        P("path", "dp", None, None, None),
        P(("path", "dp")),
    )
    return jax.shard_map(local, mesh=mesh, in_specs=in_specs, out_specs=out_specs, check_vma=False)
```

profile of v0, /device:TPU:0, one launch (start us, length us, event | category | flops | bytes accessed | tf_op | source)
XLA Modules:
  0.0 1411.9 jit_solution(10332758320632946531)
XLA Ops:
  15.6 44.1 %all-reduce.19 = (f32[32]{0:T(128)S(1)}, f32[]{:T(128)}) all-reduce(f32[32]{0:T(128)S(1)} %get-tuple-element.1299, f32[]{:T(128)} %select_reduce_fusion), channel_id=1, replica_groups=mesh['path'=2,'dp'=16] {'dp'}, use_global_device_ids=true, to_apply=%region_5.6 | all-reduce | flops 33 | bytes 264 | tf_op jit(solution)/shard_map/psum | solution.py:218
  60.4 36.6 %psum.177 = f32[32]{0:T(128)S(1)} all-reduce(f32[32]{0:T(128)S(1)} %get-tuple-element.1300), channel_id=1, replica_groups=mesh['path'=2,'dp'=16] {'dp'}, use_global_device_ids=true, to_apply=%region_11.12 | all-reduce | flops 32 | bytes 256 | tf_op jit(solution)/shard_map/psum | solution.py:229
  101.9 38.6 %psum.178 = f32[32]{0:T(128)S(1)} all-reduce(f32[32]{0:T(128)S(1)} %get-tuple-element.1301), channel_id=1, replica_groups=mesh['path'=2,'dp'=16] {'dp'}, use_global_device_ids=true, to_apply=%region_17.18 | all-reduce | flops 32 | bytes 256 | tf_op jit(solution)/shard_map/psum | solution.py:218
  140.5 36.6 %psum.179 = f32[32]{0:T(128)S(1)} all-reduce(f32[32]{0:T(128)S(1)} %get-tuple-element.1302), channel_id=1, replica_groups=mesh['path'=2,'dp'=16] {'dp'}, use_global_device_ids=true, to_apply=%region_21.22 | all-reduce | flops 32 | bytes 256 | tf_op jit(solution)/shard_map/psum | solution.py:229
  182.1 38.6 %psum.180 = f32[128]{0:T(128)S(1)} all-reduce(f32[128]{0:T(128)S(1)} %get-tuple-element.1303), channel_id=1, replica_groups=mesh['path'=2,'dp'=16] {'dp'}, use_global_device_ids=true, to_apply=%region_27.28 | all-reduce | flops 128 | bytes 1024 | tf_op jit(solution)/shard_map/psum | solution.py:218
  221.2 36.5 %psum.181 = f32[128]{0:T(128)S(1)} all-reduce(f32[128]{0:T(128)S(1)} %get-tuple-element.1304), channel_id=1, replica_groups=mesh['path'=2,'dp'=16] {'dp'}, use_global_device_ids=true, to_apply=%region_31.32 | all-reduce | flops 128 | bytes 1024 | tf_op jit(solution)/shard_map/psum | solution.py:229
  266.6 85.1 %collective-permute-done = bf16[1,16,16,2560]{3,2,1,0:T(8,128)(2,1)} collective-permute-done((bf16[1,16,16,2560]{3,2,1,0:T(8,128)(2,1)}, bf16[1,16,16,2560]{3,2,1,0:T(8,128)(2,1)}, u32[]{:S(2)}, u32[]{:S(2)}) %collective-permute-start) | collective-permute-done | bytes 1310752 | tf_op jit(solution)/shard_map/ppermute | solution.py:21
  370.8 38.8 %psum.182 = f32[1280]{0:T(1024)S(1)} all-reduce(f32[1280]{0:T(1024)S(1)} %get-tuple-element.1306), channel_id=1, replica_groups=mesh['path'=2,'dp'=16] {'dp'}, use_global_device_ids=true, to_apply=%region_42.43 | all-reduce | flops 1280 | bytes 10240 | tf_op jit(solution)/shard_map/psum | solution.py:218
  416.7 37.4 %psum.183 = f32[1280]{0:T(1024)S(1)} all-reduce(f32[1280]{0:T(1024)S(1)} %get-tuple-element.1307), channel_id=1, replica_groups=mesh['path'=2,'dp'=16] {'dp'}, use_global_device_ids=true, to_apply=%region_47.48 | all-reduce | flops 1280 | bytes 10240 | tf_op jit(solution)/shard_map/psum | solution.py:229
  468.5 38.3 %psum.184 = f32[256]{0:T(256)S(1)} all-reduce(f32[256]{0:T(256)S(1)} %get-tuple-element.1308), channel_id=1, replica_groups=mesh['path'=2,'dp'=16] {'dp'}, use_global_device_ids=true, to_apply=%region_53.54 | all-reduce | flops 256 | bytes 2048 | tf_op jit(solution)/shard_map/psum | solution.py:218
  507.6 36.8 %psum.185 = f32[256]{0:T(256)S(1)} all-reduce(f32[256]{0:T(256)S(1)} %get-tuple-element.1309), channel_id=1, replica_groups=mesh['path'=2,'dp'=16] {'dp'}, use_global_device_ids=true, to_apply=%region_57.58 | all-reduce | flops 256 | bytes 2048 | tf_op jit(solution)/shard_map/psum | solution.py:229
  556.1 38.3 %psum.186 = f32[1024]{0:T(1024)S(1)} all-reduce(f32[1024]{0:T(1024)S(1)} %get-tuple-element.1310), channel_id=1, replica_groups=mesh['path'=2,'dp'=16] {'dp'}, use_global_device_ids=true, to_apply=%region_63.64 | all-reduce | flops 1024 | bytes 8192 | tf_op jit(solution)/shard_map/psum | solution.py:218
  600.8 36.8 %psum.187 = f32[1024]{0:T(1024)S(1)} all-reduce(f32[1024]{0:T(1024)S(1)} %get-tuple-element.1311), channel_id=1, replica_groups=mesh['path'=2,'dp'=16] {'dp'}, use_global_device_ids=true, to_apply=%region_67.68 | all-reduce | flops 1024 | bytes 8192 | tf_op jit(solution)/shard_map/psum | solution.py:229
  637.6 30.6 %conditional.49 = (bf16[1,16,16,4096]{3,2,1,0:T(8,128)(2,1)}, f32[1,16,16,4,1024]{4,3,2,1,0:T(4,128)}, f32[2048]{0:T(1024)S(1)}, f32[2048]{0:T(1024)S(1)}) conditional(s32[]{:T(128)} %convert_element_type.157, () %tuple.250, (f32[1024]{0:T(1024)S(1)}, f32[1,16,16,4,1024]{4,2,3,1,0:T(8,128)}, f32[1024]{0:T(1024)S(1)}, f32[1024]{0:T(1024)S(1)}, ...), branch_computations={%region_68.69_spmd, %region_69.73_spmd} | conditional | flops 48235520 | bytes 37840928 | solution.py:50
  668.1 73.4 %all-reduce.18 = (f32[2048]{0:T(1024)S(1)}, f32[2048]{0:T(1024)S(1)}) all-reduce(f32[2048]{0:T(1024)S(1)} %get-tuple-element.696, f32[2048]{0:T(1024)S(1)} %get-tuple-element.697), channel_id=1, replica_groups=mesh['path'=2,'dp'=16] {'dp'}, use_global_device_ids=true, to_apply=%region_74.75 | all-reduce | flops 4096 | bytes 32768 | tf_op jit(solution)/shard_map/psum | solution.py:248
  757.3 36.6 %all-reduce.17 = (f32[256]{0:T(256)S(1)}, f32[256]{0:T(256)S(1)}) all-reduce(f32[256]{0:T(256)S(1)} %get-tuple-element.700, f32[256]{0:T(256)S(1)} %get-tuple-element.701), channel_id=1, replica_groups=mesh['path'=2,'dp'=16] {'dp'}, use_global_device_ids=true, to_apply=%region_80.81 | all-reduce | flops 512 | bytes 4096 | tf_op jit(solution)/shard_map/psum | solution.py:248
  793.8 23.2 %conditional.51 = (f32[1,16,16,4,256]{4,2,3,1,0:T(8,128)}, f32[256]{0:T(256)S(1)}, f32[256]{0:T(256)S(1)}, f32[589824]{0:T(1024)}) conditional(s32[]{:T(128)} %convert_element_type.157, () %tuple.278, (f32[256]{0:T(256)S(1)}, f32[256]{0:T(256)S(1)}, f32[1,16,16,1,1]{2,1,4,3,0:T(8,128)S(1)}, f32[256]{0:T(256)S(1)}, f32[256]{0:T(256)S(1)}, ...), branch_computations={%region_81.82_spmd, %region_82.85_spmd} | conditional | flops 2427715328 | bytes 48659520 | solution.py:50
  817.1 38.5 %all-reduce.16 = (f32[256]{0:T(256)S(1)}, f32[256]{0:T(256)S(1)}) all-reduce(f32[256]{0:T(256)S(1)} %get-tuple-element.704, f32[256]{0:T(256)S(1)} %get-tuple-element.705), channel_id=1, replica_groups=mesh['path'=2,'dp'=16] {'dp'}, use_global_device_ids=true, to_apply=%region_86.87 | all-reduce | flops 512 | bytes 4096 | tf_op jit(solution)/shard_map/psum | solution.py:248
  855.6 20.6 %conditional.52 = (bf16[1,16,16,4096]{3,2,1,0:T(8,128)(2,1)}, bf16[1,16,16,4,256]{4,2,3,1,0:T(8,128)(2,1)S(1)}, f32[327680]{0:T(1024)S(1)}, f32[1310720]{0:T(1024)}) conditional(s32[]{:T(128)} %convert_element_type.157, () %tuple.277, (f32[256]{0:T(256)S(1)}, f32[256]{0:T(256)S(1)}, f32[1,16,16,1,1]{2,1,4,3,0:T(8,128)S(1)}, f32[256]{0:T(256)S(1)}, ...), branch_computations={%region_87.88_spmd, %region_88.89_spmd} | conditional | flops 6726352896 | bytes 75900024 | solution.py:50
  896.4 36.6 %all-reduce.15 = (f32[128]{0:T(128)S(1)}, f32[128]{0:T(128)S(1)}) all-reduce(f32[128]{0:T(128)S(1)} %get-tuple-element.710, f32[128]{0:T(128)S(1)} %get-tuple-element.711), channel_id=1, replica_groups=mesh['path'=2,'dp'=16] {'dp'}, use_global_device_ids=true, to_apply=%region_96.97 | all-reduce | flops 256 | bytes 2048 | tf_op jit(solution)/shard_map/psum | solution.py:248
  935.6 38.6 %all-reduce.14 = (f32[32]{0:T(128)S(1)}, f32[32]{0:T(128)S(1)}) all-reduce(f32[32]{0:T(128)S(1)} %get-tuple-element.714, f32[32]{0:T(128)S(1)} %get-tuple-element.715), channel_id=1, replica_groups=mesh['path'=2,'dp'=16] {'dp'}, use_global_device_ids=true, to_apply=%region_102.103 | all-reduce | flops 64 | bytes 512 | tf_op jit(solution)/shard_map/psum | solution.py:248
  982.6 36.6 %all-reduce.13 = (f32[32]{0:T(128)S(1)}, f32[32]{0:T(128)S(1)}) all-reduce(f32[32]{0:T(128)S(1)} %get-tuple-element.718, f32[32]{0:T(128)S(1)} %get-tuple-element.719), channel_id=1, replica_groups=mesh['path'=2,'dp'=16] {'dp'}, use_global_device_ids=true, to_apply=%region_108.109 | all-reduce | flops 64 | bytes 512 | tf_op jit(solution)/shard_map/psum | solution.py:248
  1020.8 89.7 %concatenate.21 = f32[2685312]{0:T(1024)} concatenate(f32[327680]{0:T(1024)} %copy-done.14, f32[589824]{0:T(1024)} %get-tuple-element.724, f32[262144]{0:T(1024)S(1)} %copy-done.18, f32[1310720]{0:T(1024)} %get-tuple-element.726, f32[256]{0:T(256)S(1)} %copy-done.56, f32[256]{0:T(256)S(1)} %copy-done.52, f32[2048]{0:T(1024)S(1)} %copy-done.36, f32[256]{0:T(256)S(1)} %copy-done.54, ...), dimensions={0} | concatenate | bytes 21482496 | tf_op jit(solution)/shard_map/concatenate | solution.py:622
  1116.8 286.2 %all-reduce.22.cloned.1.call-done = f32[2685312]{0:T(1024)} async-done(((f32[2685312]{0:T(1024)}), f32[2685312]{0:T(1024)}) %all-reduce.22.cloned.1.call-update) | async-done | bytes 10741264
  (282 shorter events, 306.9 us)
Async XLA Ops:
  7.2 1395.8 %all-reduce.22.cloned.1.call-start = ((), (), s32[]{:S(2)}) async-start(), calls=%async_computation | async-start | bytes 21487616
  9.3 249.0 %copy-start.57 = (f32[128]{0:T(128)}, f32[128]{0:T(128)S(1)}, u32[]{:S(2)}) copy-start(f32[128]{0:T(128)S(1)} %slice.401) | copy-start | bytes 1540
  10.1 87.4 %copy-start.43 = (f32[32]{0:T(128)}, f32[32]{0:T(128)S(1)}, u32[]{:S(2)}) copy-start(f32[32]{0:T(128)S(1)} %get-tuple-element.1206) | copy-start | bytes 388
  10.1 87.4 %copy-start.45 = (f32[32]{0:T(128)}, f32[32]{0:T(128)S(1)}, u32[]{:S(2)}) copy-start(f32[32]{0:T(128)S(1)} %get-tuple-element.1203) | copy-start | bytes 388
  10.1 167.5 %copy-start.61 = (f32[32]{0:T(128)}, f32[32]{0:T(128)S(1)}, u32[]{:S(2)}) copy-start(f32[32]{0:T(128)S(1)} %get-tuple-element.1207) | copy-start | bytes 388
  10.1 167.5 %copy-start.63 = (f32[32]{0:T(128)}, f32[32]{0:T(128)S(1)}, u32[]{:S(2)}) copy-start(f32[32]{0:T(128)S(1)} %get-tuple-element.1202) | copy-start | bytes 388
  10.9 247.4 %copy-start.59 = (f32[128]{0:T(128)}, f32[128]{0:T(128)S(1)}, u32[]{:S(2)}) copy-start(f32[128]{0:T(128)S(1)} %slice.402) | copy-start | bytes 1540
  12.9 245.4 %copy-start.5 = (bf16[32,8,32,128]{3,2,1,0:T(8,128)(2,1)}, bf16[32,8,32,128]{3,2,1,0:T(8,128)(2,1)S(1)}, u32[]{:S(2)}) copy-start(bf16[32,8,32,128]{3,2,1,0:T(8,128)(2,1)S(1)} %copy.249) | copy-start | bytes 6291460
  15.6 81.9 %copy-start.29 = (bf16[9,32,32]{2,1,0:T(8,128)(2,1)S(1)}, bf16[9,32,32]{2,1,0:T(8,128)(2,1)}, u32[]{:S(2)}) copy-start(bf16[9,32,32]{2,1,0:T(8,128)(2,1)} %param.83) | copy-start | bytes 55300
  99.9 77.7 %copy-start.39 = (bf16[32,128]{1,0:T(8,128)(2,1)S(1)}, bf16[32,128]{1,0:T(8,128)(2,1)}, u32[]{:S(2)}) copy-start(bf16[32,128]{1,0:T(8,128)(2,1)} %param.84) | copy-start | bytes 24580
  261.1 94.8 %copy-start.27 = (bf16[5,128,256]{2,1,0:T(8,128)(2,1)S(1)}, bf16[5,128,256]{2,1,0:T(8,128)(2,1)}, u32[]{:S(2)}) copy-start(bf16[5,128,256]{2,1,0:T(8,128)(2,1)} %param.85) | copy-start | bytes 983044
  261.1 90.6 %collective-permute-start = (bf16[1,16,16,2560]{3,2,1,0:T(8,128)(2,1)}, bf16[1,16,16,2560]{3,2,1,0:T(8,128)(2,1)}, u32[]{:S(2)}, u32[]{:S(2)}) collective-permute-start(bf16[1,16,16,2560]{3,2,1,0:T(8,128)(2,1)} %get-tuple-element.690), channel_id=1, source_target_pairs={{16,0},{17,1},{18,2},{19,3},{20,4},{21,5},{22,6},{23,7},{24,8},{25... | collective-permute-start | bytes 3932168 | tf_op jit(solution)/shard_map/ppermute | solution.py:21
  265.9 93.5 %copy-start.10 = (bf16[1,16,16,4,1024]{4,3,2,1,0:T(4,128)(2,1)}, bf16[1,16,16,4,1024]{4,3,2,1,0:T(4,128)(2,1)S(1)}, u32[]{:S(2)}) copy-start(bf16[1,16,16,4,1024]{4,3,2,1,0:T(4,128)(2,1)S(1)} %reshape_squeeze.9) | copy-start | bytes 6291460
  668.1 73.4 %copy-start.33 = (f32[2048]{0:T(1024)}, f32[2048]{0:T(1024)S(1)}, u32[]{:S(2)}) copy-start(f32[2048]{0:T(1024)S(1)} %get-tuple-element.696) | copy-start | bytes 24580
  668.1 73.4 %copy-start.35 = (f32[2048]{0:T(1024)}, f32[2048]{0:T(1024)S(1)}, u32[]{:S(2)}) copy-start(f32[2048]{0:T(1024)S(1)} %get-tuple-element.697) | copy-start | bytes 24580
  887.9 4.1 collective-permute-start.1
  893.9 39.1 %copy-start.40 = (bf16[32,128]{1,0:T(8,128)(2,1)S(1)}, bf16[32,128]{1,0:T(8,128)(2,1)}, u32[]{:S(2)}) copy-start(bf16[32,128]{1,0:T(8,128)(2,1)} %param.84) | copy-start | bytes 24580
  893.9 39.1 %copy-start.48 = (f32[32]{0:T(128)S(1)}, f32[32]{0:T(128)}, u32[]{:S(2)}) copy-start(f32[32]{0:T(128)} %copy-done.47) | copy-start | bytes 388
  893.9 39.1 %copy-start.62 = (f32[32]{0:T(128)S(1)}, f32[32]{0:T(128)}, u32[]{:S(2)}) copy-start(f32[32]{0:T(128)} %copy-done.61) | copy-start | bytes 388
  933.0 41.1 %copy-start.30 = (bf16[9,32,32]{2,1,0:T(8,128)(2,1)S(1)}, bf16[9,32,32]{2,1,0:T(8,128)(2,1)}, u32[]{:S(2)}) copy-start(bf16[9,32,32]{2,1,0:T(8,128)(2,1)} %param.83) | copy-start | bytes 55300
  933.0 41.1 %copy-start.42 = (f32[32]{0:T(128)S(1)}, f32[32]{0:T(128)}, u32[]{:S(2)}) copy-start(f32[32]{0:T(128)} %copy-done.41) | copy-start | bytes 388
  933.0 41.1 %copy-start.44 = (f32[32]{0:T(128)S(1)}, f32[32]{0:T(128)}, u32[]{:S(2)}) copy-start(f32[32]{0:T(128)} %copy-done.43) | copy-start | bytes 388
  933.1 41.1 %copy-start.46 = (f32[32]{0:T(128)S(1)}, f32[32]{0:T(128)}, u32[]{:S(2)}) copy-start(f32[32]{0:T(128)} %copy-done.45) | copy-start | bytes 388
  974.2 45.0 %copy-start.32 = (bf16[3,128,32]{1,2,0:T(8,128)(2,1)S(1)}, bf16[3,128,32]{1,2,0:T(8,128)(2,1)}, u32[]{:S(2)}) copy-start(bf16[3,128,32]{1,2,0:T(8,128)(2,1)} %param.82) | copy-start | bytes 73732
  (37 other events, 420.1 us)
Sparse Core Ops, SparseCore 0:
  1110.7 292.2 all-reduce.21
where the time goes:
time: 1420 us; the launch traced here: 1410 us
  blocking collectives  718 us (51%)
  waiting for transfers between devices  374 us (26%)
  local copies, waits for them, and re-layouts  162 us (11%)
  other arithmetic  69.5 us (5%)
  matrix products  60.8 us (4%)
  between operations  16.8 us (1%)
    unnamed x2, waiting for transfers between devices  286 us
    psum x6, blocking collectives, global_terms(): return lax.psum((bias_gradient_terms, gain_gradient_terms), 'dp')  260 us
    psum x6, blocking collectives, moments(): means = lax.psum(sums, 'dp') / valid_count  237 us
    psum x6, blocking collectives, moments(): spreads = lax.psum(deviations, 'dp') / valid_count  221 us
    concatenate x1, local copies, waits for them, and re-layouts, local(): jnp.concatenate([grad_w_sa.reshape(-1), grad_w_sb.reshape(-1), grad_w_sc....  89.7 us
    ppermute x2, waiting for transfers between devices, shifted(): return lax.ppermute(block, axis, route)  87.9 us
    reduce_sum x9, other arithmetic, partial_sums(): return jnp.sum(values * valid_region, axis=(0, 1, 2, 3))  40.1 us
  transfers between devices with their start and end apart: 3, of which 3 were waited for; matrix products, arithmetic and copies ran while one was open for 1% of the time, Pallas kernels for 0%

commit v1 on v0

v1 whole, which is shorter than its diff:
```python
import functools

import jax
import jax.numpy as jnp
from jax import lax
from jax.experimental import pallas as pl
from jax.experimental.pallas import tpu as pltpu
from jax.sharding import PartitionSpec as P

TS = 4
ALPHA = 8
CS = 1024
CS_MID = 256
CF = 128
CF_MID = 32
LAT = 256
TF = 32
LN = 128
EPS = 1e-05
GELU_C = 0.7978845608028654
GELU_A = 0.044715

F32 = jnp.float32
BF16 = jnp.bfloat16
SWAP = [(0, 1), (1, 0)]

ROW_SA = 0
ROW_SB = ROW_SA + (CS + LAT) * CS_MID // LN
ROW_SC = ROW_SB + 9 * CS_MID * CS_MID // LN
ROW_SP = ROW_SC + CS_MID * CS // LN
ROW_SG = ROW_SP + (CS + LAT) * CS // LN
SLOW_VEC = (2 * CS_MID + 2 * CS) // LN
ROW_FA = ROW_SG + 2 * SLOW_VEC
ROW_LAT = ROW_FA + (3 * CF * CF_MID + 9 * CF_MID * CF_MID + CF_MID * CF) // LN
ROW_FG = ROW_LAT + 5 * CF * LAT // LN
ROWS = ROW_FG + 3


def dot(a, b):
    return lax.dot_general(a, b, (((1,), (0,)), ((), ())), preferred_element_type=F32)


def dot_t(a, b):
    return lax.dot_general(a, b, (((1,), (1,)), ((), ())), preferred_element_type=F32)


def call(body, outs, scratch, *args, smem=1, limit=48):
    one = not isinstance(outs, list)
    shapes = [jax.ShapeDtypeStruct(s, d) for s, d in ([outs] if one else outs)]
    specs = [pl.BlockSpec(memory_space=pltpu.SMEM)] * smem
    specs += [pl.BlockSpec(memory_space=pltpu.VMEM)] * (len(args) - smem)
    res = pl.pallas_call(
        body,
        out_shape=shapes,
        in_specs=specs,
        out_specs=[pl.BlockSpec(memory_space=pltpu.VMEM)] * len(shapes),
        scratch_shapes=scratch,
        compiler_params=pltpu.CompilerParams(vmem_limit_bytes=limit * 1024 * 1024),
    )(*args)
    return res[0] if one else res


def empty(shape, dtype):
    def body(out_ref):
        pass

    return pl.pallas_call(
        body,
        out_shape=jax.ShapeDtypeStruct(shape, dtype),
        out_specs=pl.BlockSpec(memory_space=pl.ANY),
    )()


def lanes(index):
    if isinstance(index, int):
        return slice(index * LN, (index + 1) * LN)
    return pl.ds(pl.multiple_of(index * LN, LN), LN)


def region(side, px, grid):
    bits = grid.bit_length() - 1
    r = lax.broadcasted_iota(jnp.int32, (px, LN), 0)
    inside = jnp.logical_and((r >> bits) < side, (r & (grid - 1)) < side)
    return jnp.where(inside, 1.0, 0.0).astype(F32)


def rows8(x):
    return x.reshape(x.shape[0] // 8, 8, LN).sum(axis=0)


def total(acc, fold):
    if fold:
        acc = acc + pltpu.roll(acc, 32, 1)
        acc = acc + pltpu.roll(acc, 64, 1)
    return acc.sum(axis=0, keepdims=True)


def gelu_parts(v):
    v2 = v * v
    t = jnp.tanh(v * (GELU_C + (GELU_C * GELU_A) * v2))
    return v2, t


def gelu(v):
    _, t = gelu_parts(v)
    h = 0.5 * v
    return h + h * t


def gelu_both(v):
    v2, t = gelu_parts(v)
    h = 0.5 * v
    slope = 0.5 + 0.5 * t + h * ((1.0 - t * t) * (GELU_C + (3.0 * GELU_C * GELU_A) * v2))
    return h + h * t, slope


def gelu_slope(v):
    return gelu_both(v)[1]


def loop(n, body, init, unroll=False):
    if unroll:
        for i in range(n):
            init = body(i, init)
        return init
    return lax.fori_loop(0, n, body, init)


def moments(ref, out, row, blocks, params, fold, mask, count):
    inv = 1.0 / jnp.maximum(count, 1.0)
    for p in range(params):
        n = blocks // params

        def first(i, acc):
            return acc + rows8(ref[:, lanes(p + i * params)] * mask)

        zero = jnp.zeros((8, LN), F32)
        s = total(loop(n, first, zero, n <= 4), fold)
        mean = s * inv

        def second(i, acc):
            d = (ref[:, lanes(p + i * params)] - mean) * mask
            return acc + rows8(d * d)

        m2 = total(loop(n, second, zero, n <= 4), fold)
        out[row + p : row + p + 1, :] = s
        out[row + params + p : row + params + p + 1, :] = m2


def send(pay_ref, rows_ref):
    value = rows_ref[...]
    for d in range(pay_ref.shape[0]):
        pay_ref[d] = value


def combine(recv_ref, row, params, count_row, cst_ref, at):
    n = recv_ref[:, count_row : count_row + 1, :]
    s = recv_ref[:, row : row + params, :]
    m2 = recv_ref[:, row + params : row + 2 * params, :]
    k = n.sum(axis=0)
    mean = s.sum(axis=0) / k
    off = s / jnp.maximum(n, 1.0) - mean[None]
    var = (m2 + n * off * off).sum(axis=0) / k
    cst_ref[at : at + params, :] = mean
    cst_ref[at + params : at + 2 * params, :] = lax.rsqrt(var + EPS)
    return k


def pack3(pad, b, mid, left, right, px, grid):
    g, half = b // 2, b % 2
    for slot, value in enumerate((left, mid, right)):
        at = g * 768 + slot * 256 + half * 128
        pad[grid : grid + px, at : at + LN] = value.astype(BF16)


def neighbours(h, px, grid):
    col = lax.broadcasted_iota(jnp.int32, (px, LN), 0) & (grid - 1)
    before = jnp.where(col == 0, 0.0, pltpu.roll(h, 1, 0))
    after = jnp.where(col == grid - 1, 0.0, pltpu.roll(h, px - 1, 0))
    return before, after


def clear_edges(pad, px, grid):
    zero = jnp.zeros((grid, pad.shape[1]), BF16)
    pad[0:grid, :] = zero
    pad[grid + px : grid + px + grid, :] = zero


def put_count(rows_ref, row, count):
    rows_ref[row : row + 1, :] = jnp.zeros((1, LN), F32) + count


def side_sq(side, frames):
    s = side.astype(F32)
    return s * s * frames


class Net:
    def __init__(self, ndp, grid):
        self.ndp = ndp
        self.grid = grid
        self.px = grid * grid

    def fast_first(self, side, xf, wa):
        px, grid, ndp = self.px, self.grid, self.ndp

        def body(side_ref, xf_ref, wa_ref, fa_ref, band_ref, pay_ref, row_ref):
            pick = jnp.where(
                (lax.broadcasted_iota(jnp.int32, (CF_MID, 256), 1) & (CF_MID - 1))
                == lax.broadcasted_iota(jnp.int32, (CF_MID, 256), 0),
                1.0,
                0.0,
            ).astype(BF16)
            wide = [dot(wa_ref[k], pick) for k in range(3)]
            group = lax.broadcasted_iota(jnp.int32, (CF, 256), 1) >> 5
            for j in range(10):
                acc = jnp.zeros((CF, 256), F32)
                for k in range(3):
                    if 0 <= j - k < 8:
                        acc = jnp.where(group == j - k, wide[k], acc)
                band_ref[j * CF : (j + 1) * CF, :] = acc.astype(BF16)
            for g in range(4):
                lo, hi = max(8 * g - 1, 0), min(8 * g + 9, TF)
                k0 = lo - (8 * g - 1)
                fa_ref[:, g * 256 : (g + 1) * 256] = dot(
                    xf_ref[:, lo * CF : hi * CF], band_ref[k0 * CF : (k0 + hi - lo) * CF, :]
                )
            side_v = side_ref[0]
            count = side_sq(side_v, TF)
            moments(fa_ref, row_ref, 0, 8, 1, True, region(side_v, px, grid), count)
            put_count(row_ref, 2, count)
            send(pay_ref, row_ref)

        return call(
            body,
            [((px, 1024), F32), ((10 * CF, 256), BF16), ((ndp, 8, LN), F32)],
            [pltpu.VMEM((8, LN), F32)],
            side, xf, wa,
        )

    def fast_weights(self, wb, wbt, wc):
        def body(wb_ref, wbt_ref, wc_ref, b_ref, bt_ref, c_ref):
            pick = jnp.where(
                (lax.broadcasted_iota(jnp.int32, (CF_MID, 256), 1) & (CF_MID - 1))
                == lax.broadcasted_iota(jnp.int32, (CF_MID, 256), 0),
                1.0,
                0.0,
            ).astype(BF16)
            same = (lax.broadcasted_iota(jnp.int32, (256, 256), 0) >> 5) == (
                lax.broadcasted_iota(jnp.int32, (256, 256), 1) >> 5
            )
            for source, target in ((wb_ref, b_ref), (wbt_ref, bt_ref)):
                for tap in range(9):
                    tiled = jnp.concatenate([dot(source[tap], pick)] * 8, axis=0)
                    target[tap // 3, (tap % 3) * 256 : (tap % 3 + 1) * 256, :] = jnp.where(
                        same, tiled, 0.0
                    ).astype(BF16)
            c_ref[...] = jnp.zeros_like(c_ref)
            for i in range(8):
                c_ref[i * CF_MID : (i + 1) * CF_MID, i * CF : (i + 1) * CF] = wc_ref[...]

        return call(
            body,
            [((3, 768, 256), BF16), ((3, 768, 256), BF16), ((256, 1024), BF16)],
            [],
            wb, wbt, wc, smem=0,
        )

    def conv_stage(self, side, recv, row, crow, x, par, w, params, frames):
        px, grid, ndp = self.px, self.grid, self.ndp
        fold = params == 1

        def body(side_ref, recv_ref, x_ref, par_ref, w_ref, h_ref, y_ref, cst_ref, pay_ref, row_ref, pad):
            side_v = side_ref[0]
            mask = region(side_v, px, grid)
            combine(recv_ref, row, params, crow, cst_ref, 0)
            mean, rs = cst_ref[0:params, :], cst_ref[params : 2 * params, :]
            scale = par_ref[0:params, :] * rs
            shift = par_ref[params : 2 * params, :] - mean * scale
            clear_edges(pad, px, grid)
            for b in range(8):
                p = b % params
                v = x_ref[:, lanes(b)] * scale[p : p + 1] + shift[p : p + 1]
                h = gelu(v) * mask
                h_ref[:, lanes(b)] = h.astype(BF16)
                before, after = neighbours(h, px, grid)
                pack3(pad, b, h, before, after, px, grid)
            for g in range(4):
                acc = None
                for i in range(3):
                    part = dot(pad[grid * i : grid * i + px, g * 768 : (g + 1) * 768], w_ref[i])
                    acc = part if acc is None else acc + part
                y_ref[:, g * 256 : (g + 1) * 256] = acc
            count = side_sq(side_v, frames)
            moments(y_ref, row_ref, 0, 8, params, fold, mask, count)
            put_count(row_ref, 2 * params, count)
            send(pay_ref, row_ref)

        return call(
            body,
            [((px, 1024), BF16), ((px, 1024), F32), ((8, LN), F32), ((ndp, 8, LN), F32)],
            [pltpu.VMEM((8, LN), F32), pltpu.VMEM((px + 2 * grid, 4 * 768), BF16)],
            side, recv, x, par, w,
        )

    def expand_stage(self, side, recv, y, par, w, params, wide, frames):
        px, grid, ndp = self.px, self.grid, self.ndp
        rows = -(-(2 * wide + 1) // 8) * 8

        def body(side_ref, recv_ref, y_ref, par_ref, w_ref, h_ref, cst_ref, pay_ref, row_ref, c_ref):
            side_v = side_ref[0]
            mask = region(side_v, px, grid)
            combine(recv_ref, 0, params, 2 * params, cst_ref, 0)
            mean, rs = cst_ref[0:params, :], cst_ref[params : 2 * params, :]
            scale = par_ref[0:params, :] * rs
            shift = par_ref[params : 2 * params, :] - mean * scale
            for b in range(8):
                p = b % params
                v = y_ref[:, lanes(b)] * scale[p : p + 1] + shift[p : p + 1]
                h_ref[:, lanes(b)] = (gelu(v) * mask).astype(BF16)
            for g in range(4):
                c_ref[:, g * 1024 : (g + 1) * 1024] = dot(h_ref[:, g * 256 : (g + 1) * 256], w_ref[...])
            count = side_sq(side_v, frames)
            moments(c_ref, row_ref, 0, 32, wide, False, mask, count)
            put_count(row_ref, 2 * wide, count)
            send(pay_ref, row_ref)

        return call(
            body,
            [((px, 1024), BF16), ((8, LN), F32), ((ndp, rows, LN), F32)],
            [pltpu.VMEM((rows, LN), F32), pltpu.VMEM((px, 4096), F32)],
            side, recv, y, par, w,
        )

    def fast_finish(self, side, recv, h2, w, xf, par, wlat):
        px, grid = self.px, self.grid

        def body(side_ref, recv_ref, h_ref, w_ref, xf_ref, par_ref, wl_ref, out_ref, lat_ref, cst_ref, c_ref):
            mask = region(side_ref[0], px, grid)
            combine(recv_ref, 0, 1, 2, cst_ref, 0)
            scale = par_ref[0:1, :] * cst_ref[1:2, :]
            shift = par_ref[1:2, :] - cst_ref[0:1, :] * scale
            for g in range(4):
                c_ref[...] = dot(h_ref[:, g * 256 : (g + 1) * 256], w_ref[...])

                def step(i, carry):
                    f = g * 8 + i
                    v = c_ref[:, lanes(i)] * scale + shift + xf_ref[:, lanes(f)].astype(F32)
                    out_ref[:, lanes(f)] = (gelu(v) * mask).astype(BF16)
                    return carry

                loop(8, step, 0)
            for t in range(TS):
                lo = max(ALPHA * t - 2, 0)
                k0 = lo - (ALPHA * t - 2)
                lat_ref[:, t * LAT : (t + 1) * LAT] = dot(
                    out_ref[:, lo * CF : (ALPHA * t + 3) * CF], wl_ref[k0 * CF :, :]
                ).astype(BF16)

        return call(
            body,
            [((px, 4096), BF16), ((px, 1024), BF16), ((8, LN), F32)],
            [pltpu.VMEM((px, 1024), F32)],
            side, recv, h2, w, xf, par, wlat,
        )

    def fast_slope(self, side, h2, w, xf, par, cst):
        px, grid = self.px, self.grid

        def body(side_ref, h_ref, w_ref, xf_ref, par_ref, cst_ref, gp_ref, c_ref):
            mask = region(side_ref[0], px, grid)
            scale = par_ref[0:1, :] * cst_ref[1:2, :]
            shift = par_ref[1:2, :] - cst_ref[0:1, :] * scale
            for g in range(4):
                c_ref[...] = dot(h_ref[:, g * 256 : (g + 1) * 256], w_ref[...])

                def step(i, carry):
                    f = g * 8 + i
                    v = c_ref[:, lanes(i)] * scale + shift + xf_ref[:, lanes(f)].astype(F32)
                    gp_ref[:, lanes(f)] = gelu_slope(v) * mask
                    return carry

                loop(8, step, 0)

        return call(body, ((px, 4096), F32), [pltpu.VMEM((px, 1024), F32)], side, h2, w, xf, par, cst)

    def slow_start(self, xs, wa, wp):
        px = self.px

        def body(x_ref, wa_ref, wp_ref, a_ref, p_ref):
            for t in range(TS):
                x = x_ref[:, t * CS : (t + 1) * CS]
                a_ref[:, t * CS_MID : (t + 1) * CS_MID] = dot(x, wa_ref[0:CS, :])
                p_ref[:, t * CS : (t + 1) * CS] = dot(x, wp_ref[0:CS, :])

        return call(body, [((px, 1024), F32), ((px, 4096), F32)], [], xs, wa, wp, smem=0)

    def slow_first(self, side, pa, pp, lat, wa, wp):
        px, grid, ndp = self.px, self.grid, self.ndp

        def body(side_ref, pa_ref, pp_ref, lat_ref, wa_ref, wp_ref, sa_ref, sp_ref, pay_ref, row_ref):
            side_v = side_ref[0]
            mask = region(side_v, px, grid)
            for t in range(TS):
                x = lat_ref[:, t * LAT : (t + 1) * LAT]
                a, p = slice(t * CS_MID, (t + 1) * CS_MID), slice(t * CS, (t + 1) * CS)
                sa_ref[:, a] = pa_ref[:, a] + dot(x, wa_ref[...])
                sp_ref[:, p] = pp_ref[:, p] + dot(x, wp_ref[...])
            count = side_sq(side_v, TS)
            moments(sa_ref, row_ref, 0, 8, 2, False, mask, count)
            moments(sp_ref, row_ref, 4, 32, 8, False, mask, count)
            put_count(row_ref, 20, count)
            send(pay_ref, row_ref)

        return call(
            body,
            [((px, 1024), F32), ((px, 4096), F32), ((ndp, 24, LN), F32)],
            [pltpu.VMEM((24, LN), F32)],
            side, pa, pp, lat, wa, wp,
        )

    def slow_top(self, side, recv3, recv1, h2, w, sp, gs, parc, parp):
        px, grid, ndp = self.px, self.grid, self.ndp

        def body(
            side_ref, r3_ref, r1_ref, h_ref, w_ref, sp_ref, gs_ref, pc_ref, pp_ref,
            ys_ref, ds_ref, cc_ref, cp_ref, pay_ref, row_ref, c_ref, acc_ref,
        ):
            mask = region(side_ref[0], px, grid)
            combine(r3_ref, 0, 8, 16, cc_ref, 0)
            combine(r1_ref, 4, 8, 20, cp_ref, 0)
            acc_ref[...] = jnp.zeros_like(acc_ref)
            for t in range(TS):
                c_ref[...] = dot(h_ref[:, t * 256 : (t + 1) * 256], w_ref[...])

                def step(b, carry):
                    at = lanes(t * 8 + b)
                    one = pl.ds(b, 1)
                    up = pl.ds(b + 8, 1)
                    xc = (c_ref[:, lanes(b)] - cc_ref[one, :]) * cc_ref[up, :]
                    xp = (sp_ref[:, at] - cp_ref[one, :]) * cp_ref[up, :]
                    v = (
                        xc * pc_ref[one, :]
                        + xp * pp_ref[one, :]
                        + (pc_ref[up, :] + pp_ref[up, :])
                    )
                    y, slope = gelu_both(v)
                    ys_ref[:, at] = (y * mask).astype(BF16)
                    d = gs_ref[:, at].astype(F32) * slope * mask
                    ds_ref[:, at] = d
                    acc_ref[b] += rows8(d)
                    acc_ref[8 + b] += rows8(d * xc)
                    acc_ref[16 + b] += rows8(d * xp)
                    return carry

                loop(8, step, 0)
            row_ref[...] = acc_ref[...].sum(axis=1)
            send(pay_ref, row_ref)

        return call(
            body,
            [
                ((px, 4096), BF16), ((px, 4096), F32), ((16, LN), F32), ((16, LN), F32),
                ((ndp, 24, LN), F32),
            ],
            [pltpu.VMEM((24, LN), F32), pltpu.VMEM((px, 1024), F32), pltpu.VMEM((24, 8, LN), F32)],
            side, recv3, recv1, h2, w, sp, gs, parc, parp,
        )

    def fast_top(self, dlat, wlat, gf, gp, h2, w, cst):
        px, ndp = self.px, self.ndp

        def body(dl_ref, wl_ref, gf_ref, gp_ref, h_ref, w_ref, cst_ref, ds_ref, pay_ref, row_ref, lt_ref, c_ref, acc_ref):
            for t in range(TS):
                lt_ref[:, t * 640 : (t + 1) * 640] = dot_t(dl_ref[:, t * LAT : (t + 1) * LAT], wl_ref[...])
            lt_ref[:, TS * 640 : TS * 640 + 256] = jnp.zeros((px, 256), F32)
            acc_ref[...] = jnp.zeros_like(acc_ref)
            mean, rs = cst_ref[0:1, :], cst_ref[1:2, :]
            for g in range(4):
                c_ref[...] = dot(h_ref[:, g * 256 : (g + 1) * 256], w_ref[...])
                for i in range(8):
                    at = lanes(g * 8 + i)
                    d = gf_ref[:, at].astype(F32)
                    if i < 3:
                        d = d + lt_ref[:, lanes(g * 5 + i + 2)]
                    elif i >= 6:
                        d = d + lt_ref[:, lanes((g + 1) * 5 + i - 6)]
                    d = d * gp_ref[:, at]
                    ds_ref[:, at] = d
                    xh = (c_ref[:, lanes(i)] - mean) * rs
                    acc_ref[0] += rows8(d)
                    acc_ref[1] += rows8(d * xh)
            row_ref[...] = jnp.zeros_like(row_ref)
            row_ref[0:2, :] = acc_ref[...].sum(axis=1)
            send(pay_ref, row_ref)

        return call(
            body,
            [((px, 4096), F32), ((ndp, 8, LN), F32)],
            [
                pltpu.VMEM((8, LN), F32), pltpu.VMEM((px, TS * 640 + 256), F32),
                pltpu.VMEM((px, 1024), F32), pltpu.VMEM((2, 8, LN), F32),
            ],
            dlat, wlat, gf, gp, h2, w, cst, smem=0,
        )

    def expand_back(self, side, kcount, recv, ds, h2, w, cstw, parw, y, cst, par, params, wide, shortcut=None):
        px, grid, ndp = self.px, self.grid, self.ndp
        fold = params == 1
        both = shortcut is not None
        srows = 3 * wide if both else 8

        def body(*refs):
            side_ref, k_ref, recv_ref, ds_ref, h_ref, w_ref, cw_ref, pw_ref, y_ref, cs_ref, par_ref = refs[:11]
            refs = refs[11:]
            if both:
                sp_ref, cp_ref, pp_ref = refs[:3]
                refs = refs[3:]
                dp_ref = refs[0]
                refs = refs[1:]
            dc_ref, dn_ref, sum_ref, pay_ref, row_ref, c_ref, k3_ref = refs
            mask = region(side_ref[0], px, grid)
            inv_k = 1.0 / k_ref[0]
            sums = recv_ref[...].sum(axis=0)
            sum_ref[...] = sums
            a = pw_ref[0:wide, :] * cw_ref[wide : 2 * wide, :]
            k3_ref[0:wide, :] = a
            k3_ref[wide : 2 * wide, :] = a * inv_k * sums[0:wide]
            k3_ref[2 * wide : 3 * wide, :] = a * inv_k * cw_ref[wide : 2 * wide, :] * sums[wide : 2 * wide]
            if both:
                a = pp_ref[0:wide, :] * cp_ref[wide : 2 * wide, :]
                k3_ref[3 * wide : 4 * wide, :] = a
                k3_ref[4 * wide : 5 * wide, :] = a * inv_k * sums[0:wide]
                k3_ref[5 * wide : 6 * wide, :] = (
                    a * inv_k * cp_ref[wide : 2 * wide, :] * sums[2 * wide : 3 * wide]
                )
            mean, rs = cs_ref[0:params, :], cs_ref[params : 2 * params, :]
            accs = [[jnp.zeros((8, LN), F32) for _ in range(params)] for _ in range(2)]
            for g in range(4):
                c_ref[...] = dot(h_ref[:, g * 256 : (g + 1) * 256], w_ref[...])

                def step(b, carry):
                    at = lanes(g * 8 + b)
                    p = b if wide == 8 else 0
                    d = ds_ref[:, at]
                    e = (c_ref[:, lanes(b)] - cw_ref[pl.ds(p, 1), :]) * k3_ref[pl.ds(2 * wide + p, 1), :]
                    e = d * k3_ref[pl.ds(p, 1), :] - k3_ref[pl.ds(wide + p, 1), :] - e
                    dc_ref[:, at] = (e * mask).astype(BF16)
                    if both:
                        e = (sp_ref[:, at] - cp_ref[pl.ds(p, 1), :]) * k3_ref[pl.ds(5 * wide + p, 1), :]
                        e = d * k3_ref[pl.ds(3 * wide + p, 1), :] - k3_ref[pl.ds(4 * wide + p, 1), :] - e
                        dp_ref[:, at] = (e * mask).astype(BF16)
                    return carry

                loop(8, step, 0)
                dh = dot_t(dc_ref[:, g * 1024 : (g + 1) * 1024], w_ref[...])
                for half in range(2):
                    b = g * 2 + half
                    p = b % params
                    xh = (y_ref[:, lanes(b)] - mean[p : p + 1]) * rs[p : p + 1]
                    v = xh * par_ref[p : p + 1, :] + par_ref[params + p : params + p + 1, :]
                    d = dh[:, half * LN : (half + 1) * LN] * gelu_slope(v) * mask
                    dn_ref[:, lanes(b)] = d
                    accs[0][p] = accs[0][p] + rows8(d)
                    accs[1][p] = accs[1][p] + rows8(d * xh)
            row_ref[...] = jnp.zeros_like(row_ref)
            for q in range(2):
                for p in range(params):
                    row_ref[q * params + p : q * params + p + 1, :] = total(accs[q][p], fold)
            send(pay_ref, row_ref)

        outs = [((px, 4096), BF16)] if both else []
        outs += [((px, 4096), BF16), ((px, 1024), F32), ((srows, LN), F32), ((ndp, 8, LN), F32)]
        extra = list(shortcut) if both else []
        return call(
            body,
            outs,
            [pltpu.VMEM((8, LN), F32), pltpu.VMEM((px, 1024), F32), pltpu.VMEM((max(6 * wide, 8), LN), F32)],
            side, kcount, recv, ds, h2, w, cstw, parw, y, cst, par, *extra, smem=2,
        )

    def conv_back(self, side, kcount, recv, dn, y, cst2, par2, wt, x, cst1, par1, params):
        px, grid, ndp = self.px, self.grid, self.ndp
        fold = params == 1

        def body(
            side_ref, k_ref, recv_ref, dn_ref, y_ref, c2_ref, p2_ref, w_ref, x_ref, c1_ref, p1_ref,
            db_ref, dn1_ref, sum_ref, pay_ref, row_ref, pad,
        ):
            mask = region(side_ref[0], px, grid)
            inv_k = 1.0 / k_ref[0]
            sums = recv_ref[...].sum(axis=0)
            sum_ref[...] = sums
            mean2, rs2 = c2_ref[0:params, :], c2_ref[params : 2 * params, :]
            a = p2_ref[0:params, :] * rs2
            b0 = a * inv_k * sums[0:params]
            c0 = a * inv_k * rs2 * sums[params : 2 * params]
            clear_edges(pad, px, grid)
            for b in range(8):
                p = b % params
                e = (y_ref[:, lanes(b)] - mean2[p : p + 1]) * c0[p : p + 1]
                e = (dn_ref[:, lanes(b)] * a[p : p + 1] - b0[p : p + 1] - e) * mask
                db_ref[:, lanes(b)] = e.astype(BF16)
                before, after = neighbours(e, px, grid)
                pack3(pad, b, e, after, before, px, grid)
            mean, rs = c1_ref[0:params, :], c1_ref[params : 2 * params, :]
            accs = [[jnp.zeros((8, LN), F32) for _ in range(params)] for _ in range(2)]
            for g in range(4):
                dh = None
                for i in range(3):
                    part = dot(pad[grid * i : grid * i + px, g * 768 : (g + 1) * 768], w_ref[2 - i])
                    dh = part if dh is None else dh + part
                for half in range(2):
                    b = g * 2 + half
                    p = b % params
                    xh = (x_ref[:, lanes(b)] - mean[p : p + 1]) * rs[p : p + 1]
                    v = xh * p1_ref[p : p + 1, :] + p1_ref[params + p : params + p + 1, :]
                    d = dh[:, half * LN : (half + 1) * LN] * gelu_slope(v) * mask
                    dn1_ref[:, lanes(b)] = d
                    accs[0][p] = accs[0][p] + rows8(d)
                    accs[1][p] = accs[1][p] + rows8(d * xh)
            row_ref[...] = jnp.zeros_like(row_ref)
            for q in range(2):
                for p in range(params):
                    row_ref[q * params + p : q * params + p + 1, :] = total(accs[q][p], fold)
            send(pay_ref, row_ref)

        return call(
            body,
            [((px, 1024), BF16), ((px, 1024), F32), ((8, LN), F32), ((ndp, 8, LN), F32)],
            [pltpu.VMEM((8, LN), F32), pltpu.VMEM((px + 2 * grid, 4 * 768), BF16)],
            side, kcount, recv, dn, y, cst2, par2, wt, x, cst1, par1, smem=2,
        )

    def slow_last(self, side, kcount, recv, dn, x, cst, par, dp, wa, wp):
        px, grid = self.px, self.grid

        def body(side_ref, k_ref, recv_ref, dn_ref, x_ref, cst_ref, par_ref, dp_ref, wa_ref, wp_ref, da_ref, dl_ref, sum_ref):
            mask = region(side_ref[0], px, grid)
            inv_k = 1.0 / k_ref[0]
            sums = recv_ref[...].sum(axis=0)
            sum_ref[...] = sums
            mean, rs = cst_ref[0:2, :], cst_ref[2:4, :]
            a = par_ref[0:2, :] * rs
            b0 = a * inv_k * sums[0:2]
            c0 = a * inv_k * rs * sums[2:4]
            for b in range(8):
                p = b % 2
                e = (x_ref[:, lanes(b)] - mean[p : p + 1]) * c0[p : p + 1]
                e = (dn_ref[:, lanes(b)] * a[p : p + 1] - b0[p : p + 1] - e) * mask
                da_ref[:, lanes(b)] = e.astype(BF16)
            for t in range(TS):
                h = slice(t * CS_MID, (t + 1) * CS_MID)
                dl_ref[:, t * LAT : (t + 1) * LAT] = (
                    dot_t(da_ref[:, h], wa_ref[...])
                    + dot_t(dp_ref[:, t * CS : (t + 1) * CS], wp_ref[...])
                ).astype(BF16)

        return call(
            body,
            [((px, 1024), BF16), ((px, 1024), BF16), ((8, LN), F32)],
            [],
            side, kcount, recv, dn, x, cst, par, dp, wa, wp, smem=2,
        )

    def slow_input_grad(self, da, dp, wa, wp):
        px = self.px

        def body(da_ref, dp_ref, wa_ref, wp_ref, dx_ref):
            for t in range(TS):
                dx_ref[:, t * CS : (t + 1) * CS] = (
                    dot_t(da_ref[:, t * CS_MID : (t + 1) * CS_MID], wa_ref[0:CS, :])
                    + dot_t(dp_ref[:, t * CS : (t + 1) * CS], wp_ref[0:CS, :])
                ).astype(BF16)

        return call(body, ((px, 4096), BF16), [], da, dp, wa, wp, smem=0)

    def fast_last(self, side, kcount, recv, dn, x, cst, par, ds, band):
        px, grid = self.px, self.grid

        def body(side_ref, k_ref, recv_ref, dn_ref, x_ref, cst_ref, par_ref, ds_ref, band_ref, da_ref, dx_ref, sum_ref, acc_ref):
            mask = region(side_ref[0], px, grid)
            inv_k = 1.0 / k_ref[0]
            sums = recv_ref[...].sum(axis=0)
            sum_ref[...] = sums
            mean, rs = cst_ref[0:1, :], cst_ref[1:2, :]
            a = par_ref[0:1, :] * rs
            b0 = a * inv_k * sums[0:1]
            c0 = a * inv_k * rs * sums[1:2]
            for b in range(8):
                e = (x_ref[:, lanes(b)] - mean) * c0
                e = (dn_ref[:, lanes(b)] * a - b0 - e) * mask
                da_ref[:, lanes(b)] = e.astype(BF16)
            for g in range(4):
                part = dot_t(da_ref[:, g * 256 : (g + 1) * 256], band_ref[...])
                base = 8 * g * CF
                if g == 0:
                    acc_ref[:, 0 : 10 * CF] = part
                else:
                    acc_ref[:, base : base + 2 * CF] += part[:, 0 : 2 * CF]
                    acc_ref[:, base + 2 * CF : base + 10 * CF] = part[:, 2 * CF :]

            def step(f, carry):
                dx_ref[:, lanes(f)] = (ds_ref[:, lanes(f)] + acc_ref[:, lanes(f + 1)]).astype(BF16)
                return carry

            loop(TF, step, 0)

        return call(
            body,
            [((px, 1024), BF16), ((px, 4096), BF16), ((8, LN), F32)],
            [pltpu.VMEM((px, 34 * CF), F32)],
            side, kcount, recv, dn, x, cst, par, ds, band, smem=2,
        )

    def fast_kernel_grads(self, xf, da, h1, db, h2, dc):
        px, grid = self.px, self.grid

        def body(x_ref, da_ref, h1_ref, db_ref, h2_ref, dc_ref, ga_ref, gb_ref, gc_ref, pad):
            group = lax.broadcasted_iota(jnp.int32, (CF, 256), 1) >> 5

            def fold(v):
                v = v[:, 0:LN] + v[:, LN:256]
                v = v + pltpu.roll(v, 32, 1)
                v = v + pltpu.roll(v, 64, 1)
                return v[:, 0:CF_MID]

            accs = [jnp.zeros((CF, 256), F32) for _ in range(3)]
            for g in range(4):
                lo, hi = max(8 * g - 1, 0), min(8 * g + 9, TF)
                k0 = lo - (8 * g - 1)
                d = da_ref[:, g * 256 : (g + 1) * 256]
                for j in range(k0, k0 + hi - lo):
                    f = 8 * g - 1 + j
                    part = dot(x_ref[:, f * CF : (f + 1) * CF].T, d)
                    for k in range(3):
                        if 0 <= j - k < 8:
                            accs[k] = accs[k] + jnp.where(group == j - k, part, 0.0)
            for k in range(3):
                ga_ref[k] = fold(accs[k])
            clear_edges(pad, px, grid)
            for b in range(8):
                h = h1_ref[:, lanes(b)].astype(F32)
                before, after = neighbours(h, px, grid)
                pack3(pad, b, h, before, after, px, grid)
            same = (lax.broadcasted_iota(jnp.int32, (256, 256), 0) >> 5) == (
                lax.broadcasted_iota(jnp.int32, (256, 256), 1) >> 5
            )
            for i in range(3):
                for s in range(3):
                    acc = jnp.zeros((256, 256), F32)
                    for g in range(4):
                        at = g * 768 + s * 256
                        acc = acc + dot(
                            pad[grid * i : grid * i + px, at : at + 256].T,
                            db_ref[:, g * 256 : (g + 1) * 256],
                        )
                    acc = jnp.where(same, acc, 0.0).reshape(8, CF_MID, 256).sum(axis=0)
                    gb_ref[3 * i + s] = fold(acc)
            acc = jnp.zeros((256, 1024), F32)
            for g in range(4):
                acc = acc + dot(h2_ref[:, g * 256 : (g + 1) * 256].T, dc_ref[:, g * 1024 : (g + 1) * 1024])
            out = None
            for i in range(8):
                part = acc[i * CF_MID : (i + 1) * CF_MID, i * CF : (i + 1) * CF]
                out = part if out is None else out + part
            gc_ref[...] = out

        return call(
            body,
            [((3, CF, CF_MID), F32), ((9, CF_MID, CF_MID), F32), ((CF_MID, CF), F32)],
            [pltpu.VMEM((px + 2 * grid, 4 * 768), BF16)],
            xf, da, h1, db, h2, dc, smem=0,
        )

    def slow_kernel_grads(self, plan, xs, lat, da, dp, h1, db, h2, dc, yf, dlat, pay1, pay2, pay3):
        px, grid = self.px, self.grid
        inner, outer, first, chunk = plan.inner, plan.outer, plan.first, plan.chunk
        ndp = self.ndp

        def body(
            x_ref, lat_ref, da_ref, dp_ref, h1_ref, db_ref, h2_ref, dc_ref, yf_ref, dl_ref,
            p1_ref, p2_ref, p3_ref, out_ref, buf, pad, xt,
        ):
            def put(base, value, wide):
                n = value.shape[0]
                for j in range(wide):
                    buf[pl.ds(base + j, n, stride=wide), :] = value[:, j * LN : (j + 1) * LN]

            for c in range((CS + LAT) // 256):
                acc_a = acc_p = None
                for t in range(TS):
                    if c < CS // 256:
                        x = x_ref[:, t * CS + c * 256 : t * CS + (c + 1) * 256]
                    else:
                        x = lat_ref[:, t * LAT : (t + 1) * LAT]
                    xt[:, t * px : (t + 1) * px] = x.T
                for t in range(TS):
                    part = dot(xt[:, t * px : (t + 1) * px], da_ref[:, t * CS_MID : (t + 1) * CS_MID])
                    acc_a = part if acc_a is None else acc_a + part
                put(ROW_SA + c * 512, acc_a, 2)
                for q in range(4):
                    acc_p = None
                    for t in range(TS):
                        at = t * CS + q * 256
                        part = dot(xt[:, t * px : (t + 1) * px], dp_ref[:, at : at + 256])
                        acc_p = part if acc_p is None else acc_p + part
                    for j in range(2):
                        buf[pl.ds(ROW_SP + c * 2048 + 2 * q + j, 256, stride=8), :] = acc_p[:, j * LN : (j + 1) * LN]
            for t in range(TS):
                xt[:, t * px : (t + 1) * px] = h2_ref[:, t * 256 : (t + 1) * 256].T
            for q in range(4):
                acc_p = None
                for t in range(TS):
                    at = t * CS + q * 256
                    part = dot(xt[:, t * px : (t + 1) * px], dc_ref[:, at : at + 256])
                    acc_p = part if acc_p is None else acc_p + part
                for j in range(2):
                    buf[pl.ds(ROW_SC + 2 * q + j, 256, stride=8), :] = acc_p[:, j * LN : (j + 1) * LN]
            clear_edges(pad, px, grid)
            for b in range(8):
                h = h1_ref[:, lanes(b)].astype(F32)
                before, after = neighbours(h, px, grid)
                pack3(pad, b, h, before, after, px, grid)
            for i in range(3):
                for s in range(3):
                    acc = None
                    for t in range(TS):
                        at = t * 768 + s * 256
                        part = dot(
                            pad[grid * i : grid * i + px, at : at + 256].T,
                            db_ref[:, t * 256 : (t + 1) * 256],
                        )
                        acc = part if acc is None else acc + part
                    put(ROW_SB + (3 * i + s) * 512, acc, 2)
            for k in range(5):
                acc = jnp.zeros((CF, LAT), F32)
                for t in range(TS):
                    f = ALPHA * t - 2 + k
                    if f >= 0:
                        acc = acc + dot(yf_ref[:, f * CF : (f + 1) * CF].T, dl_ref[:, t * LAT : (t + 1) * LAT])
                put(ROW_LAT + k * 256, acc, 2)
            for gain, base in ((1, ROW_SG), (0, ROW_SG + SLOW_VEC)):
                buf[base : base + 2, :] = p1_ref[0, 2 * gain : 2 * gain + 2, :]
                buf[base + 2 : base + 4, :] = p2_ref[0, 2 * gain : 2 * gain + 2, :]
                buf[base + 4 : base + 12, :] = p3_ref[0, 8 * gain : 8 * gain + 8, :]
                buf[base + 12 : base + 20, :] = p3_ref[0, 16 * gain : 16 * gain + 8, :]
            buf[ROW_FA:ROW_LAT, :] = jnp.zeros((ROW_LAT - ROW_FA, LN), F32)
            buf[ROW_FG:, :] = jnp.zeros((buf.shape[0] - ROW_FG, LN), F32)
            for path in range(2):
                for dp_at in range(ndp):
                    r0 = first[path * ndp + dp_at]
                    out_ref[dp_at % inner, dp_at // inner, path] = buf[r0 : r0 + chunk, :].astype(BF16)

        return call(
            body,
            ((inner, outer, 2, chunk, LN), BF16),
            [
                pltpu.VMEM((plan.rows, LN), F32),
                pltpu.VMEM((px + 2 * grid, 4 * 768), BF16),
                pltpu.VMEM((256, TS * px), BF16),
            ],
            xs, lat, da, dp, h1, db, h2, dc, yf, dlat, pay1, pay2, pay3, smem=0, limit=56,
        )

    def window(self, plan, ints, mine, theirs, small, tail):
        chunk, out_rows = plan.chunk, plan.out_rows
        pad = small.shape[0] + 8

        def body(int_ref, mine_ref, theirs_ref, small_ref, tail_ref, out_ref, a_ref):
            fast = int_ref[0]
            r0 = int_ref[1]
            row = int_ref[2]
            lane = int_ref[3]
            a_ref[...] = jnp.zeros_like(a_ref)
            ns = small_ref.shape[0]
            for ref, start in ((small_ref, ROW_FA), (tail_ref, ROW_FG)):
                at = jnp.clip(start - r0, -ref.shape[0], chunk) + pad
                a_ref[pl.ds(at, ref.shape[0]), :] = ref[...]
            body_rows = a_ref[pad : pad + chunk, :]
            body_rows = jnp.where(fast == 1, theirs_ref[...] + body_rows, mine_ref[...])
            a_ref[pad : pad + chunk, :] = body_rows
            one = a_ref[pl.ds(pad + row, out_rows), :]
            two = a_ref[pl.ds(pad + row + 1, out_rows), :]
            shift = (LN - lane) & (LN - 1)
            one = pltpu.roll(one, shift, 1)
            two = pltpu.roll(two, shift, 1)
            at = lax.broadcasted_iota(jnp.int32, (out_rows, LN), 1)
            out_ref[...] = jnp.where(at < LN - lane, one, two)

        return call(
            body,
            ((out_rows, LN), F32),
            [pltpu.VMEM((chunk + 2 * pad + 8, LN), F32)],
            ints, mine, theirs, small, tail,
        )


class Plan:
    def __init__(self, ndp):
        n = 2 * ndp
        total_values = 2685312
        self.share = total_values // n
        self.first = [self.share * d // LN // 16 * 16 for d in range(n)]
        ends = [-(-self.share * (d + 1) // LN) for d in range(n)]
        self.chunk = -(-max(e - f for e, f in zip(ends, self.first)) // 16) * 16
        self.rows = -(-max(max(f + self.chunk for f in self.first), ROWS) // 16) * 16
        self.out_rows = -(-self.share // LN)
        self.outer = 4 if ndp % 4 == 0 else 1
        self.inner = ndp // self.outer
        self.near = [[o * self.inner + i for i in range(self.inner)] for o in range(self.outer)]
        self.far = [[o * self.inner + i for o in range(self.outer)] for i in range(self.inner)]


def exchange(x, groups=None):
    return lax.all_to_all(x, "dp", 0, 0, axis_index_groups=groups)


def local(
    acts, cotangent, clip_res, w_slow_a, w_slow_b, w_slow_c, w_slow_proj, slow_gain, slow_bias,
    w_fast_a, w_fast_b, w_fast_c, w_lateral, fast_gain, fast_bias,
):
    grid = acts.shape[2]
    px = grid * grid
    ndp = lax.axis_size("dp")
    net = Net(ndp, grid)
    plan = Plan(ndp)
    is_fast = lax.axis_index("path") == 1
    level = clip_res[0]
    side = jnp.where(
        level == 1, grid * 5 // 8, jnp.where(level == 2, grid * 7 // 8, jnp.where(level == 3, grid, 0))
    ).astype(jnp.int32).reshape(1)
    x = acts.reshape(px, 4096)
    cot = cotangent.reshape(px, 4096)

    sg, sb_ = slow_gain.reshape(SLOW_VEC, LN), slow_bias.reshape(SLOW_VEC, LN)

    def slow_par(a, b):
        return jnp.concatenate([sg[a:b], sb_[a:b]], axis=0)

    def fast_par(a, b):
        one = jnp.stack([fast_gain[a:b], fast_bias[a:b]])
        return jnp.tile(one, (1, LN // (b - a)))

    wlat = w_lateral.reshape(5 * CF, LAT)
    wa_lat, wp_lat = w_slow_a[CS:], w_slow_proj[CS:]

    def fast_forward(x):
        p1, p2, p3 = fast_par(0, 32), fast_par(32, 64), fast_par(64, 192)
        wb, wbt, wc = net.fast_weights(w_fast_b, w_fast_b.transpose(0, 2, 1), w_fast_c)
        fa, band, pay = net.fast_first(side, x, w_fast_a)
        r1 = exchange(pay)
        h1, fb, c1, pay = net.conv_stage(side, r1, 0, 2, fa, p1, wb, 1, TF)
        r2 = exchange(pay)
        h2, c2, pay = net.expand_stage(side, r2, fb, p2, wc, 1, 1, TF)
        r3 = exchange(pay)
        out, lat, c3 = net.fast_finish(side, r3, h2, wc, x, p3, wlat)
        pixels = r1[:, 2, 0].sum().reshape(1)
        return fa, h1, fb, h2, out, lat, empty((px, 4096), F32), band, wbt, wc, c1, c2, c3, pixels

    def slow_forward(x):
        pa, pp = net.slow_start(x, w_slow_a, w_slow_proj)
        wt = w_slow_b.transpose(0, 2, 1).reshape(3, 768, 256)
        e = empty
        return (
            pa, e((px, 1024), BF16), e((px, 1024), F32), e((px, 1024), BF16), e((px, 4096), BF16),
            e((px, 1024), BF16), pp, e((10 * CF, 256), BF16), wt, e((256, 1024), BF16),
            e((8, LN), F32), e((8, LN), F32), e((8, LN), F32), e((1,), F32),
        )

    first, h1, second, h2, out_f, lat, pp, band, wt, wc, c1, c2, c3, kf = lax.cond(
        is_fast, fast_forward, slow_forward, x
    )
    lat_s = lax.ppermute(lat, "path", SWAP)
    yf_s = lax.ppermute(out_f, "path", SWAP)

    def slow_middle(args):
        lat_s, pa, pp, wt = args[:4]
        p1, p2, p3, pp3 = slow_par(0, 2), slow_par(2, 4), slow_par(4, 12), slow_par(12, 20)
        sa, sp, pay = net.slow_first(side, pa, pp, lat_s, wa_lat, wp_lat)
        r1 = exchange(pay)
        h1, sb, c1, pay = net.conv_stage(side, r1, 0, 20, sa, p1, w_slow_b.reshape(3, 768, 256), 2, TS)
        r2 = exchange(pay)
        h2, c2, pay = net.expand_stage(side, r2, sb, p2, w_slow_c, 2, 8, TS)
        r3 = exchange(pay)
        ks = r3[:, 16, 0].sum().reshape(1)
        ys, ds, cc, cp, pay3 = net.slow_top(side, r3, r1, h2, w_slow_c, sp, cot, p3, pp3)
        r = exchange(pay3)
        dp, dc, dn2, _, pay2 = net.expand_back(
            side, ks, r, ds, h2, w_slow_c, cc, p3, sb, c2, p2, 2, 8, (sp, cp, pp3)
        )
        r = exchange(pay2)
        db, dn1, _, pay1 = net.conv_back(side, ks, r, dn2, sb, c2, p2, wt, sa, c1, p1, 2)
        r = exchange(pay1)
        da, dlat, _ = net.slow_last(side, ks, r, dn1, sa, c1, p1, dp, wa_lat, wp_lat)
        return (
            ys, dlat, da, dp, dc, db, h1, h2, pay1, pay2, pay3, empty((px, 4096), F32),
        )

    def fast_middle(args):
        x, h2, wc, c3, out_f = args[4:]
        gp = net.fast_slope(side, h2, wc, x, fast_par(64, 192), c3)
        e = empty
        return (
            out_f, e((px, 1024), BF16), e((px, 1024), BF16), e((px, 4096), BF16), e((px, 4096), BF16),
            e((px, 1024), BF16), e((px, 1024), BF16), e((px, 1024), BF16), e((ndp, 8, LN), F32),
            e((ndp, 8, LN), F32), e((ndp, 24, LN), F32), gp,
        )

    out, dlat, da_s, dp_s, dc_s, db_s, h1_s, h2_s, pay1, pay2, pay3, gp = lax.cond(
        is_fast, fast_middle, slow_middle, (lat_s, first, pp, wt, x, h2, wc, c3, out_f)
    )
    dlat_f = lax.ppermute(dlat, "path", SWAP)

    def fast_backward(args):
        dlat, gp, x, fa, h1, fb, h2, wbt, wc, band, c1, c2, c3, kf = args[:14]
        p1, p2, p3 = fast_par(0, 32), fast_par(32, 64), fast_par(64, 192)
        ds, pay = net.fast_top(dlat, wlat, cot, gp, h2, wc, c3)
        r = exchange(pay)
        dc, dn2, s3, pay = net.expand_back(side, kf, r, ds, h2, wc, c3, p3, fb, c2, p2, 1, 1)
        r = exchange(pay)
        db, dn1, s2, pay = net.conv_back(side, kf, r, dn2, fb, c2, p2, wbt, fa, c1, p1, 1)
        r = exchange(pay)
        da, dx, s1 = net.fast_last(side, kf, r, dn1, fa, c1, p1, ds, band)
        ga, gb, gc = net.fast_kernel_grads(x, da, h1, db, h2, dc)
        rows = jnp.concatenate([v.reshape(-1, LN) for v in (ga, gb, gc)], axis=0)
        rows = jnp.pad(rows, ((0, -rows.shape[0] % 16), (0, 0))).astype(BF16)
        small = exchange(jnp.broadcast_to(rows[None], (ndp,) + rows.shape)).astype(F32).sum(axis=0)
        tail = jnp.concatenate(
            [s1[1, :32], s2[1, :32], s3[1], s1[0, :32], s2[0, :32], s3[0]]
        ).reshape(3, LN)
        tail = jnp.pad(tail, ((0, 5), (0, 0)))
        return dx, empty((2, plan.chunk, LN), F32), small, tail

    def slow_backward(args):
        x, yf, lat, dlat, da, dp, dc, db, h1, h2, pay1, pay2, pay3 = args[14:]
        parts = net.slow_kernel_grads(plan, x, lat, da, dp, h1, db, h2, dc, yf, dlat, pay1, pay2, pay3)
        near = exchange(parts, plan.near).astype(F32).sum(axis=0).astype(BF16)
        far = exchange(near, plan.far).astype(F32).sum(axis=0)
        dx = net.slow_input_grad(da, dp, w_slow_a, w_slow_proj)
        return dx, far, jnp.zeros((208, LN), F32), jnp.zeros((8, LN), F32)

    dx, far, small, tail = lax.cond(
        is_fast,
        fast_backward,
        slow_backward,
        (
            dlat_f, gp, x, first, h1, second, h2, wt, wc, band, c1, c2, c3, kf,
            x, yf_s, lat_s, dlat, da_s, dp_s, dc_s, db_s, h1_s, h2_s, pay1, pay2, pay3,
        ),
    )
    theirs = lax.ppermute(far[1], "path", SWAP)
    device = lax.axis_index("path") * ndp + lax.axis_index("dp")
    start = device * plan.share
    r0 = start // LN // 16 * 16
    off = start - r0 * LN
    ints = jnp.stack([is_fast.astype(jnp.int32), r0, off // LN, off % LN]).astype(jnp.int32)
    flat = net.window(plan, ints, far[0], theirs, small, tail).reshape(-1)[: plan.share]
    return (out.reshape(acts.shape), dx.reshape(acts.shape), flat)


def solution(mesh):
    data = P("path", "dp", None, None, None)
    in_specs = (data, data, P("dp")) + (P(),) * 12
    out_specs = (data, data, P(("path", "dp")))
    return jax.shard_map(local, mesh=mesh, in_specs=in_specs, out_specs=out_specs, check_vma=False)
```

time: 1420 us -> 296 us (0.21)
  blocking collectives: 718 us -> 51.2 us
  waiting for transfers between devices: 374 us -> 66.7 us
  local copies, waits for them, and re-layouts: 162 us -> 13.2 us
  Pallas kernels: 0 us -> 71.4 us
  starting transfers between devices: 2.81 us -> 68.5 us
  matrix products: 60.8 us -> 0 us
  other arithmetic: 69.5 us -> 8.79 us
  between operations: 16.8 us -> 1.68 us
    psum x18 -> x0, blocking collectives: 718 us -> none  [the longest x6 260 us: global_terms(): return lax.psum((bias_gradient_terms, gain_gradient_terms), 'dp')]
    unnamed x2 -> x0, waiting for transfers between devices: 286 us -> none
    concatenate x1 -> x0, local copies, waits for them, and re-layouts: 89.7 us -> none  [local(): jnp.concatenate([grad_w_sa.reshape(-1), grad_w_sb.reshape(-1), grad_w_sc....]
    ppermute x2 -> x4, waiting for transfers between devices: 87.9 us -> 8.46 us  [the longest x1 4.86 us: local(): lat_s = lax.ppermute(lat, 'path', SWAP)]
    pallas_call x0 -> x23, Pallas kernels: none -> 71.4 us  [the longest x11 71.4 us: call(): pl.pallas_call(body, out_shape=shapes, in_specs=specs, out_specs=[pl.Bloc...]
    dot_general x39 -> x0, matrix products: 60.8 us -> none  [the longest x12 21 us: product(): jnp.einsum('chwti,io->chwto', features, kernel, preferred_element_type=jn...]
    all_to_all x0 -> x6, waiting for transfers between devices: none -> 58.3 us  [exchange(): return lax.all_to_all(x, 'dp', 0, 0, axis_index_groups=groups)]
    all_to_all x0 -> x2, blocking collectives: none -> 51.2 us  [exchange(): return lax.all_to_all(x, 'dp', 0, 0, axis_index_groups=groups)]
  transfers between devices with their start and end apart: 3 -> 10, of which waited for: 3 -> 9; matrix products, arithmetic and copies ran while one was open for 1% -> 2% of each run, Pallas kernels for 0% -> 17%
where the time goes in v1:
time: 296 us; the launch traced here: 292 us
  Pallas kernels  71.4 us (24%)
  starting transfers between devices  68.5 us (23%)
  waiting for transfers between devices  66.7 us (23%)
  blocking collectives  51.2 us (17%)
  local copies, waits for them, and re-layouts  13.2 us (4%)
  loops' own time  10.2 us (3%)
  other arithmetic  8.79 us (3%)
    pallas_call x11, Pallas kernels, call(): pl.pallas_call(body, out_shape=shapes, in_specs=specs, out_specs=[pl.Bloc...  71.4 us
    all_to_all x6, waiting for transfers between devices, exchange(): return lax.all_to_all(x, 'dp', 0, 0, axis_index_groups=groups)  58.3 us
    all_to_all x2, blocking collectives, exchange(): return lax.all_to_all(x, 'dp', 0, 0, axis_index_groups=groups)  51.2 us
    ppermute x1, starting transfers between devices, local(): yf_s = lax.ppermute(out_f, 'path', SWAP)  46.1 us
    all_to_all x6, starting transfers between devices, exchange(): return lax.all_to_all(x, 'dp', 0, 0, axis_index_groups=groups)  22.3 us
    another operation x1, loops' own time, local(): lax.cond(is_fast, fast_middle, slow_middle, (lat_s, first, pp, wt, x, h2,...  8.79 us
    cond x18, local copies, waits for them, and re-layouts  6.39 us
  transfers between devices with their start and end apart: 10, of which 9 were waited for; matrix products, arithmetic and copies ran while one was open for 2% of the time, Pallas kernels for 17%

profile of v1, /device:TPU:0, one launch (start us, length us, event | category | flops | bytes accessed | tf_op | source)
XLA Modules:
  0.0 291.7 jit_solution(8492915284637777416)
XLA Ops:
  1.3 10.3 %conditional.3 = (f32[256,1024]{1,0:T(8,128)}, bf16[256,1024]{1,0:T(8,128)(2,1)}, f32[256,1024]{1,0:T(8,128)}, bf16[256,1024]{1,0:T(8,128)(2,1)}, bf16[256,4096]...) conditional(s32[]{:T(128)} %convert_element_type.12, ...), branch_computations={%region_0.1_spmd, %region_1.3_spmd} | conditional | flops 399 | bytes 13384636 | solution.py:971
  1.3 7.5 %branch_0_fun.22 = (f32[256,1024]{1,0:T(8,128)}, f32[256,4096]{1,0:T(8,128)}) custom-call(bf16[256,4096]{1,0:T(8,128)(2,1)} %get-tuple-element.137.x_ref, bf16[1280,256]{1,0:T(8,128)(2,1)} %get-tuple-element.138.wa_ref, bf16[1280,1024]{1,0:T(8,128)(2,1)} %get-tuple-element.139.wp_ref), custom_call_target="tpu_custom_call" | custom-call | tf_op jit(solution)/shard_map/cond/branch_0_fun/pallas_call | solution.py:52
  11.6 46.1 %collective-permute-start.1 = (bf16[256,4096]{1,0:T(8,128)(2,1)}, bf16[256,4096]{1,0:T(8,128)(2,1)}, u32[]{:S(2)}, u32[]{:S(2)}) collective-permute-start(bf16[256,4096]{1,0:T(8,128)(2,1)} %get-tuple-element.301), channel_id=1, source_target_pairs={{0,16},{16,0},{1,17},{17,1},{2,18},{18,2},{3,19},{19,3},{4,20},{20... | collective-permute-start | bytes 6291464 | tf_op jit(solution)/shard_map/ppermute | solution.py:975
  57.7 4.9 %collective-permute-done = bf16[256,1024]{1,0:T(8,128)(2,1)} collective-permute-done((bf16[256,1024]{1,0:T(8,128)(2,1)}, bf16[256,1024]{1,0:T(8,128)(2,1)}, u32[]{:S(2)}, u32[]{:S(2)}) %collective-permute-start) | collective-permute-done | bytes 524320 | tf_op jit(solution)/shard_map/ppermute | solution.py:974
  62.6 126.0 %conditional.4 = (bf16[256,4096]{1,0:T(8,128)(2,1)}, bf16[256,1024]{1,0:T(8,128)(2,1)}, bf16[256,1024]{1,0:T(8,128)(2,1)S(1)}, bf16[256,4096]{1,0:T(8,128)(2,1)}...) conditional(s32[]{:T(128)} %convert_element_type.12, ...), branch_computations={%region_3.5_spmd, %region_5.6_spmd} | conditional | flops 5135 | bytes 47727056 | solution.py:1010
  64.8 5.3 %branch_0_fun.34 = (f32[256,1024]{1,0:T(8,128)S(1)}, f32[256,4096]{1,0:T(8,128)S(1)}, f32[16,24,128]{2,1,0:T(8,128)}) custom-call(s32[1]{0:T(128)} %get-tuple-element.167.side_ref.refs_0_, f32[256,1024]{1,0:T(8,128)} %get-tuple-element.168.pa_ref, f32[256,4096]{1,0:T(8,128)} %get-tuple-element.169.pp_ref, bf16[256,1024]{1,0:T(8,128)(2,1)} %get-tuple-element.170.lat_ref, ...), custom_call_target="tpu_custom_call" | custom-call | tf_op jit(solution)/shard_map/cond/branch_0_fun/pallas_call | solution.py:52
  77.1 6.7 %all-to-all-done.3.recv_ref.r1_ref = f32[16,24,128]{2,1,0:T(8,128)S(1)} async-done(((f32[16,24,128]{2,1,0:T(8,128)}), f32[16,24,128]{2,1,0:T(8,128)S(1)}, u32[]{:S(2)}, u32[]{:S(2)}) %all-to-all-start.3) | async-done | bytes 196640 | tf_op jit(solution)/shard_map/cond/branch_0_fun/all_to_all | solution.py:916
  83.8 4.2 %branch_0_fun.35 = (bf16[256,1024]{1,0:T(8,128)(2,1)}, f32[256,1024]{1,0:T(8,128)S(1)}, f32[8,128]{1,0:T(8,128)S(1)}, f32[16,8,128]{2,1,0:T(8,128)}) custom-call(s32[1]{0:T(128)} %get-tuple-element.167.side_ref.refs_0_, f32[16,24,128]{2,1,0:T(8,128)S(1)} %all-to-all-done.3.recv_ref.r1_ref, f32[256,1024]{1,0:T(8,128)S(1)} %get-tuple-element.174.x_ref, ...), custom_call_target="tpu_custom_call" | custom-call | tf_op jit(solution)/shard_map/cond/branch_0_fun/pallas_call | solution.py:52
  92.2 6.8 %all-to-all-done.4.recv_ref = f32[16,8,128]{2,1,0:T(8,128)S(1)} async-done(((f32[16,8,128]{2,1,0:T(8,128)}), f32[16,8,128]{2,1,0:T(8,128)S(1)}, u32[]{:S(2)}, u32[]{:S(2)}) %all-to-all-start.4) | async-done | bytes 65568 | tf_op jit(solution)/shard_map/cond/branch_0_fun/all_to_all | solution.py:916
  106.1 7.2 %all-to-all-done.5.r3_ref = f32[16,24,128]{2,1,0:T(8,128)S(1)} async-done(((f32[16,24,128]{2,1,0:T(8,128)}), f32[16,24,128]{2,1,0:T(8,128)S(1)}, u32[]{:S(2)}, u32[]{:S(2)}) %all-to-all-start.5) | async-done | bytes 196640 | tf_op jit(solution)/shard_map/cond/branch_0_fun/all_to_all | solution.py:916
  113.3 11.2 %branch_0_fun.37 = (bf16[256,4096]{1,0:T(8,128)(2,1)}, f32[256,4096]{1,0:T(8,128)S(1)}, f32[16,128]{1,0:T(8,128)S(1)}, f32[16,128]{1,0:T(8,128)S(1)}, f32[16,24,128]{2,1,0:T(8,128)}) custom-call(s32[1]{0:T(128)} %get-tuple-element.167.side_ref.refs_0_, f32[16,24,128]{2,1,0:T(8,128)S(1)} %all-to-all-done.5.r3_ref, ...), custom_call_target="tpu_custom_call" | custom-call | tf_op jit(solution)/shard_map/cond/branch_0_fun/pallas_call | solution.py:52
  130.7 7.5 %all-to-all-done.6.refs_2_ = f32[16,24,128]{2,1,0:T(8,128)S(1)} async-done(((f32[16,24,128]{2,1,0:T(8,128)}), f32[16,24,128]{2,1,0:T(8,128)S(1)}, u32[]{:S(2)}, u32[]{:S(2)}) %all-to-all-start.6) | async-done | bytes 196640 | tf_op jit(solution)/shard_map/cond/branch_0_fun/all_to_all | solution.py:916
  138.2 10.8 %branch_0_fun.38 = (bf16[256,4096]{1,0:T(8,128)(2,1)}, bf16[256,4096]{1,0:T(8,128)(2,1)}, f32[256,1024]{1,0:T(8,128)S(1)}, f32[24,128]{1,0:T(8,128)}, f32[16,8,128]{2,1,0:T(8,128)S(1)}) custom-call(s32[1]{0:T(128)} %get-tuple-element.167.side_ref.refs_0_, f32[1]{0:T(128)} %bitcast.19.refs_1_.k_ref, f32[16,24,128]{2,1,0:T(8,128)S(1)} %all-to-all-done.6.refs_2_, ...), custom_call_target="tpu_custom_call" | custom-call | tf_op jit(solution)/shard_map/cond/branch_0_fun/pallas_call | solution.py:52
  149.0 10.5 %all_to_all.60.recv_ref = f32[16,8,128]{2,1,0:T(8,128)S(1)} all-to-all(f32[16,8,128]{2,1,0:T(8,128)S(1)} %get-tuple-element.435), channel_id=1, replica_groups=mesh['path'=2,'dp'=16] {'dp'}, dimensions={0} | all-to-all | bytes 131072 | tf_op jit(solution)/shard_map/cond/branch_0_fun/all_to_all | solution.py:916
  159.5 4.7 %branch_0_fun.39 = (bf16[256,1024]{1,0:T(8,128)(2,1)}, f32[256,1024]{1,0:T(8,128)S(1)}, f32[8,128]{1,0:T(8,128)}, f32[16,8,128]{2,1,0:T(8,128)}) custom-call(s32[1]{0:T(128)} %get-tuple-element.167.side_ref.refs_0_, f32[1]{0:T(128)} %bitcast.19.refs_1_.k_ref, f32[16,8,128]{2,1,0:T(8,128)S(1)} %all_to_all.60.recv_ref, ...), custom_call_target="tpu_custom_call" | custom-call | tf_op jit(solution)/shard_map/cond/branch_0_fun/pallas_call | solution.py:52
  168.7 7.5 %all-to-all-done.8.recv_ref = f32[16,8,128]{2,1,0:T(8,128)S(1)} async-done(((f32[16,8,128]{2,1,0:T(8,128)}), f32[16,8,128]{2,1,0:T(8,128)S(1)}, u32[]{:S(2)}, u32[]{:S(2)}) %all-to-all-start.8) | async-done | bytes 65568 | tf_op jit(solution)/shard_map/cond/branch_0_fun/all_to_all | solution.py:916
  176.2 3.9 %branch_0_fun.40 = (bf16[256,1024]{1,0:T(8,128)(2,1)S(1)}, bf16[256,1024]{1,0:T(8,128)(2,1)}, f32[8,128]{1,0:T(8,128)}) custom-call(s32[1]{0:T(128)} %get-tuple-element.167.side_ref.refs_0_, f32[1]{0:T(128)} %bitcast.19.refs_1_.k_ref, f32[16,8,128]{2,1,0:T(8,128)S(1)} %all-to-all-done.8.recv_ref, f32[256,1024]{1,0:T(8,128)S(1)} %copy-done.5, ...), custom_call_target="tpu_custom_call" | custom-call | tf_op jit(solution)/shard_map/cond/branch_0_fun/pallas_call | solution.py:52
  190.8 96.2 %conditional.5 = (f32[2,672,128]{2,1,0:T(8,128)}, f32[208,128]{1,0:T(8,128)S(1)}, f32[8,128]{1,0:T(8,128)S(1)}, bf16[1,1,16,16,4096]{4,3,2,1,0:T(8,128)(2,1)}) conditional(s32[]{:T(128)} %convert_element_type.12, (bf16[256,4096]{1,0:T(8,128)(2,1)}, bf16[256,1024]{1,0:T(8,128)(2,1)}, bf16[256,1024]{1,0:T(8,128)(2,1)S(1)}, ...), branch_computations={%region_6.9_spmd, %region_9.11_spmd} | conditional | flops 3268608 | bytes 49408384 | solution.py:1043
  190.8 13.6 %branch_0_fun.42 = bf16[4,4,2,672,128]{4,3,2,1,0:T(8,128)(2,1)} custom-call(bf16[256,4096]{1,0:T(8,128)(2,1)} %get-tuple-element.211.x_ref, bf16[256,1024]{1,0:T(8,128)(2,1)} %get-tuple-element.212.lat_ref, bf16[256,1024]{1,0:T(8,128)(2,1)S(1)} %get-tuple-element.213.da_ref, bf16[256,4096]{1,0:T(8,128)(2,1)} %get-tuple-element.214.dp_ref, ...), custom_call_target="tpu_custom_call" | custom-call | tf_op jit(solution)/shard_map/cond/branch_0_fun/pallas_call | solution.py:52
  204.3 40.7 %all_to_all.61 = bf16[4,4,2,672,128]{4,3,2,1,0:T(8,128)(2,1)} all-to-all(bf16[4,4,2,672,128]{4,3,2,1,0:T(8,128)(2,1)} %branch_0_fun.42), channel_id=1, replica_groups={{0,1,2,3},{4,5,6,7},{8,9,10,11},{12,13,14,15},{16,17,18,19},{20,21,22,2..., dimensions={0} | all-to-all | bytes 11010048 | tf_op jit(solution)/shard_map/cond/branch_0_fun/all_to_all | solution.py:916
  245.0 5.0 %reduce_sum.45 = bf16[4,2,672,128]{3,2,1,0:T(8,128)(2,1)} reduce(bf16[4,4,2,672,128]{4,3,2,1,0:T(8,128)(2,1)} %all_to_all.61, bf16[]{:T(256)} %constant.69.clone), dimensions={0}, to_apply=%region_7.7 | reduce | flops 2064384 | bytes 6881282 | tf_op jit(solution)/shard_map/cond/branch_0_fun/reduce_sum | solution.py:1038
  250.0 4.6 %all-to-all-start.10 = ((bf16[4,2,672,128]{3,2,1,0:T(8,128)(2,1)}), bf16[4,2,672,128]{3,2,1,0:T(8,128)(2,1)}, u32[]{:S(2)}, u32[]{:S(2)}) async-start(bf16[4,2,672,128]{3,2,1,0:T(8,128)(2,1)} %reduce_sum.45), calls=%async_computation.10 | async-start | bytes 2752512 | tf_op jit(solution)/shard_map/cond/branch_0_fun/all_to_all | solution.py:916
  254.6 6.0 %branch_0_fun.43 = bf16[256,4096]{1,0:T(8,128)(2,1)} custom-call(bf16[256,1024]{1,0:T(8,128)(2,1)} %copy-done.13, bf16[256,4096]{1,0:T(8,128)(2,1)} %get-tuple-element.214.dp_ref, bf16[1280,256]{1,0:T(8,128)(2,1)S(1)} %copy-done.12, bf16[1280,1024]{1,0:T(8,128)(2,1)S(1)} %copy-done.9), custom_call_target="tpu_custom_call" | custom-call | tf_op jit(solution)/shard_map/cond/branch_0_fun/pallas_call | solution.py:52
  260.6 22.6 %all-to-all-done.10 = bf16[4,2,672,128]{3,2,1,0:T(8,128)(2,1)} async-done(((bf16[4,2,672,128]{3,2,1,0:T(8,128)(2,1)}), bf16[4,2,672,128]{3,2,1,0:T(8,128)(2,1)}, u32[]{:S(2)}, u32[]{:S(2)}) %all-to-all-start.10) | async-done | bytes 1376288 | tf_op jit(solution)/shard_map/cond/branch_0_fun/all_to_all | solution.py:916
  (60 shorter events, 42.8 us)
Async XLA Ops:
  8.8 1.3 copy-start.10
  11.6 51.0 %copy-start.16 = (f32[8,128]{1,0:T(8,128)}, f32[8,128]{1,0:T(8,128)S(1)}, u32[]{:S(2)}) copy-start(f32[8,128]{1,0:T(8,128)S(1)} %get-tuple-element.300) | copy-start | bytes 12292
  11.6 179.1 %collective-permute-start.1 = (bf16[256,4096]{1,0:T(8,128)(2,1)}, bf16[256,4096]{1,0:T(8,128)(2,1)}, u32[]{:S(2)}, u32[]{:S(2)}) collective-permute-start(bf16[256,4096]{1,0:T(8,128)(2,1)} %get-tuple-element.301), channel_id=1, source_target_pairs={{0,16},{16,0},{1,17},{17,1},{2,18},{18,2},{3,19},{19,3},{4,20},{20... | collective-permute-start | bytes 6291464 | tf_op jit(solution)/shard_map/ppermute | solution.py:975
  57.7 4.9 %collective-permute-start = (bf16[256,1024]{1,0:T(8,128)(2,1)}, bf16[256,1024]{1,0:T(8,128)(2,1)}, u32[]{:S(2)}, u32[]{:S(2)}) collective-permute-start(bf16[256,1024]{1,0:T(8,128)(2,1)} %get-tuple-element.296), channel_id=1, source_target_pairs={{0,16},{16,0},{1,17},{17,1},{2,18},{18,2},{3,19},{19,3},{4,20},{20... | collective-permute-start | bytes 1572872 | tf_op jit(solution)/shard_map/ppermute | solution.py:974
  70.1 2.0 copy-start
  72.1 26.9 %copy-start.11 = (bf16[256,1024]{1,0:T(8,128)(2,1)S(1)}, bf16[256,1024]{1,0:T(8,128)(2,1)}, u32[]{:S(2)}) copy-start(bf16[256,1024]{1,0:T(8,128)(2,1)} %get-tuple-element.335.w_ref.refs_5_) | copy-start | bytes 1572868 | tf_op jit(solution)/shard_map/cond
  72.1 11.7 %all-to-all-start.3 = ((f32[16,24,128]{2,1,0:T(8,128)}), f32[16,24,128]{2,1,0:T(8,128)S(1)}, u32[]{:S(2)}, u32[]{:S(2)}) async-start(f32[16,24,128]{2,1,0:T(8,128)} %get-tuple-element.173), calls=%async_computation.3 | async-start | bytes 393216 | tf_op jit(solution)/shard_map/cond/branch_0_fun/all_to_all | solution.py:916
  88.0 11.0 %all-to-all-start.4 = ((f32[16,8,128]{2,1,0:T(8,128)}), f32[16,8,128]{2,1,0:T(8,128)S(1)}, u32[]{:S(2)}, u32[]{:S(2)}) async-start(f32[16,8,128]{2,1,0:T(8,128)} %get-tuple-element.178), calls=%async_computation.4 | async-start | bytes 131072 | tf_op jit(solution)/shard_map/cond/branch_0_fun/all_to_all | solution.py:916
  101.7 11.6 %all-to-all-start.5 = ((f32[16,24,128]{2,1,0:T(8,128)}), f32[16,24,128]{2,1,0:T(8,128)S(1)}, u32[]{:S(2)}, u32[]{:S(2)}) async-start(f32[16,24,128]{2,1,0:T(8,128)} %get-tuple-element.181), calls=%async_computation.5 | async-start | bytes 393216 | tf_op jit(solution)/shard_map/cond/branch_0_fun/all_to_all | solution.py:916
  124.5 2.1 copy-start.3
  126.6 11.6 %all-to-all-start.6 = ((f32[16,24,128]{2,1,0:T(8,128)}), f32[16,24,128]{2,1,0:T(8,128)S(1)}, u32[]{:S(2)}, u32[]{:S(2)}) async-start(f32[16,24,128]{2,1,0:T(8,128)} %get-tuple-element.436), calls=%async_computation.6 | async-start | bytes 393216 | tf_op jit(solution)/shard_map/cond/branch_0_fun/all_to_all | solution.py:916
  164.2 1.0 copy-start.4
  165.2 11.0 %all-to-all-start.8 = ((f32[16,8,128]{2,1,0:T(8,128)}), f32[16,8,128]{2,1,0:T(8,128)S(1)}, u32[]{:S(2)}, u32[]{:S(2)}) async-start(f32[16,8,128]{2,1,0:T(8,128)} %get-tuple-element.434), calls=%async_computation.8 | async-start | bytes 131072 | tf_op jit(solution)/shard_map/cond/branch_0_fun/all_to_all | solution.py:916
  168.7 7.5 %copy-start.5 = (f32[256,1024]{1,0:T(8,128)S(1)}, f32[256,1024]{1,0:T(8,128)}, u32[]{:S(2)}) copy-start(f32[256,1024]{1,0:T(8,128)} %copy-done.4) | copy-start | bytes 3145732 | tf_op jit(solution)/shard_map/cond
  188.6 2.2 collective-permute-start.2
  190.8 13.6 %copy-start.13 = (bf16[256,1024]{1,0:T(8,128)(2,1)}, bf16[256,1024]{1,0:T(8,128)(2,1)S(1)}, u32[]{:S(2)}) copy-start(bf16[256,1024]{1,0:T(8,128)(2,1)S(1)} %get-tuple-element.213.da_ref) | copy-start | bytes 1572868 | tf_op jit(solution)/shard_map/cond
  245.0 9.6 %copy-start.12 = (bf16[1280,256]{1,0:T(8,128)(2,1)S(1)}, bf16[1280,256]{1,0:T(8,128)(2,1)}, u32[]{:S(2)}) copy-start(bf16[1280,256]{1,0:T(8,128)(2,1)} %get-tuple-element.224.wa_ref) | copy-start | bytes 1966084 | tf_op jit(solution)/shard_map/cond
  250.0 4.6 %copy-start.9 = (bf16[1280,1024]{1,0:T(8,128)(2,1)S(1)}, bf16[1280,1024]{1,0:T(8,128)(2,1)}, u32[]{:S(2)}) copy-start(bf16[1280,1024]{1,0:T(8,128)(2,1)} %get-tuple-element.225.wp_ref) | copy-start | bytes 7864324 | tf_op jit(solution)/shard_map/cond
  250.0 33.2 %all-to-all-start.10 = ((bf16[4,2,672,128]{3,2,1,0:T(8,128)(2,1)}), bf16[4,2,672,128]{3,2,1,0:T(8,128)(2,1)}, u32[]{:S(2)}, u32[]{:S(2)}) async-start(bf16[4,2,672,128]{3,2,1,0:T(8,128)(2,1)} %reduce_sum.45), calls=%async_computation.10 | async-start | bytes 2752512 | tf_op jit(solution)/shard_map/cond/branch_0_fun/all_to_all | solution.py:916
  288.1 1.7 collective-permute-start.3

commit v2 on v1

v2 whole, which is shorter than its diff:
```python
import functools

import jax
import jax.numpy as jnp
from jax import lax
from jax.experimental import pallas as pl
from jax.experimental.pallas import tpu as pltpu
from jax.sharding import PartitionSpec as P

TS = 4
ALPHA = 8
CS = 1024
CS_MID = 256
CF = 128
CF_MID = 32
LAT = 256
TF = 32
LN = 128
EPS = 1e-05
GELU_C = 0.7978845608028654
GELU_A = 0.044715

F32 = jnp.float32
BF16 = jnp.bfloat16
SWAP = [(0, 1), (1, 0)]

ROW_SA = 0
ROW_SB = ROW_SA + (CS + LAT) * CS_MID // LN
ROW_SC = ROW_SB + 9 * CS_MID * CS_MID // LN
ROW_SP = ROW_SC + CS_MID * CS // LN
ROW_SG = ROW_SP + (CS + LAT) * CS // LN
SLOW_VEC = (2 * CS_MID + 2 * CS) // LN
ROW_FA = ROW_SG + 2 * SLOW_VEC
ROW_LAT = ROW_FA + (3 * CF * CF_MID + 9 * CF_MID * CF_MID + CF_MID * CF) // LN
ROW_FG = ROW_LAT + 5 * CF * LAT // LN
VALUES = 2685312


def dot(a, b):
    return lax.dot_general(a, b, (((1,), (0,)), ((), ())), preferred_element_type=F32)


def dot_t(a, b):
    return lax.dot_general(a, b, (((1,), (1,)), ((), ())), preferred_element_type=F32)


class Near:
    def __init__(self, array):
        self.array = array


class Far:
    def __init__(self, array, block=None, index=None):
        self.array = pltpu.with_memory_space_constraint(array, pltpu.HBM)
        self.block, self.index = block, index


class Manual(Far):
    def __init__(self, array, pinned=True):
        if isinstance(array, Near):
            self.array = pltpu.with_memory_space_constraint(array.array, pltpu.HBM)
        else:
            self.array = pltpu.with_memory_space_constraint(array, pltpu.HBM) if pinned else array
        self.block = None


def dot_l(a, b):
    return lax.dot_general(a, b, (((0,), (0,)), ((), ())), preferred_element_type=F32)


def call(body, outs, scratch, *args, smem=1, limit=20, us=2.0, after=(), token=False, through=()):
    one = not isinstance(outs, list)
    shapes, out_specs, specs, operands = [], [], [], []
    vmem, anywhere = pl.BlockSpec(memory_space=pltpu.VMEM), pl.BlockSpec(memory_space=pl.ANY)
    for out in [outs] if one else outs:
        place = out[2] if len(out) > 2 else "near"
        shapes.append(pltpu.HBM(out[0], out[1]))
        out_specs.append(anywhere if place == "manual" else vmem)
    if token:
        shapes.append(pltpu.HBM((8, LN), F32))
        out_specs.append(anywhere)
    for k, a in enumerate(args):
        if k < smem:
            specs.append(pl.BlockSpec(memory_space=pltpu.SMEM))
        elif isinstance(a, Manual):
            specs.append(anywhere)
        elif isinstance(a, Far) and a.block is not None:
            index = a.index
            specs.append(pl.BlockSpec(a.block, lambda i, index=index: index))
        else:
            specs.append(vmem)
        if isinstance(a, Near):
            a = pltpu.with_memory_space_constraint(a.array, pltpu.HBM)
        operands.append(a.array if isinstance(a, Far) else a)
    for a in after:
        specs.append(anywhere)
        operands.append(pltpu.with_memory_space_constraint(a, pltpu.HBM))
    aliases = {}
    for a in through:
        aliases[len(operands)] = len(shapes)
        specs.append(anywhere)
        operands.append(pltpu.with_memory_space_constraint(a, pltpu.HBM))
        shapes.append(pltpu.HBM(a.shape, a.dtype))
        out_specs.append(anywhere)
    n_in, n_out = len(args), len(shapes) - token - len(through)
    cut = any(isinstance(a, Far) and a.block is not None for a in args)

    def wrapped(*refs):
        rest = refs[n_in + len(after) + len(through) :]
        body(*refs[:n_in], *rest[:n_out], *rest[n_out + token + len(through) :])

    res = pl.pallas_call(
        wrapped,
        out_shape=shapes,
        grid=(1,) if cut else (),
        in_specs=specs,
        out_specs=out_specs,
        scratch_shapes=scratch,
        input_output_aliases=aliases,
        cost_estimate=pl.CostEstimate(flops=int(us * 1e9), bytes_accessed=0, transcendentals=0),
        compiler_params=pltpu.CompilerParams(vmem_limit_bytes=limit * 1024 * 1024),
    )(*operands)
    got = [
        Near(r) if len(out) == 2 else r for r, out in zip(res, [outs] if one else outs)
    ]
    got = got[0] if one else got
    if through:
        return got, list(res[n_out + token :])
    return (got, res[n_out]) if token else got


def lanes(index):
    if isinstance(index, int):
        return slice(index * LN, (index + 1) * LN)
    return pl.ds(pl.multiple_of(index * LN, LN), LN)


def region(side, px, grid):
    bits = grid.bit_length() - 1
    r = lax.broadcasted_iota(jnp.int32, (px, LN), 0)
    inside = jnp.logical_and((r >> bits) < side, (r & (grid - 1)) < side)
    return jnp.where(inside, 1.0, 0.0).astype(F32)


def rows8(x):
    return x.reshape(x.shape[0] // 8, 8, LN).sum(axis=0)


def total(acc, fold):
    if fold:
        acc = acc + pltpu.roll(acc, 32, 1)
        acc = acc + pltpu.roll(acc, 64, 1)
    return acc.sum(axis=0, keepdims=True)


def gelu(v, half_mask):
    t = jnp.tanh(v * (GELU_C + (GELU_C * GELU_A) * (v * v)))
    return v * (half_mask + half_mask * t)


def gelu_both(v, half_mask):
    w = GELU_C + (GELU_C * GELU_A) * (v * v)
    t = jnp.tanh(v * w)
    q = half_mask + half_mask * t
    return v * q, q * (1.0 + (v - v * t) * (3.0 * w - 2.0 * GELU_C))


def loop(n, body, init, unroll=False):
    if unroll:
        for i in range(n):
            init = body(i, init)
        return init
    return lax.fori_loop(0, n, body, init)


def moments(ref, out, row, blocks, params, fold, mask, count):
    inv = 1.0 / jnp.maximum(count, 1.0)
    for p in range(params):
        n = blocks // params

        def first(i, acc):
            return acc + rows8(ref[:, lanes(p + i * params)] * mask)

        zero = jnp.zeros((8, LN), F32)
        s = total(loop(n, first, zero, n <= 4), fold)
        mean = s * inv

        def second(i, acc):
            d = (ref[:, lanes(p + i * params)] - mean) * mask
            return acc + rows8(d * d)

        m2 = total(loop(n, second, zero, n <= 4), fold)
        out[row + p : row + p + 1, :] = s
        out[row + params + p : row + params + p + 1, :] = m2


def send(pay_ref, rows_ref):
    value = rows_ref[...].astype(pay_ref.dtype)
    for d in range(pay_ref.shape[0]):
        pay_ref[d] = value


def combine(recv, row, params, n, cst_ref):
    s = recv[:, row : row + params, :]
    m2 = recv[:, row + params : row + 2 * params, :]
    k = n.sum(axis=0)
    mean = s.sum(axis=0) / k
    off = s / jnp.maximum(n, 1.0) - mean[None]
    cst_ref[0:params, :] = mean
    cst_ref[params : 2 * params, :] = lax.rsqrt((m2 + n * off * off).sum(axis=0) / k + EPS)


def pick_half(int_ref, other_ref, ref, b):
    if other_ref is None:
        return ref[:, lanes(b)]
    return jnp.where(int_ref[1] == 0, other_ref[:, lanes(b)], ref[:, lanes(b)])


def fold32(v):
    v = v[:, 0:LN] + v[:, LN:256]
    v = v + pltpu.roll(v, 32, 1)
    v = v + pltpu.roll(v, 64, 1)
    return v[:, 0:CF_MID]


def pack3(pad, b, mid, left, right, px, grid):
    g, half = b // 2, b % 2
    for slot, value in enumerate((left, mid, right)):
        at = g * 768 + slot * 256 + half * 128
        pad[grid : grid + px, at : at + LN] = value.astype(BF16)


def neighbours(h, px, grid):
    col = lax.broadcasted_iota(jnp.int32, (px, LN), 0) & (grid - 1)
    before = jnp.where(col == 0, 0.0, pltpu.roll(h, 1, 0))
    after = jnp.where(col == grid - 1, 0.0, pltpu.roll(h, px - 1, 0))
    return before, after


def clear_edges(pad, px, grid):
    zero = jnp.zeros((grid, pad.shape[1]), BF16)
    pad[0:grid, :] = zero
    pad[grid + px : grid + px + grid, :] = zero


def put_count(rows_ref, row, count):
    rows_ref[row : row + 1, :] = jnp.zeros((1, LN), F32) + count


def side_sq(side, frames):
    s = side.astype(F32)
    return s * s * frames


class Net:
    def __init__(self, ndp, grid):
        self.ndp = ndp
        self.n = 2 * ndp
        self.grid = grid
        self.px = grid * grid

    def fast_first(self, ints, xf, wa, **kw):
        px, grid, n = self.px, self.grid, self.n

        def body(int_ref, xf_ref, wa_ref, lo_ref, hi_ref, band_ref, pay_ref, row_ref, fa_ref):
            side = int_ref[0]
            row_ref[...] = jnp.zeros_like(row_ref)

            @pl.when(int_ref[1] == 1)
            def _():
                pick = jnp.where(
                    (lax.broadcasted_iota(jnp.int32, (CF_MID, 256), 1) & (CF_MID - 1))
                    == lax.broadcasted_iota(jnp.int32, (CF_MID, 256), 0),
                    1.0,
                    0.0,
                ).astype(BF16)
                wide = [dot_l(wa_ref[k], pick) for k in range(3)]
                group = lax.broadcasted_iota(jnp.int32, (CF, 256), 1) >> 5
                for j in range(10):
                    acc = jnp.zeros((CF, 256), F32)
                    for k in range(3):
                        if 0 <= j - k < 8:
                            acc = jnp.where(group == j - k, wide[k], acc)
                    band_ref[j * CF : (j + 1) * CF, :] = acc.astype(BF16)
                for g in range(4):
                    lo, hi = max(8 * g - 1, 0), min(8 * g + 9, TF)
                    k0 = lo - (8 * g - 1)
                    out = dot(
                        xf_ref[:, lo * CF : hi * CF], band_ref[k0 * CF : (k0 + hi - lo) * CF, :]
                    )
                    fa_ref[:, g * 256 : (g + 1) * 256] = out
                    target = lo_ref if g < 2 else hi_ref
                    target[:, (g % 2) * 256 : (g % 2 + 1) * 256] = out
                moments(fa_ref, row_ref, 0, 8, 1, True, region(side, px, grid), side_sq(side, TF))

            put_count(row_ref, 2, side_sq(side, 1))
            send(pay_ref, row_ref)

        return call(
            body,
            [((px, 512), F32, "far"), ((px, 512), F32), ((10 * CF, 256), BF16), ((n, 4, LN), F32, "far")],
            [pltpu.VMEM((4, LN), F32), pltpu.VMEM((px, 1024), F32)],
            ints, xf, wa,
            **kw,
        )

    def fast_weights(self, wb, wbt, wc, **kw):
        def body(wb_ref, wbt_ref, wc_ref, b_ref, bt_ref, c_ref):
            pick = jnp.where(
                (lax.broadcasted_iota(jnp.int32, (CF_MID, 256), 1) & (CF_MID - 1))
                == lax.broadcasted_iota(jnp.int32, (CF_MID, 256), 0),
                1.0,
                0.0,
            ).astype(BF16)
            same = (lax.broadcasted_iota(jnp.int32, (256, 256), 0) >> 5) == (
                lax.broadcasted_iota(jnp.int32, (256, 256), 1) >> 5
            )
            for source, target in ((wb_ref, b_ref), (wbt_ref, bt_ref)):
                for tap in range(9):
                    tiled = jnp.concatenate([dot(source[tap], pick)] * 8, axis=0)
                    target[tap // 3, (tap % 3) * 256 : (tap % 3 + 1) * 256, :] = jnp.where(
                        same, tiled, 0.0
                    ).astype(BF16)
            c_ref[...] = jnp.zeros_like(c_ref)
            for i in range(8):
                c_ref[i * CF_MID : (i + 1) * CF_MID, i * CF : (i + 1) * CF] = wc_ref[...]

        return call(
            body,
            [((3, 768, 256), BF16), ((3, 768, 256), BF16), ((256, 1024), BF16)],
            [],
            wb, wbt, wc, smem=0,
            **kw,
        )

    def conv_stage(self, ints, recv, counts, x, par, w, params, frames, other=None, more=None, **kw):
        px, grid, n, ndp = self.px, self.grid, self.n, self.ndp
        fold = params == 1
        two = other is not None
        rows = 4 + (0 if more is None else more.shape[0])

        def body(int_ref, recv_ref, n_ref, x_ref, par_ref, w_ref, *refs):
            o_ref = None
            if two:
                o_ref, refs = refs[0], refs[1:]
            if more is not None:
                m_ref, refs = refs[0], refs[1:]
            h_ref, y_ref, cst_ref, pay_ref = refs[:4]
            row_ref, pad = refs[-2:]
            if two:
                refs[4][...] = recv_ref[...]
            side = int_ref[0]
            mask = region(side, px, grid)
            half_mask = 0.5 * mask
            if two:
                stats, count = recv_ref[ndp:], n_ref[ndp:, 2:3, :] * float(TF)
            else:
                stats, count = recv_ref[...], n_ref[:, 2:3, :] * float(frames)
            combine(stats, 0, params, count, cst_ref)
            mean, rs = cst_ref[0:params, :], cst_ref[params : 2 * params, :]
            scale = par_ref[0:params, :] * rs
            shift = par_ref[params : 2 * params, :] - mean * scale
            clear_edges(pad, px, grid)
            for b in range(4):
                p = b % params
                v = pick_half(int_ref, o_ref, x_ref, b) * scale[p : p + 1] + shift[p : p + 1]
                h = gelu(v, half_mask)
                h_ref[:, lanes(b)] = h.astype(BF16)
                before, after = neighbours(h, px, grid)
                pack3(pad, b, h, before, after, px, grid)
            for g in range(2):
                acc = None
                for i in range(3):
                    part = dot(pad[grid * i : grid * i + px, g * 768 : (g + 1) * 768], w_ref[i])
                    acc = part if acc is None else acc + part
                y_ref[:, g * 256 : (g + 1) * 256] = acc
            moments(y_ref, row_ref, 0, 4, params, fold, mask, side_sq(side, frames))
            if more is not None:
                row_ref[4:rows, :] = m_ref[...]
            send(pay_ref, row_ref)

        extra = [other] if two else []
        extra += [] if more is None else [more]
        return call(
            body,
            [((px, 512), BF16), ((px, 512), F32), ((8, LN), F32), ((n, rows, LN), F32, "far")]
            + ([((n, 4, LN), F32)] if two else []),
            [pltpu.VMEM((rows, LN), F32), pltpu.VMEM((px + 2 * grid, 2 * 768), BF16)],
            ints, recv, counts, x, par, w, *extra,
            **kw,
        )

    def expand_stage(self, ints, recv, counts, y, par, w, params, wide, frames, edge=False, **kw):
        px, grid, n = self.px, self.grid, self.n
        rows = max(2 * wide, 4)

        def body(int_ref, recv_ref, n_ref, y_ref, par_ref, w_ref, h_ref, cst_ref, pay_ref, *refs):
            row_ref, c_ref = refs[-2:]
            side = int_ref[0]
            mask = region(side, px, grid)
            half_mask = 0.5 * mask
            combine(recv_ref[...], 0, params, n_ref[:, 2:3, :] * float(frames), cst_ref)
            mean, rs = cst_ref[0:params, :], cst_ref[params : 2 * params, :]
            scale = par_ref[0:params, :] * rs
            shift = par_ref[params : 2 * params, :] - mean * scale
            for b in range(4):
                p = b % params
                v = y_ref[:, lanes(b)] * scale[p : p + 1] + shift[p : p + 1]
                h_ref[:, lanes(b)] = gelu(v, half_mask).astype(BF16)
            if edge:
                refs[0][...] = h_ref[:, lanes(3)]
            for g in range(2):
                c_ref[:, g * 1024 : (g + 1) * 1024] = dot(h_ref[:, g * 256 : (g + 1) * 256], w_ref[...])
            moments(c_ref, row_ref, 0, 16, wide, False, mask, side_sq(side, frames))
            send(pay_ref, row_ref)

        return call(
            body,
            [((px, 512), BF16), ((8, LN), F32), ((n, rows, LN), F32, "far")]
            + ([((px, LN), BF16, "far")] if edge else []),
            [pltpu.VMEM((rows, LN), F32), pltpu.VMEM((px, 2048), F32)],
            ints, recv, counts, y, par, w,
            **kw,
        )

    def fast_finish(self, ints, recv, counts, h2, h2_other, w, xf, par, wlat, **kw):
        px, grid = self.px, self.grid

        def body(
            int_ref, recv_ref, n_ref, h_ref, ho_ref, w_ref, xf_ref, par_ref, wl_ref,
            y_ref, lat_ref, cst_ref, c_ref,
        ):
            half_mask = 0.5 * region(int_ref[0], px, grid)
            combine(recv_ref[...], 0, 1, n_ref[:, 2:3, :] * float(TF // 2), cst_ref)
            scale = par_ref[0:1, :] * cst_ref[1:2, :]
            shift = par_ref[1:2, :] - cst_ref[0:1, :] * scale
            c_ref[:, 0:256] = dot(ho_ref[...], w_ref[0:LN, 256:512])
            edge = half_mask * int_ref[1].astype(F32)
            for f in range(2):
                v = c_ref[:, lanes(f)] * scale + shift + xf_ref[:, lanes(f)].astype(F32)
                y_ref[:, lanes(f)] = jnp.where(int_ref[1] == 1, gelu(v, edge), 0.0).astype(BF16)
            for g in range(2):
                c_ref[...] = dot(h_ref[:, g * 256 : (g + 1) * 256], w_ref[...])

                def step(i, carry):
                    f = 2 + g * 8 + i
                    v = c_ref[:, lanes(i)] * scale + shift + xf_ref[:, lanes(f)].astype(F32)
                    y_ref[:, lanes(f)] = gelu(v, half_mask).astype(BF16)
                    return carry

                loop(8, step, 0)
            for t in range(2):
                at = ALPHA * t * CF
                lat_ref[:, t * LAT : (t + 1) * LAT] = dot(y_ref[:, at : at + 5 * CF], wl_ref[...]).astype(BF16)

        return call(
            body,
            [((px, 18 * CF), BF16), ((px, 512), BF16), ((8, LN), F32)],
            [pltpu.VMEM((px, 1024), F32)],
            ints, recv, counts, h2, h2_other, w, xf, par, wlat,
            **kw,
        )

    def fast_slope(self, ints, h2, w, xf, par, cst, **kw):
        px, grid = self.px, self.grid

        def body(int_ref, h_ref, w_ref, xf_ref, par_ref, cst_ref, gp_ref, c_ref):
            half_mask = 0.5 * region(int_ref[0], px, grid)
            scale = par_ref[0:1, :] * cst_ref[1:2, :]
            shift = par_ref[1:2, :] - cst_ref[0:1, :] * scale
            for g in range(2):
                c_ref[...] = dot(h_ref[:, g * 256 : (g + 1) * 256], w_ref[...])

                def step(i, carry):
                    f = g * 8 + i
                    v = c_ref[:, lanes(i)] * scale + shift + xf_ref[:, lanes(f + 2)].astype(F32)
                    gp_ref[:, lanes(f)] = gelu_both(v, half_mask)[1]
                    return carry

                loop(8, step, 0)

        return call(body, ((px, 2048), F32), [pltpu.VMEM((px, 1024), F32)], ints, h2, w, xf, par, cst, **kw)

    def slow_start(self, xs, wa, wp, **kw):
        px = self.px

        def body(x_ref, wa_ref, wp_ref, a_ref, p_ref):
            for t in range(2):
                x = x_ref[:, t * CS : (t + 1) * CS]
                a_ref[:, t * CS_MID : (t + 1) * CS_MID] = dot(x, wa_ref[0:CS, :])
                p_ref[:, t * CS : (t + 1) * CS] = dot(x, wp_ref[0:CS, :])

        return call(body, [((px, 512), F32), ((px, 2048), F32)], [], xs, wa, wp, smem=0, **kw)

    def slow_join(self, ints, part, lat, w, params, alone=True, **kw):
        px, grid, n = self.px, self.grid, self.n
        width = params * LN
        rows = max(2 * params, 4)

        def body(int_ref, part_ref, lat_ref, w_ref, out_ref, pay_ref, *refs):
            row_ref = refs[0] if alone else pay_ref
            side = int_ref[0]
            for t in range(2):
                at = slice(t * width, (t + 1) * width)
                out_ref[:, at] = part_ref[:, at] + dot(lat_ref[:, t * LAT : (t + 1) * LAT], w_ref[...])
            moments(
                out_ref, row_ref, 0, 2 * params, params, False, region(side, px, grid), side_sq(side, TS // 2)
            )
            if alone:
                send(pay_ref, row_ref)

        return call(
            body,
            [((px, 2 * width), F32), ((n, rows, LN) if alone else (rows, LN), F32, "far")],
            [pltpu.VMEM((rows, LN), F32)] if alone else [],
            ints, part, lat, w,
            **kw,
        )

    def slow_top(self, ints, recv3, recvp, counts, h2, w, sp, gs, parc, parp, **kw):
        px, grid, n = self.px, self.grid, self.n

        def body(
            int_ref, r3_ref, rp_ref, n_ref, h_ref, w_ref, sp_ref, gs_ref, pc_ref, pp_ref,
            ys_ref, ds_ref, cc_ref, cp_ref, pay_ref, row_ref, c_ref, acc_ref, k_ref,
        ):
            half_mask = 0.5 * region(int_ref[0], px, grid)
            count = n_ref[:, 2:3, :] * float(TS // 2)
            combine(r3_ref[...], 0, 8, count, cc_ref)
            combine(rp_ref[...], 4, 8, count, cp_ref)
            k_ref[0:8, :] = pc_ref[0:8, :] * cc_ref[8:16, :]
            k_ref[8:16, :] = pp_ref[0:8, :] * cp_ref[8:16, :]
            k_ref[16:24, :] = pc_ref[8:16, :] + pp_ref[8:16, :]
            acc_ref[...] = jnp.zeros_like(acc_ref)
            for t in range(2):
                c_ref[...] = dot(h_ref[:, t * 256 : (t + 1) * 256], w_ref[...])

                def step(b, carry):
                    at = lanes(t * 8 + b)
                    one = pl.ds(b, 1)
                    xc = c_ref[:, lanes(b)] - cc_ref[one, :]
                    xp = sp_ref[:, at] - cp_ref[one, :]
                    v = xc * k_ref[one, :] + (xp * k_ref[pl.ds(b + 8, 1), :] + k_ref[pl.ds(b + 16, 1), :])
                    y, slope = gelu_both(v, half_mask)
                    ys_ref[:, at] = y.astype(BF16)
                    d = gs_ref[:, at].astype(F32) * slope
                    ds_ref[:, at] = d
                    acc_ref[b] += rows8(d)
                    acc_ref[8 + b] += rows8(d * xc)
                    acc_ref[16 + b] += rows8(d * xp)
                    return carry

                loop(8, step, 0)
            row_ref[...] = acc_ref[...].sum(axis=1)
            row_ref[8:16, :] = row_ref[8:16, :] * cc_ref[8:16, :]
            row_ref[16:24, :] = row_ref[16:24, :] * cp_ref[8:16, :]
            send(pay_ref, row_ref)

        return call(
            body,
            [
                ((px, 2048), BF16), ((px, 2048), F32), ((16, LN), F32), ((16, LN), F32),
                ((n, 24, LN), BF16, "far"),
            ],
            [
                pltpu.VMEM((24, LN), F32), pltpu.VMEM((px, 1024), F32),
                pltpu.VMEM((24, 8, LN), F32), pltpu.VMEM((24, LN), F32),
            ],
            ints, recv3, recvp, counts, h2, w, sp, gs, parc, parp,
            **kw,
        )

    def fast_top(self, ints, dl0, dl1, dl_other, wlat, gf, gp, h2, w, cst, **kw):
        px, n = self.px, self.n

        def body(
            int_ref, d0_ref, d1_ref, do_ref, wl_ref, gf_ref, gp_ref, h_ref, w_ref, cst_ref,
            ds_ref, pay_ref, row_ref, lt_ref, c_ref, acc_ref,
        ):
            first = (1 - int_ref[1]).astype(F32)
            lt_ref[:, 0 : 3 * CF] = dot_t(d0_ref[...], wl_ref[2 * CF :, :])
            lt_ref[:, 3 * CF : 8 * CF] = dot_t(d1_ref[...], wl_ref[...])
            edge = dot_t(do_ref[...], wl_ref[0 : 2 * CF, :])
            lt_ref[:, 8 * CF : 10 * CF] = jnp.where(int_ref[1] == 0, edge, 0.0)
            acc_ref[...] = jnp.zeros_like(acc_ref)
            mean, rs = cst_ref[0:1, :], cst_ref[1:2, :]
            where = {0: 0, 1: 1, 2: 2, 6: 3, 7: 4, 8: 5, 9: 6, 10: 7, 14: 8, 15: 9}
            for g in range(2):
                c_ref[...] = dot(h_ref[:, g * 256 : (g + 1) * 256], w_ref[...])
                for i in range(8):
                    f = g * 8 + i
                    d = gf_ref[:, lanes(f)].astype(F32)
                    if f in where:
                        d = d + lt_ref[:, lanes(where[f])]
                    d = d * gp_ref[:, lanes(f)]
                    ds_ref[:, lanes(f)] = d
                    acc_ref[0] += rows8(d)
                    acc_ref[1] += rows8(d * (c_ref[:, lanes(i)] - mean))
            row_ref[...] = jnp.zeros_like(row_ref)
            row_ref[0:1, :] = acc_ref[0].sum(axis=0, keepdims=True)
            row_ref[1:2, :] = acc_ref[1].sum(axis=0, keepdims=True) * rs
            send(pay_ref, row_ref)

        return call(
            body,
            [((px, 2048), F32), ((n, 4, LN), F32, "far")],
            [
                pltpu.VMEM((4, LN), F32), pltpu.VMEM((px, 10 * CF), F32),
                pltpu.VMEM((px, 1024), F32), pltpu.VMEM((2, 8, LN), F32),
            ],
            ints, dl0, dl1, dl_other, wlat, gf, gp, h2, w, cst,
            **kw,
        )

    def expand_back(self, ints, counts, recv, ds, h2, w, cstw, parw, y, cst, par, params, wide, frames, shortcut=None, **kw):
        px, grid, n = self.px, self.grid, self.n
        fold = params == 1
        both = shortcut is not None
        srows = 3 * wide if both else 4

        def body(*refs):
            int_ref, n_ref, recv_ref, ds_ref, h_ref, w_ref, cw_ref, pw_ref, y_ref, cs_ref, par_ref = refs[:11]
            refs = refs[11:]
            if both:
                sp_ref, cp_ref, pp_ref, dp_ref = refs[:4]
                refs = refs[4:]
            dc_ref, dn_ref, sum_ref, pay_ref, row_ref, c_ref, k3_ref = refs
            mask = region(int_ref[0], px, grid)
            half_mask = 0.5 * mask
            inv_k = 1.0 / (n_ref[:, 2:3, :].sum(axis=0) * float(frames))
            sums = recv_ref[...].astype(F32).sum(axis=0)
            sum_ref[...] = sums
            a = pw_ref[0:wide, :] * cw_ref[wide : 2 * wide, :]
            k3_ref[0:wide, :] = a
            k3_ref[wide : 2 * wide, :] = a * inv_k * sums[0:wide]
            k3_ref[2 * wide : 3 * wide, :] = a * inv_k * cw_ref[wide : 2 * wide, :] * sums[wide : 2 * wide]
            if both:
                a = pp_ref[0:wide, :] * cp_ref[wide : 2 * wide, :]
                k3_ref[3 * wide : 4 * wide, :] = a
                k3_ref[4 * wide : 5 * wide, :] = a * inv_k * sums[0:wide]
                k3_ref[5 * wide : 6 * wide, :] = (
                    a * inv_k * cp_ref[wide : 2 * wide, :] * sums[2 * wide : 3 * wide]
                )
            mean, rs = cs_ref[0:params, :], cs_ref[params : 2 * params, :]
            accs = [[jnp.zeros((8, LN), F32) for _ in range(params)] for _ in range(2)]
            for g in range(2):
                c_ref[...] = dot(h_ref[:, g * 256 : (g + 1) * 256], w_ref[...])

                def step(b, carry):
                    at = lanes(g * 8 + b)
                    p = b if wide == 8 else 0
                    d = ds_ref[:, at]
                    e = (c_ref[:, lanes(b)] - cw_ref[pl.ds(p, 1), :]) * k3_ref[pl.ds(2 * wide + p, 1), :]
                    e = d * k3_ref[pl.ds(p, 1), :] - k3_ref[pl.ds(wide + p, 1), :] - e
                    dc_ref[:, at] = (e * mask).astype(BF16)
                    if both:
                        e = (sp_ref[:, at] - cp_ref[pl.ds(p, 1), :]) * k3_ref[pl.ds(5 * wide + p, 1), :]
                        e = d * k3_ref[pl.ds(3 * wide + p, 1), :] - k3_ref[pl.ds(4 * wide + p, 1), :] - e
                        dp_ref[:, at] = (e * mask).astype(BF16)
                    return carry

                loop(8, step, 0)
                dh = dot_t(dc_ref[:, g * 1024 : (g + 1) * 1024], w_ref[...])
                for half in range(2):
                    b = g * 2 + half
                    p = b % params
                    xh = (y_ref[:, lanes(b)] - mean[p : p + 1]) * rs[p : p + 1]
                    v = xh * par_ref[p : p + 1, :] + par_ref[params + p : params + p + 1, :]
                    d = dh[:, half * LN : (half + 1) * LN] * gelu_both(v, half_mask)[1]
                    dn_ref[:, lanes(b)] = d
                    accs[0][p] = accs[0][p] + rows8(d)
                    accs[1][p] = accs[1][p] + rows8(d * xh)
            row_ref[...] = jnp.zeros_like(row_ref)
            for q in range(2):
                for p in range(params):
                    row_ref[q * params + p : q * params + p + 1, :] = total(accs[q][p], fold)
            send(pay_ref, row_ref)

        outs = [((px, 2048), BF16)] if both else []
        outs += [((px, 2048), BF16), ((px, 512), F32), ((srows, LN), F32, "far"), ((n, 4, LN), F32, "far")]
        extra = list(shortcut) if both else []
        return call(
            body,
            outs,
            [pltpu.VMEM((4, LN), F32), pltpu.VMEM((px, 1024), F32), pltpu.VMEM((max(6 * wide, 8), LN), F32)],
            ints, counts, recv, ds, h2, w, cstw, parw, y, cst, par, *extra,
            **kw,
        )

    def conv_back(self, ints, counts, recv, dn, y, cst2, par2, wt, x, cst1, par1, params, frames, other=None, **kw):
        px, grid, n = self.px, self.grid, self.n
        fold = params == 1
        two = other is not None

        def body(int_ref, n_ref, recv_ref, dn_ref, y_ref, c2_ref, p2_ref, w_ref, x_ref, c1_ref, p1_ref, *refs):
            o_ref = None
            if two:
                o_ref, refs = refs[0], refs[1:]
            db_ref, dn1_ref, sum_ref, pay_ref, row_ref, pad = refs
            mask = region(int_ref[0], px, grid)
            half_mask = 0.5 * mask
            inv_k = 1.0 / (n_ref[:, 2:3, :].sum(axis=0) * float(frames))
            sums = recv_ref[...].astype(F32).sum(axis=0)
            sum_ref[...] = sums
            mean2, rs2 = c2_ref[0:params, :], c2_ref[params : 2 * params, :]
            a = p2_ref[0:params, :] * rs2
            b0 = a * inv_k * sums[0:params]
            c0 = a * inv_k * rs2 * sums[params : 2 * params]
            clear_edges(pad, px, grid)
            for b in range(4):
                p = b % params
                e = (y_ref[:, lanes(b)] - mean2[p : p + 1]) * c0[p : p + 1]
                e = (dn_ref[:, lanes(b)] * a[p : p + 1] - b0[p : p + 1] - e) * mask
                db_ref[:, lanes(b)] = e.astype(BF16)
                before, after = neighbours(e, px, grid)
                pack3(pad, b, e, after, before, px, grid)
            mean, rs = c1_ref[0:params, :], c1_ref[params : 2 * params, :]
            accs = [[jnp.zeros((8, LN), F32) for _ in range(params)] for _ in range(2)]
            for g in range(2):
                dh = None
                for i in range(3):
                    part = dot(pad[grid * i : grid * i + px, g * 768 : (g + 1) * 768], w_ref[2 - i])
                    dh = part if dh is None else dh + part
                for half in range(2):
                    b = g * 2 + half
                    p = b % params
                    xh = (pick_half(int_ref, o_ref, x_ref, b) - mean[p : p + 1]) * rs[p : p + 1]
                    v = xh * p1_ref[p : p + 1, :] + p1_ref[params + p : params + p + 1, :]
                    d = dh[:, half * LN : (half + 1) * LN] * gelu_both(v, half_mask)[1]
                    dn1_ref[:, lanes(b)] = d
                    accs[0][p] = accs[0][p] + rows8(d)
                    accs[1][p] = accs[1][p] + rows8(d * xh)
            row_ref[...] = jnp.zeros_like(row_ref)
            for q in range(2):
                for p in range(params):
                    row_ref[q * params + p : q * params + p + 1, :] = total(accs[q][p], fold)
            send(pay_ref, row_ref)

        extra = [other] if two else []
        return call(
            body,
            [((px, 512), BF16), ((px, 512), F32), ((4, LN), F32, "far"), ((n, 4, LN), F32, "far")],
            [pltpu.VMEM((4, LN), F32), pltpu.VMEM((px + 2 * grid, 2 * 768), BF16)],
            ints, counts, recv, dn, y, cst2, par2, wt, x, cst1, par1, *extra,
            **kw,
        )

    def slow_last(self, ints, counts, recv, dn, x, cst, par, dp, wa, wp, **kw):
        px, grid = self.px, self.grid

        def body(
            int_ref, n_ref, recv_ref, dn_ref, x_ref, cst_ref, par_ref, dp_ref, wa_ref, wp_ref,
            da_ref, d0_ref, d1_ref, sum_ref,
        ):
            mask = region(int_ref[0], px, grid)
            inv_k = 1.0 / (n_ref[:, 2:3, :].sum(axis=0) * float(TS // 2))
            sums = recv_ref[...].astype(F32).sum(axis=0)
            sum_ref[...] = sums
            mean, rs = cst_ref[0:2, :], cst_ref[2:4, :]
            a = par_ref[0:2, :] * rs
            b0 = a * inv_k * sums[0:2]
            c0 = a * inv_k * rs * sums[2:4]
            for b in range(4):
                p = b % 2
                e = (x_ref[:, lanes(b)] - mean[p : p + 1]) * c0[p : p + 1]
                e = (dn_ref[:, lanes(b)] * a[p : p + 1] - b0[p : p + 1] - e) * mask
                da_ref[:, lanes(b)] = e.astype(BF16)
            for t, out in ((0, d0_ref), (1, d1_ref)):
                out[...] = (
                    dot_t(da_ref[:, t * CS_MID : (t + 1) * CS_MID], wa_ref[...])
                    + dot_t(dp_ref[:, t * CS : (t + 1) * CS], wp_ref[...])
                ).astype(BF16)

        return call(
            body,
            [((px, 512), BF16), ((px, LAT), BF16), ((px, LAT), BF16), ((4, LN), F32, "far")],
            [],
            ints, counts, recv, dn, x, cst, par, dp, wa, wp,
            **kw,
        )

    def slow_input_grad(self, da, dp, wa, wp, **kw):
        px = self.px

        def body(da_ref, dp_ref, wa_ref, wp_ref, dx_ref):
            for t in range(2):
                dx_ref[:, t * CS : (t + 1) * CS] = (
                    dot_t(da_ref[:, t * CS_MID : (t + 1) * CS_MID], wa_ref[0:CS, :])
                    + dot_t(dp_ref[:, t * CS : (t + 1) * CS], wp_ref[0:CS, :])
                ).astype(BF16)

        return call(body, ((px, 2048), BF16, "far"), [], da, dp, wa, wp, smem=0, **kw)

    def fast_first_back(self, ints, counts, recv, dn_lo, dn_hi, fa_lo, fa_hi, cst, par, xf, bc, bc_other, **kw):
        px, grid, ndp = self.px, self.grid, self.ndp
        rows = bc.shape[0]

        def body(
            int_ref, n_ref, recv_ref, dl_ref, dh_ref, xl_ref, xh_ref, cst_ref, par_ref, x_ref, b0_ref, b1_ref,
            da_ref, sum_ref, pay_ref, row_ref,
        ):
            sums = recv_ref[...].sum(axis=0)
            sum_ref[...] = sums
            row_ref[...] = b0_ref[...] + b1_ref[...]

            @pl.when(int_ref[1] == 1)
            def _():
                mask = region(int_ref[0], px, grid)
                inv_k = 1.0 / (n_ref[:, 2:3, :].sum(axis=0) * float(TF // 2))
                mean, rs = cst_ref[0:1, :], cst_ref[1:2, :]
                a = par_ref[0:1, :] * rs
                b0 = a * inv_k * sums[0:1]
                c0 = a * inv_k * rs * sums[1:2]
                for dn_ref, h_ref, base in ((dl_ref, xl_ref, 0), (dh_ref, xh_ref, 4)):
                    for b in range(4):
                        e = (h_ref[:, lanes(b)] - mean) * c0
                        e = (dn_ref[:, lanes(b)] * a - b0 - e) * mask
                        da_ref[:, lanes(base + b)] = e.astype(BF16)
                accs = [None] * 3
                for g in range(4):
                    lo, hi = max(8 * g - 1, 0), min(8 * g + 9, TF)
                    k0 = lo - (8 * g - 1)
                    d = dot(da_ref[:, g * 256 : (g + 1) * 256].T, x_ref[:, lo * CF : hi * CF])
                    for k in range(3):
                        for i in range(8):
                            j = i + k - k0
                            if 0 <= j < hi - lo:
                                part = d[i * CF_MID : (i + 1) * CF_MID, j * CF : (j + 1) * CF]
                                accs[k] = part if accs[k] is None else accs[k] + part
                for k in range(3):
                    row_ref[k * CF_MID : (k + 1) * CF_MID, :] = accs[k]

            send(pay_ref, row_ref)

        return call(
            body,
            [((px, 1024), BF16), ((4, LN), F32, "far"), ((ndp, rows, LN), BF16, "far")],
            [pltpu.VMEM((rows, LN), F32)],
            ints, counts, recv, dn_lo, dn_hi, fa_lo, fa_hi, cst, par, xf, bc, bc_other,
            **kw,
        )

    def last(self, ints, da, ds_lo, ds_hi, band, dxs0, dxs1, **kw):
        px = self.px

        def body(int_ref, da_ref, sl_ref, sh_ref, band_ref, x0_ref, x1_ref, dx_ref, acc_ref, out_ref, sem):
            def part(g):
                at = slice(g * 1024, (g + 1) * 1024)
                return pltpu.make_async_copy(out_ref.at[:, at], dx_ref.at[:, at], sem.at[g])

            def half(ref, g):
                return pltpu.make_async_copy(ref, out_ref.at[:, g * 2048 : (g + 1) * 2048], sem.at[g])

            @pl.when(int_ref[1] == 0)
            def _():
                half(x0_ref, 0).start()
                half(x1_ref, 1).start()
                half(x0_ref, 0).wait()
                half(x1_ref, 1).wait()
                for g in range(4):
                    part(g).start()
                for g in range(4):
                    part(g).wait()

            @pl.when(int_ref[1] == 1)
            def _():
                acc_ref[:, 0 : 10 * CF] = dot_t(da_ref[:, 0:256], band_ref[...])
                for g in range(4):
                    if g < 3:
                        p = dot_t(da_ref[:, (g + 1) * 256 : (g + 2) * 256], band_ref[...])
                        base = 8 * (g + 1) * CF
                        acc_ref[:, base : base + 2 * CF] += p[:, 0 : 2 * CF]
                        acc_ref[:, base + 2 * CF : base + 10 * CF] = p[:, 2 * CF :]
                    s_ref = sl_ref if g < 2 else sh_ref
                    for i in range(8):
                        f = 8 * g + i
                        s = s_ref[:, lanes(f % 16)] + acc_ref[:, lanes(f + 1)]
                        out_ref[:, lanes(f)] = s.astype(BF16)
                    part(g).start()
                for g in range(4):
                    part(g).wait()

        return call(
            body,
            ((px, 4096), BF16, "manual"),
            [pltpu.VMEM((px, 34 * CF), F32), pltpu.VMEM((px, 4096), BF16), pltpu.SemaphoreType.DMA((4,))],
            ints, da, ds_lo, ds_hi, band, Manual(dxs0), Manual(dxs1),
            **kw,
        )

    def halves(self, ints, x, x_other, cot, cot_other, **kw):
        px = self.px

        def body(int_ref, x_ref, xo_ref, c_ref, co_ref, xs_ref, xf_ref, gs_ref, gf_ref, sem):
            def run(pairs):
                copies = [pltpu.make_async_copy(a, b, sem.at[k]) for k, (a, b) in enumerate(pairs)]
                for c in copies:
                    c.start()
                for c in copies:
                    c.wait()

            lo, hi = slice(0, 2048), slice(2048, 4096)

            @pl.when(int_ref[1] == 0)
            def _():
                xf_ref[:, 0 : 2 * CF] = jnp.zeros((px, 2 * CF), BF16)
                run([
                    (x_ref.at[:, lo], xs_ref), (xo_ref.at[:, lo], xf_ref.at[:, 2 * CF : 18 * CF]),
                    (c_ref.at[:, lo], gs_ref), (co_ref.at[:, lo], gf_ref),
                ])

            @pl.when(int_ref[1] == 1)
            def _():
                run([
                    (xo_ref.at[:, hi], xs_ref), (x_ref.at[:, 14 * CF :], xf_ref),
                    (co_ref.at[:, hi], gs_ref), (c_ref.at[:, hi], gf_ref),
                ])

        wide = ((px, 2048), BF16)
        return call(
            body,
            [wide, ((px, 18 * CF), BF16), wide, wide],
            [pltpu.SemaphoreType.DMA((4,))],
            ints, Manual(x), Manual(x_other), Manual(cot), Manual(cot_other),
            **kw,
        )

    def out_send(self, ints, ys, yf, **kw):
        px = self.px

        def body(int_ref, ys_ref, yf_ref, out_ref):
            for path, ref, at in ((0, yf_ref, 2 * CF), (1, ys_ref, 0)):

                @pl.when(int_ref[1] == path)
                def _():
                    out_ref[...] = ref[:, at : at + 2048]

        return call(body, ((px, 2048), BF16, "far"), [], ints, ys, yf, **kw)

    def out_join(self, ints, ys, yf, other, **kw):
        px = self.px

        def body(int_ref, ys_ref, yf_ref, o_ref, out_ref):
            for path, ref, at in ((0, ys_ref, 0), (1, yf_ref, 2 * CF)):

                @pl.when(int_ref[1] == path)
                def _():
                    mine, far = path * 2048, (1 - path) * 2048
                    out_ref[:, mine : mine + 2048] = ref[:, at : at + 2048]
                    out_ref[:, far : far + 2048] = o_ref[...]

        return call(body, ((px, 4096), BF16, "far"), [], ints, ys, yf, Far(other), **kw)

    def fast_grads_bc(self, h1, db, h2, dc, **kw):
        px, grid = self.px, self.grid

        def body(h1_ref, db_ref, h2_ref, dc_ref, gb_ref, gc_ref, pad):
            clear_edges(pad, px, grid)
            for b in range(4):
                h = h1_ref[:, lanes(b)].astype(F32)
                before, after = neighbours(h, px, grid)
                pack3(pad, b, h, before, after, px, grid)
            same = (lax.broadcasted_iota(jnp.int32, (256, 256), 0) >> 5) == (
                lax.broadcasted_iota(jnp.int32, (256, 256), 1) >> 5
            )
            for i in range(3):
                for s in range(3):
                    acc = jnp.zeros((256, 256), F32)
                    for g in range(2):
                        at = g * 768 + s * 256
                        acc = acc + dot(
                            pad[grid * i : grid * i + px, at : at + 256].T,
                            db_ref[:, g * 256 : (g + 1) * 256],
                        )
                    acc = jnp.where(same, acc, 0.0).reshape(8, CF_MID, 256).sum(axis=0)
                    gb_ref[3 * i + s] = fold32(acc)
            acc = jnp.zeros((256, 1024), F32)
            for g in range(2):
                acc = acc + dot(h2_ref[:, g * 256 : (g + 1) * 256].T, dc_ref[:, g * 1024 : (g + 1) * 1024])
            out = None
            for i in range(8):
                part = acc[i * CF_MID : (i + 1) * CF_MID, i * CF : (i + 1) * CF]
                out = part if out is None else out + part
            gc_ref[...] = out

        return call(
            body,
            [((9, CF_MID, CF_MID), F32, "far"), ((CF_MID, CF), F32, "far")],
            [pltpu.VMEM((px + 2 * grid, 2 * 768), BF16)],
            h1, db, h2, dc, smem=0,
            **kw,
        )

    def grads_early(self, plan, ints, xs, lat, dp, h2, dc, **kw):
        px = self.px
        rows = plan.early

        def body(int_ref, x_ref, lat_ref, dp_ref, h2_ref, dc_ref, keep_ref, send_ref, buf, xt):
            def put(base, q, acc):
                for j in range(2):
                    buf[pl.ds(base + 2 * q + j, 256, stride=8), :] = acc[:, j * LN : (j + 1) * LN]

            for c in range(6):
                for t in range(2):
                    if c == 5:
                        x = h2_ref[:, t * 256 : (t + 1) * 256]
                    elif c == 4:
                        x = lat_ref[:, t * LAT : (t + 1) * LAT]
                    else:
                        x = x_ref[:, t * CS + c * 256 : t * CS + (c + 1) * 256]
                    xt[:, t * px : (t + 1) * px] = x.T
                source = dc_ref if c == 5 else dp_ref
                base = (ROW_SC if c == 5 else ROW_SP + c * 2048) - ROW_SC
                for q in range(4):
                    acc = None
                    for t in range(2):
                        at = t * CS + q * 256
                        part = dot(xt[:, t * px : (t + 1) * px], source[:, at : at + 256])
                        acc = part if acc is None else acc + part
                    put(base, q, acc)
            lo = 0
            hi = plan.base[1] - ROW_SC
            mine = pl.multiple_of(jnp.where(int_ref[1] == 0, lo, hi), 16)
            other = pl.multiple_of(jnp.where(int_ref[1] == 0, hi, lo), 16)
            keep_ref[...] = buf[pl.ds(mine, rows), :].astype(BF16)
            send_ref[...] = buf[pl.ds(other, rows), :].astype(BF16)

        return call(
            body,
            [((rows, LN), BF16, "far"), ((rows, LN), BF16, "far")],
            [pltpu.VMEM((ROW_SG - ROW_SC, LN), F32), pltpu.VMEM((256, 2 * px), BF16)],
            ints, xs, lat, dp, h2, dc,
            **kw,
        )

    def grads_conv(self, h1, db, **kw):
        px, grid = self.px, self.grid

        def body(h1_ref, db_ref, out_ref, buf, pad):
            clear_edges(pad, px, grid)
            for b in range(4):
                h = h1_ref[:, lanes(b)].astype(F32)
                before, after = neighbours(h, px, grid)
                pack3(pad, b, h, before, after, px, grid)
            for i in range(3):
                for s in range(3):
                    acc = None
                    for t in range(2):
                        at = t * 768 + s * 256
                        part = dot(
                            pad[grid * i : grid * i + px, at : at + 256].T,
                            db_ref[:, t * 256 : (t + 1) * 256],
                        )
                        acc = part if acc is None else acc + part
                    for j in range(2):
                        buf[pl.ds((3 * i + s) * 512 + j, 256, stride=2), :] = acc[:, j * LN : (j + 1) * LN]
            out_ref[...] = buf[...].astype(BF16)

        return call(
            body,
            ((ROW_SC - ROW_SB, LN), BF16, "far"),
            [pltpu.VMEM((ROW_SC - ROW_SB, LN), F32), pltpu.VMEM((px + 2 * grid, 2 * 768), BF16)],
            h1, db, smem=0,
            **kw,
        )

    def grads_late(self, ints, xs, lat, da, yf, dl0, dl1, **kw):
        px = self.px
        rows = ROW_SB - ROW_SA
        lat_rows = ROW_FG - ROW_LAT

        def body(int_ref, x_ref, lat_ref, da_ref, yf_ref, d0_ref, d1_ref, keep_ref, send_ref, buf):
            for c in range(5):
                acc = None
                for t in range(2):
                    if c == 4:
                        x = lat_ref[:, t * LAT : (t + 1) * LAT]
                    else:
                        x = x_ref[:, t * CS + c * 256 : t * CS + (c + 1) * 256]
                    part = dot(x.T, da_ref[:, t * CS_MID : (t + 1) * CS_MID])
                    acc = part if acc is None else acc + part
                for j in range(2):
                    buf[pl.ds(c * 512 + j, 256, stride=2), :] = acc[:, j * LN : (j + 1) * LN]
            for k in range(5):
                acc = dot(yf_ref[:, lanes(k)].T, d0_ref[...]) + dot(yf_ref[:, lanes(8 + k)].T, d1_ref[...])
                for j in range(2):
                    buf[pl.ds(rows + k * 256 + j, CF, stride=2), :] = acc[:, j * LN : (j + 1) * LN]
            mine = pl.multiple_of(jnp.where(int_ref[1] == 0, 0, rows), 16)
            other = pl.multiple_of(jnp.where(int_ref[1] == 0, rows, 0), 16)
            keep_ref[...] = buf[pl.ds(mine, rows), :].astype(BF16)
            send_ref[...] = buf[pl.ds(other, rows), :].astype(BF16)

        return call(
            body,
            [((rows, LN), BF16, "far"), ((rows, LN), BF16, "far")],
            [pltpu.VMEM((2 * rows, LN), F32)],
            ints, xs, lat, da, yf, dl0, dl1,
            **kw,
        )

    def windows(self, plan, ints, early, conv, late, **kw):
        ndp, chunk, half = self.ndp, plan.chunk, self.ndp // 2

        def body(int_ref, e0_ref, e1_ref, c0_ref, c1_ref, l0_ref, l1_ref, keep_ref, send_ref, buf):
            def add(a, b, rows):
                return a[0:rows, :].astype(F32) + b[0:rows, :].astype(F32)

            for path in range(2):

                @pl.when(int_ref[1] == path)
                def _():
                    buf[...] = jnp.zeros_like(buf)
                    base = plan.base[path]
                    if path == 0:
                        buf[ROW_SA:ROW_SB, :] = add(l0_ref, l1_ref, ROW_SB - ROW_SA)
                        buf[ROW_SB:ROW_SC, :] = add(c0_ref, c1_ref, ROW_SC - ROW_SB)
                        rest = min(plan.length - ROW_SC, plan.early)
                        buf[ROW_SC : ROW_SC + rest, :] = add(e0_ref, e1_ref, rest)
                    else:
                        rest = ROW_SG - base
                        buf[0:rest, :] = add(e0_ref, e1_ref, rest)
                        at = ROW_LAT - base
                        buf[at : at + ROW_FG - ROW_LAT, :] = add(l0_ref, l1_ref, ROW_FG - ROW_LAT)

            path = int_ref[1]
            base = jnp.where(path == 0, plan.base[0], plan.base[1])

            def stretch(place):
                j = 0
                for step in range(plan.bits):
                    bit = (place >> (plan.bits - 1 - step)) & 1
                    j = j + jnp.where(
                        path == 0, bit << plan.order[0][step], bit << plan.order[1][step]
                    )
                at = ((path * ndp + j) * plan.share) // (16 * LN) * 16 - base
                return buf[pl.ds(pl.multiple_of(at, 16), chunk), :].astype(BF16)

            def step(q, carry):
                bit = int_ref[5]
                keep_ref[q] = stretch(bit * half + q)
                send_ref[q] = stretch((1 - bit) * half + q)
                return carry

            loop(half, step, 0)

        return call(
            body,
            [((half, chunk, LN), BF16, "far")] * 2,
            [pltpu.VMEM((plan.length, LN), F32)],
            ints, *early, *conv, *late,
            **kw,
        )

    def halve(self, plan, ints, step, keep, came, **kw):
        half = keep.shape[0] // 2

        def body(int_ref, a_ref, b_ref, keep_ref, send_ref):
            bit = int_ref[5 + step]

            def one(q, carry):
                for out, at in ((keep_ref, bit * half + q), (send_ref, (1 - bit) * half + q)):
                    out[q] = (a_ref[at].astype(F32) + b_ref[at].astype(F32)).astype(BF16)
                return carry

            loop(half, one, 0)

        return call(
            body,
            [((half, plan.chunk, LN), BF16, "far")] * 2,
            [],
            ints, Far(keep), came,
            **kw,
        )

    def window(self, plan, ints, keep, came, vectors, small, tail, **kw):
        chunk, out_rows = plan.chunk, plan.out_rows
        pad = small.shape[0] + 8

        def body(int_ref, keep_ref, came_ref, vec_ref, small_ref, tail_ref, out_ref, a_ref):
            r0 = int_ref[2]
            row = int_ref[3]
            lane = int_ref[4]
            a_ref[...] = jnp.zeros_like(a_ref)
            for ref, start, n in (
                (vec_ref, ROW_SG, 2 * SLOW_VEC), (small_ref, ROW_FA, ROW_LAT - ROW_FA), (tail_ref, ROW_FG, 3)
            ):
                at = jnp.clip(start - r0, -n, chunk) + pad
                a_ref[pl.ds(at, n), :] += ref[0:n, :]
            a_ref[pad : pad + chunk, :] += keep_ref[0].astype(F32) + came_ref[0].astype(F32)
            one = a_ref[pl.ds(pad + row, out_rows), :]
            two = a_ref[pl.ds(pad + row + 1, out_rows), :]
            shift = (LN - lane) & (LN - 1)
            one = pltpu.roll(one, shift, 1)
            two = pltpu.roll(two, shift, 1)
            at = lax.broadcasted_iota(jnp.int32, (out_rows, LN), 1)
            out_ref[...] = jnp.where(at < LN - lane, one, two)

        return call(
            body,
            ((out_rows, LN), F32, "far"),
            [pltpu.VMEM((chunk + 2 * pad + 8, LN), F32)],
            ints, keep, came, vectors, small, tail,
            **kw,
        )


class Plan:
    def __init__(self, ndp):
        n = 2 * ndp
        self.ndp = ndp
        self.share = VALUES // n
        self.first = [self.share * d // LN // 16 * 16 for d in range(n)]
        ends = [-(-self.share * (d + 1) // LN) for d in range(n)]
        self.chunk = -(-max(e - f for e, f in zip(ends, self.first)) // 16) * 16
        self.base = [self.first[0], self.first[ndp]]
        self.length = max(
            self.first[q * ndp + ndp - 1] + self.chunk - self.base[q] for q in range(2)
        )
        self.early = ROW_SG - self.base[1]
        self.out_rows = -(-self.share // LN)
        self.bits = ndp.bit_length() - 1
        one = list(range(self.bits))
        two = [b ^ 1 if (b ^ 1) < self.bits else b for b in one]
        self.order = [one, two]

    def place(self, path, j):
        at = 0
        for b in self.order[path]:
            at = 2 * at + ((j >> b) & 1)
        return at

    def pairs(self, step):
        out = []
        for q in range(2):
            b = self.order[q][step]
            out += [(q * self.ndp + j, q * self.ndp + (j ^ (1 << b))) for j in range(self.ndp)]
        return out


def exchange(x):
    return lax.all_to_all(x, ("path", "dp"), 0, 0)


def swap(x):
    x = x.array if isinstance(x, Near) else x
    return lax.ppermute(x, "path", SWAP)


def local(
    acts, cotangent, clip_res, w_slow_a, w_slow_b, w_slow_c, w_slow_proj, slow_gain, slow_bias,
    w_fast_a, w_fast_b, w_fast_c, w_lateral, fast_gain, fast_bias,
):
    grid = acts.shape[2]
    px = grid * grid
    ndp = lax.axis_size("dp")
    net = Net(ndp, grid)
    plan = Plan(ndp)
    path, chip = lax.axis_index("path"), lax.axis_index("dp")
    core0 = path == 0
    level = clip_res[0]
    side = jnp.where(
        level == 1, grid * 5 // 8, jnp.where(level == 2, grid * 7 // 8, jnp.where(level == 3, grid, 0))
    )
    start = (path * ndp + chip) * plan.share
    r0 = start // LN // 16 * 16
    off = start - r0 * LN
    bits = [
        jnp.where(core0, chip >> plan.order[0][s], chip >> plan.order[1][s]) & 1 for s in range(plan.bits)
    ]
    ints = jnp.stack([side, path, r0, off // LN, off % LN] + bits).astype(jnp.int32)
    x = acts.reshape(px, 4096)
    cot = cotangent.reshape(px, 4096)
    sg, sb_ = slow_gain.reshape(SLOW_VEC, LN), slow_bias.reshape(SLOW_VEC, LN)

    def slow_par(a, b):
        return jnp.concatenate([sg[a:b], sb_[a:b]], axis=0)

    def fast_par(a, b):
        one = jnp.stack([fast_gain[a:b], fast_bias[a:b]])
        return jnp.tile(one, (1, LN // (b - a)))

    wlat = w_lateral.reshape(5 * CF, LAT)
    wa_lat = Far(w_slow_a, (LAT, CS_MID), (CS // LAT, 0))
    wp_lat = Far(w_slow_proj, (LAT, CS), (CS // LAT, 0))
    f1, f2, f3 = fast_par(0, 32), fast_par(32, 64), fast_par(64, 192)
    s1, s2, s3, s4 = slow_par(0, 2), slow_par(2, 4), slow_par(4, 12), slow_par(12, 20)
    wb3 = w_slow_b.reshape(3, 768, 256)
    wbt3 = w_slow_b.transpose(0, 2, 1).reshape(3, 768, 256)
    half = TF // 2

    x_other = swap(x)
    cot_other = swap(cot)

    fa_lo, fa_hi, band, pay = net.fast_first(ints, x, w_fast_a.transpose(0, 2, 1), us=3.5)
    (fb_w, fbt_w, fc_w), tok = net.fast_weights(
        w_fast_b, w_fast_b.transpose(0, 2, 1), w_fast_c, us=1.0, after=[pay], token=True
    )
    fa_other = swap(fa_lo)
    r1 = exchange(pay)
    fh1, fb, fc1, pay, r1 = net.conv_stage(
        ints, r1, r1, fa_hi, f1, fb_w, 1, half, fa_other, us=2.7, after=[tok]
    )
    (xs, xf, gs, gf), tok = net.halves(ints, x, x_other, cot, cot_other, us=2.5, after=[pay], token=True)
    r = exchange(pay)
    fh2, fc2, pay, fh2_edge = net.expand_stage(
        ints, r, r1, fb, f2, fc_w, 1, 1, half, True, us=2.6, after=[tok]
    )
    fh2_other = swap(fh2_edge)
    (pa, pp), tok = net.slow_start(xs, w_slow_a, w_slow_proj, us=3.5, after=[pay], token=True)
    r = exchange(pay)
    yf, lat, fc3 = net.fast_finish(
        ints, r, r1, fh2, fh2_other, fc_w, xf, f3, wlat, us=3.0, after=[tok]
    )

    sa, pay = net.slow_join(ints, pa, lat, wa_lat, 2, us=2.0)
    (sp, sp_rows), tok = net.slow_join(ints, pp, lat, wp_lat, 8, False, us=3.0, after=[pay], token=True)
    r = exchange(pay)
    sh1, sb, sc1, pay = net.conv_stage(
        ints, r, r1, sa, s1, wb3, 2, TS // 2, more=sp_rows, us=3.0, after=[tok]
    )
    rp = exchange(pay)
    gp, tok = net.fast_slope(ints, fh2, fc_w, xf, f3, fc3, us=4.0, after=[pay], token=True)
    sh2, sc2, pay = net.expand_stage(ints, rp, r1, sb, s2, w_slow_c, 2, 8, TS // 2, us=3.0, after=[tok])
    r = exchange(pay)
    ys, ds, scc, scp, pay = net.slow_top(ints, r, rp, r1, sh2, w_slow_c, sp, gs, s3, s4, us=6.0)

    sent, tok = net.out_send(ints, ys, yf, us=2.0, after=[pay], token=True)
    r = exchange(pay)
    (dp, dc, dn, t3, pay), (sent,) = net.expand_back(
        ints, r1, r, ds, sh2, w_slow_c, scc, s3, sb, sc2, s2, 2, 8, TS // 2, (sp, scp, s4),
        us=6.0, after=[tok], through=[sent],
    )
    theirs = swap(sent)
    (early, early_out), tok = net.grads_early(
        plan, ints, xs, lat, dp, sh2, dc, us=6.0, after=[pay], token=True
    )
    r = exchange(pay)
    (db, dn, t2, pay), (early_out,) = net.conv_back(
        ints, r1, r, dn, sb, sc2, s2, wbt3, sa, sc1, s1, 2, TS // 2, us=3.0, after=[tok], through=[early_out]
    )
    early_in = swap(early_out)
    conv, tok = net.grads_conv(sh1, db, us=3.0, after=[pay], token=True)
    r = exchange(pay)
    (da, dl0, dl1, t1), (conv_out,) = net.slow_last(
        ints, r1, r, dn, sa, sc1, s1, dp, wa_lat, wp_lat, us=3.0, after=[tok], through=[conv]
    )
    dl_other = swap(dl0)

    (fds, pay), (conv_out,) = net.fast_top(
        ints, dl0, dl1, dl_other, wlat, gf, gp, fh2, fc_w, fc3, us=4.0, through=[conv_out]
    )
    conv_in = swap(conv_out)
    fds_lo = swap(fds)
    (late, late_out), tok = net.grads_late(ints, xs, lat, da, yf, dl0, dl1, us=4.0, after=[pay], token=True)
    dxs, tok2 = net.slow_input_grad(da, dp, w_slow_a, w_slow_proj, us=4.0, after=[tok], token=True)
    r = exchange(pay)
    (fdc, dn, u3, pay), (late_out, dxs_out) = net.expand_back(
        ints, r1, r, fds, fh2, fc_w, fc3, f3, fb, fc2, f2, 1, 1, half,
        us=4.0, after=[tok2], through=[late_out, dxs],
    )
    late_in = swap(late_out)
    (keep, there), tok = net.windows(
        plan, ints, (Far(early), Far(early_in)), (Far(conv_out), Far(conv_in)), (Far(late), late_in),
        us=6.0, after=[pay], token=True,
    )
    r = exchange(pay)
    (fdb, dn, u2, pay), (there, dxs_out) = net.conv_back(
        ints, r1, r, dn, fb, fc2, f2, fbt_w, fa_hi, fc1, f1, 1, half, fa_other,
        us=3.5, after=[tok], through=[there, dxs_out],
    )
    dn_lo = swap(dn)
    here = lax.ppermute(there, ("path", "dp"), plan.pairs(0))
    gb, gc = net.fast_grads_bc(fh1, fdb, fh2, fdc, us=3.5, after=[pay])
    bc = jnp.concatenate([gb.reshape(-1, LN), gc], axis=0)
    bc = jnp.pad(bc, ((0, -bc.shape[0] % 16), (0, 0)))
    bc_other = swap(bc)
    r = exchange(pay)
    fda, u1, pay = net.fast_first_back(
        ints, r1, r, dn_lo, dn, Far(fa_lo), fa_hi, fc1, f1, x, bc, bc_other, us=3.5
    )
    dxs_other = swap(dxs_out)
    dx = net.last(ints, fda, Far(fds_lo), fds, band, dxs_out, dxs_other, us=4.5, after=[pay])

    out = net.out_join(ints, ys, yf, theirs, us=3.0)

    for step in range(1, plan.bits):
        keep, there = net.halve(plan, ints, step, keep, here, us=1.5)
        here = lax.ppermute(there, ("path", "dp"), plan.pairs(step))
    small = lax.all_to_all(pay, "dp", 0, 0).astype(F32).sum(axis=0)
    bc = swap(small)
    ga = small[: 3 * CF_MID].reshape(3, CF_MID, CF).transpose(0, 2, 1).reshape(-1, LN)
    small = jnp.where(core0, 0.0, jnp.concatenate([ga, bc], axis=0))
    vectors = jnp.concatenate([t1[2:4], t2[2:4], t3[8:24], t1[0:2], t2[0:2], t3[0:8], t3[0:8]], axis=0)
    tail = jnp.concatenate([u1[1, :32], u2[1, :32], u3[1], u1[0, :32], u2[0, :32], u3[0]]).reshape(3, LN)
    tail = jnp.pad(tail, ((0, 5), (0, 0)))
    flat = net.window(plan, ints, keep, here, vectors, small, tail).reshape(-1)[: plan.share]
    return (out.reshape(acts.shape), dx.reshape(acts.shape), flat)


def solution(mesh):
    data = P("path", "dp", None, None, None)
    in_specs = (data, data, P("dp")) + (P(),) * 12
    out_specs = (data, data, P(("path", "dp")))
    return jax.shard_map(local, mesh=mesh, in_specs=in_specs, out_specs=out_specs, check_vma=False)
```

time: 296 us -> 267 us (0.902)
  Pallas kernels: 71.4 us -> 126 us
  blocking collectives: 51.2 us -> 0 us
  loops' own time: 10.2 us -> 0 us
  waiting for transfers between devices: 66.7 us -> 58.2 us
  other arithmetic: 8.79 us -> 0.84 us
    pallas_call x23 -> x33, Pallas kernels: 71.4 us -> 126 us  [call(): pl.pallas_call(wrapped, out_shape=shapes, grid=(1,) if cut else (), in_sp...]
    all_to_all x2 -> x0, blocking collectives: 51.2 us -> none  [exchange(): return lax.all_to_all(x, 'dp', 0, 0, axis_index_groups=groups)]
    ppermute x4 -> x18, starting transfers between devices: 46.2 us -> 13.1 us  [the longest x3 8.5 us: local(): here = lax.ppermute(there, ('path', 'dp'), plan.pairs(step))]
    all_to_all x6 -> x13, starting transfers between devices: 22.3 us -> 54.4 us  [the longest x12 48.7 us: exchange(): return lax.all_to_all(x, ('path', 'dp'), 0, 0)]
    another operation x3 -> x0, loops' own time: 10.2 us -> none  [the longest x1 8.79 us: local(): lax.cond(is_fast, fast_middle, slow_middle, (lat_s, first, pp, wt, x, h2,...]
    all_to_all x6 -> x13, waiting for transfers between devices: 58.3 us -> 49 us  [the longest x12 42.2 us: exchange(): return lax.all_to_all(x, ('path', 'dp'), 0, 0)]
    unnamed x2 -> x61, local copies, waits for them, and re-layouts: 0.01 us -> 8.46 us
    reduce_sum x3 -> x1, other arithmetic: 8.01 us -> 0.07 us  [local(): small = lax.all_to_all(pay, 'dp', 0, 0).astype(F32).sum(axis=0)]
  transfers between devices with their start and end apart: 10 -> 31, of which waited for: 9 -> 14; matrix products, arithmetic and copies ran while one was open for 2% -> 1% of each run, Pallas kernels for 17% -> 33%
where the time goes in v2:
time: 267 us; the launch traced here: 265 us
  Pallas kernels  126 us (47%)
  starting transfers between devices  67.5 us (25%)
  waiting for transfers between devices  58.2 us (22%)
  local copies, waits for them, and re-layouts  11.2 us (4%)
    pallas_call x33, Pallas kernels, call(): pl.pallas_call(wrapped, out_shape=shapes, grid=(1,) if cut else (), in_sp...  126 us
    all_to_all x12, starting transfers between devices, exchange(): return lax.all_to_all(x, ('path', 'dp'), 0, 0)  48.7 us
    all_to_all x12, waiting for transfers between devices, exchange(): return lax.all_to_all(x, ('path', 'dp'), 0, 0)  42.2 us
    ppermute x3, starting transfers between devices, local(): here = lax.ppermute(there, ('path', 'dp'), plan.pairs(step))  8.5 us
    unnamed x61, local copies, waits for them, and re-layouts  8.46 us
    all_to_all x1, waiting for transfers between devices, local(): small = lax.all_to_all(pay, 'dp', 0, 0).astype(F32).sum(axis=0)  6.85 us
    ppermute x1, waiting for transfers between devices, local(): here = lax.ppermute(there, ('path', 'dp'), plan.pairs(0))  6.5 us
    all_to_all x1, starting transfers between devices, local(): small = lax.all_to_all(pay, 'dp', 0, 0).astype(F32).sum(axis=0)  5.68 us
  transfers between devices with their start and end apart: 31, of which 14 were waited for; matrix products, arithmetic and copies ran while one was open for 1% of the time, Pallas kernels for 33%

profile of v2, /device:TPU:0, one launch (start us, length us, event | category | flops | bytes accessed | tf_op | source)
XLA Modules:
  0.0 265.0 jit_solution(18329500092037409435)
XLA Ops:
  6.1 9.1 %all-to-all-start = ((f32[32,4,128]{2,1,0:T(4,128)}), f32[32,4,128]{2,1,0:T(4,128)S(1)}, u32[]{:S(2)}, u32[]{:S(2)}) async-start(f32[32,4,128]{2,1,0:T(4,128)} %get-tuple-element.107.refs_3_), calls=%async_computation | async-start | bytes 131072 | tf_op jit(solution)/shard_map/all_to_all | solution.py:1241
  18.1 4.4 %all-to-all-done.refs_1_.refs_2_ = f32[32,4,128]{2,1,0:T(4,128)S(1)} async-done(((f32[32,4,128]{2,1,0:T(4,128)}), f32[32,4,128]{2,1,0:T(4,128)S(1)}, u32[]{:S(2)}, u32[]{:S(2)}) %all-to-all-start) | async-done | bytes 65568 | tf_op jit(solution)/shard_map/all_to_all | solution.py:1241
  28.9 4.8 %shard_map.169 = (bf16[256,2048]{1,0:T(8,128)(2,1)}, bf16[256,2304]{1,0:T(8,128)(2,1)}, bf16[256,2048]{1,0:T(8,128)(2,1)}, bf16[256,2048]{1,0:T(8,128)(2,1)}, f32[8,128]{1,0:T(8,128)}) custom-call(s32[9]{0:T(128)S(1)} %stack.63.refs_0_, bf16[256,4096]{1,0:T(8,128)(2,1)} %bitcast.68, bf16[256,4096]{1,0:T(8,128)(2,1)} %collective-permute-done.refs_2_, ...), custom_call_target="tpu_custom_call" | custom-call | flops 2500000000 | tf_op jit(solution)/shard_map/pallas_call | solution.py:112
  51.0 4.6 %shard_map.172 = (bf16[256,2304]{1,0:T(8,128)(2,1)}, bf16[256,512]{1,0:T(8,128)(2,1)}, f32[8,128]{1,0:T(8,128)}) custom-call(s32[9]{0:T(128)S(1)} %stack.63.refs_0_, f32[32,4,128]{2,1,0:T(4,128)S(1)} %all-to-all-done.2.refs_1_, f32[32,4,128]{2,1,0:T(4,128)} %get-tuple-element.114.refs_2_.refs_3_.refs_1_, ...), custom_call_target="tpu_custom_call" | custom-call | flops 3000000000 | tf_op jit(solution)/shard_map/pallas_call | solution.py:112
  57.8 4.7 %all-to-all-start.3 = ((f32[32,4,128]{2,1,0:T(4,128)}), f32[32,4,128]{2,1,0:T(4,128)S(1)}, u32[]{:S(2)}, u32[]{:S(2)}) async-start(f32[32,4,128]{2,1,0:T(4,128)} %get-tuple-element.125.refs_4_), calls=%async_computation.3 | async-start | bytes 131072 | tf_op jit(solution)/shard_map/all_to_all | solution.py:1241
  76.4 5.1 %shard_map.176 = (f32[256,2048]{1,0:T(8,128)}, f32[8,128]{1,0:T(8,128)}) custom-call(s32[9]{0:T(128)S(1)} %stack.63.refs_0_, bf16[256,512]{1,0:T(8,128)(2,1)} %get-tuple-element.120.refs_3_.refs_1_.refs_7_.refs_4_.refs_2_, bf16[256,1024]{1,0:T(8,128)(2,1)} %get-tuple-element.116.refs_5_.refs_2_.refs_8_, ...), custom_call_target="tpu_custom_call" | custom-call | flops 4000000000 | tf_op jit(solution)/shard_map/pallas_call | solution.py:112
  81.5 8.9 %all-to-all-done.4.refs_1_.refs_2_ = f32[32,20,128]{2,1,0:T(8,128)S(1)} async-done(((f32[32,20,128]{2,1,0:T(8,128)}), f32[32,20,128]{2,1,0:T(8,128)S(1)}, u32[]{:S(2)}, u32[]{:S(2)}) %all-to-all-start.4) | async-done | bytes 327712 | tf_op jit(solution)/shard_map/all_to_all | solution.py:1241
  96.2 11.0 %all-to-all-done.5.refs_1_ = f32[32,16,128]{2,1,0:T(8,128)S(1)} async-done(((f32[32,16,128]{2,1,0:T(8,128)}), f32[32,16,128]{2,1,0:T(8,128)S(1)}, u32[]{:S(2)}, u32[]{:S(2)}) %all-to-all-start.5) | async-done | bytes 262176 | tf_op jit(solution)/shard_map/all_to_all | solution.py:1241
  107.2 6.8 %shard_map.178 = (bf16[256,2048]{1,0:T(8,128)(2,1)}, f32[256,2048]{1,0:T(8,128)}, f32[16,128]{1,0:T(8,128)}, f32[16,128]{1,0:T(8,128)}, bf16[32,24,128]{2,1,0:T(8,128)(2,1)}) custom-call(s32[9]{0:T(128)S(1)} %stack.63.refs_0_, f32[32,16,128]{2,1,0:T(8,128)S(1)} %all-to-all-done.5.refs_1_, f32[32,20,128]{2,1,0:T(8,128)S(1)} %all-to-all-done.4.refs_1_.refs_2_, ...), custom_call_target="tpu_custom_call" | custom-call | flops 6000000000 | tf_op jit(solution)/shard_map/pallas_call | solution.py:112
  120.0 6.3 %all-to-all-done.6.refs_2_ = bf16[32,24,128]{2,1,0:T(8,128)(2,1)S(1)} async-done(((bf16[32,24,128]{2,1,0:T(8,128)(2,1)}), bf16[32,24,128]{2,1,0:T(8,128)(2,1)S(1)}, u32[]{:S(2)}, u32[]{:S(2)}) %all-to-all-start.6) | async-done | bytes 196640 | tf_op jit(solution)/shard_map/all_to_all | solution.py:1241
  126.3 6.2 %shard_map.180 = (bf16[256,2048]{1,0:T(8,128)(2,1)}, bf16[256,2048]{1,0:T(8,128)(2,1)}, f32[256,512]{1,0:T(8,128)}, f32[24,128]{1,0:T(8,128)}, f32[32,4,128]{2,1,0:T(4,128)}, /*index=5*/bf16[256,2048]{1,0:T(8,128)(2,1)}) custom-call(s32[9]{0:T(128)S(1)} %stack.63.refs_0_, ...), custom_call_target="tpu_custom_call", output_to_operand_aliasing={{5}: (15, {})} | custom-call | flops 6000000000 | tf_op jit(solution)/shard_map/pallas_call | solution.py:112
  135.1 7.0 %shard_map.182 = (bf16[8976,128]{1,0:T(8,128)(2,1)}, bf16[8976,128]{1,0:T(8,128)(2,1)}, f32[8,128]{1,0:T(8,128)}) custom-call(s32[9]{0:T(128)S(1)} %stack.63.refs_0_, bf16[256,2048]{1,0:T(8,128)(2,1)} %get-tuple-element.113.refs_0_.refs_1_, bf16[256,512]{1,0:T(8,128)(2,1)} %get-tuple-element.124.refs_2_, ...), custom_call_target="tpu_custom_call" | custom-call | flops 6000000000 | tf_op jit(solution)/shard_map/pallas_call | solution.py:112
  145.9 5.5 %all-to-all-start.8 = ((f32[32,4,128]{2,1,0:T(4,128)}), f32[32,4,128]{2,1,0:T(4,128)S(1)}, u32[]{:S(2)}, u32[]{:S(2)}) async-start(f32[32,4,128]{2,1,0:T(4,128)} %get-tuple-element.155.refs_2_), calls=%async_computation.8 | async-start | bytes 131072 | tf_op jit(solution)/shard_map/all_to_all | solution.py:1241
  163.4 4.3 %shard_map.186 = (f32[256,2048]{1,0:T(8,128)}, f32[32,4,128]{2,1,0:T(4,128)}, bf16[4608,128]{1,0:T(8,128)(2,1)}) custom-call(s32[9]{0:T(128)S(1)} %stack.63.refs_0_, bf16[256,256]{1,0:T(8,128)(2,1)} %get-tuple-element.161.refs_1_.refs_5_, bf16[256,256]{1,0:T(8,128)(2,1)} %get-tuple-element.162.refs_2_.refs_6_, ...), custom_call_target="tpu_custom_call", output_to_operand_aliasing={{2}: (10, {})} | custom-call | flops 4000000000 | tf_op jit(solution)/shard_map/pallas_call | solution.py:112
  170.6 4.2 %shard_map.187 = (bf16[2560,128]{1,0:T(8,128)(2,1)}, bf16[2560,128]{1,0:T(8,128)(2,1)}, f32[8,128]{1,0:T(8,128)}) custom-call(s32[9]{0:T(128)S(1)} %stack.63.refs_0_, bf16[256,2048]{1,0:T(8,128)(2,1)} %get-tuple-element.113.refs_0_.refs_1_, bf16[256,512]{1,0:T(8,128)(2,1)} %get-tuple-element.124.refs_2_, ...), custom_call_target="tpu_custom_call" | custom-call | flops 4000000000 | tf_op jit(solution)/shard_map/pallas_call | solution.py:112
  178.7 4.9 %shard_map.189 = (bf16[256,2048]{1,0:T(8,128)(2,1)}, f32[256,512]{1,0:T(8,128)}, f32[4,128]{1,0:T(4,128)}, f32[32,4,128]{2,1,0:T(4,128)}, bf16[2560,128]{1,0:T(8,128)(2,1)}, /*index=5*/bf16[256,2048]{1,0:T(8,128)(2,1)}) custom-call(s32[9]{0:T(128)S(1)} %stack.63.refs_0_, ...), custom_call_target="tpu_custom_call", output_to_operand_aliasing={{4}: (12, {}), {5}: (13, {})} | custom-call | flops 4000000000 | tf_op jit(solution)/shard_map/pallas_call | solution.py:112
  184.1 5.6 %all-to-all-start.10 = ((f32[32,4,128]{2,1,0:T(4,128)}), f32[32,4,128]{2,1,0:T(4,128)S(1)}, u32[]{:S(2)}, u32[]{:S(2)}) async-start(f32[32,4,128]{2,1,0:T(4,128)} %get-tuple-element.174.refs_7_), calls=%async_computation.10 | async-start | bytes 131072 | tf_op jit(solution)/shard_map/all_to_all | solution.py:1241
  190.8 5.7 %shard_map.190 = (bf16[8,672,128]{2,1,0:T(8,128)(2,1)}, bf16[8,672,128]{2,1,0:T(8,128)(2,1)}, f32[8,128]{1,0:T(8,128)}) custom-call(s32[9]{0:T(128)S(1)} %stack.63.refs_0_, bf16[8976,128]{1,0:T(8,128)(2,1)} %get-tuple-element.178.refs_1_, bf16[8976,128]{1,0:T(8,128)(2,1)} %collective-permute-done.6.refs_2_, bf16[4608,128]{1,0:T(8,128)(2,1)} %get-tuple-element.180.refs_3_, ...), custom_call_target="tpu_custom_call" | custom-call | flops 6000000000 | tf_op jit(solution)/shard_map/pallas_call | solution.py:112
  203.0 4.6 %all-to-all-start.11 = ((f32[32,4,128]{2,1,0:T(4,128)}), f32[32,4,128]{2,1,0:T(4,128)S(1)}, u32[]{:S(2)}, u32[]{:S(2)}) async-start(f32[32,4,128]{2,1,0:T(4,128)} %get-tuple-element.186.refs_4_), calls=%async_computation.11 | async-start | bytes 131072 | tf_op jit(solution)/shard_map/all_to_all | solution.py:1241
  213.6 6.5 %collective-permute-done.13.refs_2_ = bf16[8,672,128]{2,1,0:T(8,128)(2,1)S(1)} collective-permute-done((bf16[8,672,128]{2,1,0:T(8,128)(2,1)}, bf16[8,672,128]{2,1,0:T(8,128)(2,1)S(1)}, u32[]{:S(2)}, u32[]{:S(2)}) %collective-permute-start.13) | collective-permute-done | bytes 1376288 | tf_op jit(solution)/shard_map/ppermute | solution.py:1372
  229.3 5.7 %all-to-all-start.12 = ((bf16[16,112,128]{2,1,0:T(8,128)(2,1)}), bf16[16,112,128]{2,1,0:T(8,128)(2,1)S(1)}, u32[]{:S(2)}, u32[]{:S(2)}) async-start(bf16[16,112,128]{2,1,0:T(8,128)(2,1)} %get-tuple-element.196.refs_7_), calls=%async_computation.12 | async-start | bytes 917504 | tf_op jit(solution)/shard_map/all_to_all | solution.py:1389
  242.5 6.9 %all-to-all-done.12 = bf16[16,112,128]{2,1,0:T(8,128)(2,1)S(1)} async-done(((bf16[16,112,128]{2,1,0:T(8,128)(2,1)}), bf16[16,112,128]{2,1,0:T(8,128)(2,1)S(1)}, u32[]{:S(2)}, u32[]{:S(2)}) %all-to-all-start.12) | async-done | bytes 458784 | tf_op jit(solution)/shard_map/all_to_all | solution.py:1389
  252.3 5.3 %collective-permute-start.16 = (bf16[1,672,128]{2,1,0:T(8,128)(2,1)}, bf16[1,672,128]{2,1,0:T(8,128)(2,1)S(1)}, u32[]{:S(2)}, u32[]{:S(2)}) collective-permute-start(bf16[1,672,128]{2,1,0:T(8,128)(2,1)} %get-tuple-element.204), channel_id=1, source_target_pairs={{0,8},{1,9},{2,10},{3,11},{4,12},{5,13},{6,14},{7,15},{8,0},{9,1},... | collective-permute-start | bytes 516104 | tf_op jit(solution)/shard_map/ppermute | solution.py:1388
  257.6 5.4 %shard_map.194 = bf16[256,4096]{1,0:T(8,128)(2,1)} custom-call(s32[9]{0:T(128)S(1)} %stack.63.refs_0_, bf16[256,1024]{1,0:T(8,128)(2,1)} %get-tuple-element.193.refs_1_, f32[256,2048]{1,0:T(8,128)} %collective-permute-done.11.refs_2_, f32[256,2048]{1,0:T(8,128)} %get-tuple-element.167.refs_3_, bf16[1280,256]{1,0:T(8,128)(2,1)} %get-tuple-element.194.refs_4_, ...), custom_call_target="tpu_custom_call" | custom-call | flops 4499999744 | tf_op jit(solution)/shard_map/pallas_call | solution.py:112
  (166 shorter events, 119.7 us)
Async XLA Ops:
  0.6 28.3 %collective-permute-start = (bf16[256,4096]{1,0:T(8,128)(2,1)}, bf16[256,4096]{1,0:T(8,128)(2,1)}, u32[]{:S(2)}, u32[]{:S(2)}) collective-permute-start(bf16[256,4096]{1,0:T(8,128)(2,1)} %bitcast.67), channel_id=1, source_target_pairs={{0,16},{16,0},{1,17},{17,1},{2,18},{18,2},{3,19},{19,3},{4,20},{20... | collective-permute-start | bytes 6291464 | tf_op jit(solution)/shard_map/ppermute | solution.py:1246
  1.1 27.8 %collective-permute-start.1 = (bf16[256,4096]{1,0:T(8,128)(2,1)}, bf16[256,4096]{1,0:T(8,128)(2,1)}, u32[]{:S(2)}, u32[]{:S(2)}) collective-permute-start(bf16[256,4096]{1,0:T(8,128)(2,1)} %bitcast.77), channel_id=1, source_target_pairs={{0,16},{16,0},{1,17},{17,1},{2,18},{18,2},{3,19},{19,3},{4,20},{20... | collective-permute-start | bytes 6291464 | tf_op jit(solution)/shard_map/ppermute | solution.py:1246
  6.1 16.4 %all-to-all-start = ((f32[32,4,128]{2,1,0:T(4,128)}), f32[32,4,128]{2,1,0:T(4,128)S(1)}, u32[]{:S(2)}, u32[]{:S(2)}) async-start(f32[32,4,128]{2,1,0:T(4,128)} %get-tuple-element.107.refs_3_), calls=%async_computation | async-start | bytes 131072 | tf_op jit(solution)/shard_map/all_to_all | solution.py:1241
  40.3 10.7 %all-to-all-start.2 = ((f32[32,4,128]{2,1,0:T(4,128)}), f32[32,4,128]{2,1,0:T(4,128)S(1)}, u32[]{:S(2)}, u32[]{:S(2)}) async-start(f32[32,4,128]{2,1,0:T(4,128)} %get-tuple-element.118.refs_3_), calls=%async_computation.2 | async-start | bytes 131072 | tf_op jit(solution)/shard_map/all_to_all | solution.py:1241
  57.8 12.0 %all-to-all-start.3 = ((f32[32,4,128]{2,1,0:T(4,128)}), f32[32,4,128]{2,1,0:T(4,128)S(1)}, u32[]{:S(2)}, u32[]{:S(2)}) async-start(f32[32,4,128]{2,1,0:T(4,128)} %get-tuple-element.125.refs_4_), calls=%async_computation.3 | async-start | bytes 131072 | tf_op jit(solution)/shard_map/all_to_all | solution.py:1241
  73.8 16.6 %all-to-all-start.4 = ((f32[32,20,128]{2,1,0:T(8,128)}), f32[32,20,128]{2,1,0:T(8,128)S(1)}, u32[]{:S(2)}, u32[]{:S(2)}) async-start(f32[32,20,128]{2,1,0:T(8,128)} %get-tuple-element.130.refs_6_), calls=%async_computation.4 | async-start | bytes 786432 | tf_op jit(solution)/shard_map/all_to_all | solution.py:1241
  93.4 13.8 %all-to-all-start.5 = ((f32[32,16,128]{2,1,0:T(8,128)}), f32[32,16,128]{2,1,0:T(8,128)S(1)}, u32[]{:S(2)}, u32[]{:S(2)}) async-start(f32[32,16,128]{2,1,0:T(8,128)} %get-tuple-element.134), calls=%async_computation.5 | async-start | bytes 524288 | tf_op jit(solution)/shard_map/all_to_all | solution.py:1241
  114.0 12.4 %all-to-all-start.6 = ((bf16[32,24,128]{2,1,0:T(8,128)(2,1)}), bf16[32,24,128]{2,1,0:T(8,128)(2,1)S(1)}, u32[]{:S(2)}, u32[]{:S(2)}) async-start(bf16[32,24,128]{2,1,0:T(8,128)(2,1)} %get-tuple-element.140.refs_3_), calls=%async_computation.6 | async-start | bytes 393216 | tf_op jit(solution)/shard_map/all_to_all | solution.py:1241
  145.9 12.9 %all-to-all-start.8 = ((f32[32,4,128]{2,1,0:T(4,128)}), f32[32,4,128]{2,1,0:T(4,128)S(1)}, u32[]{:S(2)}, u32[]{:S(2)}) async-start(f32[32,4,128]{2,1,0:T(4,128)} %get-tuple-element.155.refs_2_), calls=%async_computation.8 | async-start | bytes 131072 | tf_op jit(solution)/shard_map/all_to_all | solution.py:1241
  151.4 38.3 %collective-permute-start.6 = (bf16[8976,128]{1,0:T(8,128)(2,1)}, bf16[8976,128]{1,0:T(8,128)(2,1)}, u32[]{:S(2)}, u32[]{:S(2)}) collective-permute-start(bf16[8976,128]{1,0:T(8,128)(2,1)} %get-tuple-element.179), channel_id=1, source_target_pairs={{0,16},{16,0},{1,17},{17,1},{2,18},{18,2},{3,19},{19,3},{4,20},{20... | collective-permute-start | bytes 6893576 | tf_op jit(solution)/shard_map/ppermute | solution.py:1246
  167.7 11.0 %all-to-all-start.9 = ((f32[32,4,128]{2,1,0:T(4,128)}), f32[32,4,128]{2,1,0:T(4,128)S(1)}, u32[]{:S(2)}, u32[]{:S(2)}) async-start(f32[32,4,128]{2,1,0:T(4,128)} %get-tuple-element.166.refs_7_), calls=%async_computation.9 | async-start | bytes 131072 | tf_op jit(solution)/shard_map/all_to_all | solution.py:1241
  170.5 19.3 %collective-permute-start.7 = (bf16[4608,128]{1,0:T(8,128)(2,1)}, bf16[4608,128]{1,0:T(8,128)(2,1)S(1)}, u32[]{:S(2)}, u32[]{:S(2)}) collective-permute-start(bf16[4608,128]{1,0:T(8,128)(2,1)} %get-tuple-element.180.refs_3_), channel_id=1, source_target_pairs={{0,16},{16,0},{1,17},{17,1},{2,18},{18,2},{3,19},{19,3},{4,20},{20... | collective-permute-start | bytes 3538952 | tf_op jit(solution)/shard_map/ppermute | solution.py:1246
  184.1 12.9 %all-to-all-start.10 = ((f32[32,4,128]{2,1,0:T(4,128)}), f32[32,4,128]{2,1,0:T(4,128)S(1)}, u32[]{:S(2)}, u32[]{:S(2)}) async-start(f32[32,4,128]{2,1,0:T(4,128)} %get-tuple-element.174.refs_7_), calls=%async_computation.10 | async-start | bytes 131072 | tf_op jit(solution)/shard_map/all_to_all | solution.py:1241
  201.0 19.1 %collective-permute-start.13 = (bf16[8,672,128]{2,1,0:T(8,128)(2,1)}, bf16[8,672,128]{2,1,0:T(8,128)(2,1)S(1)}, u32[]{:S(2)}, u32[]{:S(2)}) collective-permute-start(bf16[8,672,128]{2,1,0:T(8,128)(2,1)} %get-tuple-element.198), channel_id=1, source_target_pairs={{0,1},{1,0},{2,3},{3,2},{4,5},{5,4},{6,7},{7,6},{8,9},{9,8},{10,11... | collective-permute-start | bytes 4128776 | tf_op jit(solution)/shard_map/ppermute | solution.py:1372
  202.3 32.7 %collective-permute-start.4 = (bf16[256,2048]{1,0:T(8,128)(2,1)}, bf16[256,2048]{1,0:T(8,128)(2,1)}, u32[]{:S(2)}, u32[]{:S(2)}) collective-permute-start(bf16[256,2048]{1,0:T(8,128)(2,1)} %get-tuple-element.147), channel_id=1, source_target_pairs={{0,16},{16,0},{1,17},{17,1},{2,18},{18,2},{3,19},{19,3},{4,20},{20... | collective-permute-start | bytes 3145736 | tf_op jit(solution)/shard_map/ppermute | solution.py:1246
  202.5 55.1 %collective-permute-start.11 = (f32[256,2048]{1,0:T(8,128)}, f32[256,2048]{1,0:T(8,128)}, u32[]{:S(2)}, u32[]{:S(2)}) collective-permute-start(f32[256,2048]{1,0:T(8,128)} %get-tuple-element.167.refs_3_), channel_id=1, source_target_pairs={{0,16},{16,0},{1,17},{17,1},{2,18},{18,2},{3,19},{19,3},{4,20},{20... | collective-permute-start | bytes 6291464 | tf_op jit(solution)/shard_map/ppermute | solution.py:1246
  203.0 23.7 %all-to-all-start.11 = ((f32[32,4,128]{2,1,0:T(4,128)}), f32[32,4,128]{2,1,0:T(4,128)S(1)}, u32[]{:S(2)}, u32[]{:S(2)}) async-start(f32[32,4,128]{2,1,0:T(4,128)} %get-tuple-element.186.refs_4_), calls=%async_computation.11 | async-start | bytes 131072 | tf_op jit(solution)/shard_map/all_to_all | solution.py:1241
  207.7 19.1 %collective-permute-start.9 = (f32[256,512]{1,0:T(8,128)}, f32[256,512]{1,0:T(8,128)}, u32[]{:S(2)}, u32[]{:S(2)}) collective-permute-start(f32[256,512]{1,0:T(8,128)} %get-tuple-element.187.refs_4_), channel_id=1, source_target_pairs={{0,16},{16,0},{1,17},{17,1},{2,18},{18,2},{3,19},{19,3},{4,20},{20... | collective-permute-start | bytes 1572872 | tf_op jit(solution)/shard_map/ppermute | solution.py:1246
  213.3 12.1 %collective-permute-start.10 = (f32[112,128]{1,0:T(8,128)S(1)}, f32[112,128]{1,0:T(8,128)S(1)}, u32[]{:S(2)}, u32[]{:S(2)}) collective-permute-start(f32[112,128]{1,0:T(8,128)S(1)} %select_maximum_fusion.refs_10_), channel_id=1, source_target_pairs={{0,16},{16,0},{1,17},{17,1},{2,18},{18,2},{3,19},{19,3},{4,20},{20... | collective-permute-start | bytes 172040 | tf_op jit(solution)/shard_map/ppermute | solution.py:1246
  221.2 36.4 %collective-permute-start.12 = (bf16[256,2048]{1,0:T(8,128)(2,1)}, bf16[256,2048]{1,0:T(8,128)(2,1)}, u32[]{:S(2)}, u32[]{:S(2)}) collective-permute-start(bf16[256,2048]{1,0:T(8,128)(2,1)} %get-tuple-element.195.refs_5_), channel_id=1, source_target_pairs={{0,16},{16,0},{1,17},{17,1},{2,18},{18,2},{3,19},{19,3},{4,20},{20... | collective-permute-start | bytes 3145736 | tf_op jit(solution)/shard_map/ppermute | solution.py:1246
  225.5 12.9 %collective-permute-start.14 = (bf16[4,672,128]{2,1,0:T(8,128)(2,1)}, bf16[4,672,128]{2,1,0:T(8,128)(2,1)S(1)}, u32[]{:S(2)}, u32[]{:S(2)}) collective-permute-start(bf16[4,672,128]{2,1,0:T(8,128)(2,1)} %get-tuple-element.200), channel_id=1, source_target_pairs={{0,2},{1,3},{2,0},{3,1},{4,6},{5,7},{6,4},{7,5},{8,10},{9,11},{10,... | collective-permute-start | bytes 2064392 | tf_op jit(solution)/shard_map/ppermute | solution.py:1388
  229.3 20.1 %all-to-all-start.12 = ((bf16[16,112,128]{2,1,0:T(8,128)(2,1)}), bf16[16,112,128]{2,1,0:T(8,128)(2,1)S(1)}, u32[]{:S(2)}, u32[]{:S(2)}) async-start(bf16[16,112,128]{2,1,0:T(8,128)(2,1)} %get-tuple-element.196.refs_7_), calls=%async_computation.12 | async-start | bytes 917504 | tf_op jit(solution)/shard_map/all_to_all | solution.py:1389
  249.5 13.9 %collective-permute-start.17 = (f32[112,128]{1,0:T(8,128)S(1)}, f32[112,128]{1,0:T(8,128)S(1)}, u32[]{:S(2)}, u32[]{:S(2)}) collective-permute-start(f32[112,128]{1,0:T(8,128)S(1)} %convert_reduce_fusion), channel_id=1, source_target_pairs={{0,16},{16,0},{1,17},{17,1},{2,18},{18,2},{3,19},{19,3},{4,20},{20... | collective-permute-start | bytes 172040 | tf_op jit(solution)/shard_map/ppermute | solution.py:1246
  252.3 11.0 %collective-permute-start.16 = (bf16[1,672,128]{2,1,0:T(8,128)(2,1)}, bf16[1,672,128]{2,1,0:T(8,128)(2,1)S(1)}, u32[]{:S(2)}, u32[]{:S(2)}) collective-permute-start(bf16[1,672,128]{2,1,0:T(8,128)(2,1)} %get-tuple-element.204), channel_id=1, source_target_pairs={{0,8},{1,9},{2,10},{3,11},{4,12},{5,13},{6,14},{7,15},{8,0},{9,1},... | collective-permute-start | bytes 516104 | tf_op jit(solution)/shard_map/ppermute | solution.py:1388
  (37 other events, 224.3 us)

commit v3 on v2

--- a/solution.py
+++ b/solution.py
@@ -200,9 +200,40 @@
         pay_ref[d] = value
 
 
+def split(v):
+    high = v.astype(BF16).astype(F32)
+    return high, v - high
+
+
+def encode(code_ref, rows_ref, narrow, wide):
+    at = 0
+    if narrow:
+        high, low = split(rows_ref[0:narrow, :])
+        code_ref[0:narrow, :] = high
+        code_ref[narrow : 2 * narrow, :] = low
+        at = 2 * narrow
+    if wide:
+        high, low = split(rows_ref[narrow : narrow + wide, :])
+        code_ref[at : at + wide, :] = high
+        code_ref[at + wide : at + 2 * wide, :] = low
+        code_ref[at + 2 * wide : at + 3 * wide, :] = rows_ref[narrow + wide : narrow + 2 * wide, :]
+
+
 def combine(recv, row, params, n, cst_ref):
-    s = recv[:, row : row + params, :]
-    m2 = recv[:, row + params : row + 2 * params, :]
+    combine_sums(recv[:, row : row + params, :], recv[:, row + params : row + 2 * params, :], n, params, cst_ref)
+
+
+def combine_coded(recv, row, params, n, cst_ref, narrow=False):
+    v = recv.astype(F32)
+    if narrow:
+        v = v[:, 0 : 2 * params] + v[:, 2 * params : 4 * params]
+        combine_sums(v[:, 0:params], v[:, params:], n, params, cst_ref)
+        return
+    s = v[:, row : row + params] + v[:, row + params : row + 2 * params]
+    combine_sums(s, v[:, row + 2 * params : row + 3 * params], n, params, cst_ref)
+
+
+def combine_sums(s, m2, n, params, cst_ref):
     k = n.sum(axis=0)
     mean = s.sum(axis=0) / k
     off = s / jnp.maximum(n, 1.0) - mean[None]
@@ -219,8 +250,17 @@
 def fold32(v):
     v = v[:, 0:LN] + v[:, LN:256]
     v = v + pltpu.roll(v, 32, 1)
-    v = v + pltpu.roll(v, 64, 1)
-    return v[:, 0:CF_MID]
+    return v + pltpu.roll(v, 64, 1)
+
+
+def tiled_rows(scratch, tiled):
+    c = tiled.shape[0]
+    scratch[0:c, :] = tiled
+    group = lax.broadcasted_iota(jnp.int32, (c // 4, LN), 1) >> 5
+    out = jnp.zeros((c // 4, LN), F32)
+    for q in range(4):
+        out = jnp.where(group == q, scratch[pl.ds(q, c // 4, stride=4), :], out)
+    return out
 
 
 def pack3(pad, b, mid, left, right, px, grid):
@@ -337,7 +377,8 @@
         px, grid, n, ndp = self.px, self.grid, self.n, self.ndp
         fold = params == 1
         two = other is not None
-        rows = 4 + (0 if more is None else more.shape[0])
+        rows = 4 + (0 if more is None else more.array.shape[0])
+        coded = 8 + 3 * (rows - 4) // 2
 
         def body(int_ref, recv_ref, n_ref, x_ref, par_ref, w_ref, *refs):
             o_ref = None
@@ -346,7 +387,8 @@
             if more is not None:
                 m_ref, refs = refs[0], refs[1:]
             h_ref, y_ref, cst_ref, pay_ref = refs[:4]
-            row_ref, pad = refs[-2:]
+            row_ref, pad = refs[4 + two : 6 + two]
+            code_ref = refs[-1]
             if two:
                 refs[4][...] = recv_ref[...]
             side = int_ref[0]
@@ -375,17 +417,21 @@
                     acc = part if acc is None else acc + part
                 y_ref[:, g * 256 : (g + 1) * 256] = acc
             moments(y_ref, row_ref, 0, 4, params, fold, mask, side_sq(side, frames))
-            if more is not None:
+            if more is None:
+                send(pay_ref, row_ref)
+            else:
                 row_ref[4:rows, :] = m_ref[...]
-            send(pay_ref, row_ref)
+                encode(code_ref, row_ref, 4, rows // 2 - 2)
+                send(pay_ref, code_ref)
 
         extra = [other] if two else []
         extra += [] if more is None else [more]
         return call(
             body,
-            [((px, 512), BF16), ((px, 512), F32), ((8, LN), F32), ((n, rows, LN), F32, "far")]
+            [((px, 512), BF16), ((px, 512), F32), ((8, LN), F32), ((n, rows, LN), F32, "far") if more is None else ((n, coded, LN), BF16, "far")]
             + ([((n, 4, LN), F32)] if two else []),
-            [pltpu.VMEM((rows, LN), F32), pltpu.VMEM((px + 2 * grid, 2 * 768), BF16)],
+            [pltpu.VMEM((rows, LN), F32), pltpu.VMEM((px + 2 * grid, 2 * 768), BF16)]
+            + ([] if more is None else [pltpu.VMEM((coded, LN), F32)]),
             ints, recv, counts, x, par, w, *extra,
             **kw,
         )
@@ -393,13 +439,20 @@
     def expand_stage(self, ints, recv, counts, y, par, w, params, wide, frames, edge=False, **kw):
         px, grid, n = self.px, self.grid, self.n
         rows = max(2 * wide, 4)
+        code = wide > 1
+        coded = 3 * wide
 
         def body(int_ref, recv_ref, n_ref, y_ref, par_ref, w_ref, h_ref, cst_ref, pay_ref, *refs):
-            row_ref, c_ref = refs[-2:]
+            row_ref, c_ref = refs[edge : edge + 2]
+            code_ref = refs[-1]
             side = int_ref[0]
             mask = region(side, px, grid)
             half_mask = 0.5 * mask
-            combine(recv_ref[...], 0, params, n_ref[:, 2:3, :] * float(frames), cst_ref)
+            count = n_ref[:, 2:3, :] * float(frames)
+            if code:
+                combine_coded(recv_ref[...], 0, params, count, cst_ref, True)
+            else:
+                combine(recv_ref[...], 0, params, count, cst_ref)
             mean, rs = cst_ref[0:params, :], cst_ref[params : 2 * params, :]
             scale = par_ref[0:params, :] * rs
             shift = par_ref[params : 2 * params, :] - mean * scale
@@ -412,23 +465,26 @@
             for g in range(2):
                 c_ref[:, g * 1024 : (g + 1) * 1024] = dot(h_ref[:, g * 256 : (g + 1) * 256], w_ref[...])
             moments(c_ref, row_ref, 0, 16, wide, False, mask, side_sq(side, frames))
-            send(pay_ref, row_ref)
-
-        return call(
-            body,
-            [((px, 512), BF16), ((8, LN), F32), ((n, rows, LN), F32, "far")]
+            if code:
+                encode(code_ref, row_ref, 0, wide)
+            send(pay_ref, code_ref if code else row_ref)
+
+        return call(
+            body,
+            [((px, 512), BF16), ((8, LN), F32), ((n, coded, LN), BF16, "far") if code else ((n, rows, LN), F32, "far")]
             + ([((px, LN), BF16, "far")] if edge else []),
-            [pltpu.VMEM((rows, LN), F32), pltpu.VMEM((px, 2048), F32)],
+            [pltpu.VMEM((rows, LN), F32), pltpu.VMEM((px, 2048), F32)]
+            + ([pltpu.VMEM((coded, LN), F32)] if code else []),
             ints, recv, counts, y, par, w,
             **kw,
         )
 
-    def fast_finish(self, ints, recv, counts, h2, h2_other, w, xf, par, wlat, **kw):
-        px, grid = self.px, self.grid
+    def fast_finish(self, ints, recv, counts, h2, h2_other, w, xf, par, wlat, pa, wa, **kw):
+        px, grid, n = self.px, self.grid, self.n
 
         def body(
-            int_ref, recv_ref, n_ref, h_ref, ho_ref, w_ref, xf_ref, par_ref, wl_ref,
-            y_ref, lat_ref, cst_ref, c_ref,
+            int_ref, recv_ref, n_ref, h_ref, ho_ref, w_ref, xf_ref, par_ref, wl_ref, pa_ref, wa_ref,
+            y_ref, lat_ref, cst_ref, sa_ref, pay_ref, c_ref, row_ref,
         ):
             half_mask = 0.5 * region(int_ref[0], px, grid)
             combine(recv_ref[...], 0, 1, n_ref[:, 2:3, :] * float(TF // 2), cst_ref)
@@ -452,12 +508,17 @@
             for t in range(2):
                 at = ALPHA * t * CF
                 lat_ref[:, t * LAT : (t + 1) * LAT] = dot(y_ref[:, at : at + 5 * CF], wl_ref[...]).astype(BF16)
-
-        return call(
-            body,
-            [((px, 18 * CF), BF16), ((px, 512), BF16), ((8, LN), F32)],
-            [pltpu.VMEM((px, 1024), F32)],
-            ints, recv, counts, h2, h2_other, w, xf, par, wlat,
+                a = slice(t * CS_MID, (t + 1) * CS_MID)
+                sa_ref[:, a] = pa_ref[:, a] + dot(lat_ref[:, t * LAT : (t + 1) * LAT], wa_ref[...])
+            side = int_ref[0]
+            moments(sa_ref, row_ref, 0, 4, 2, False, region(side, px, grid), side_sq(side, TS // 2))
+            send(pay_ref, row_ref)
+
+        return call(
+            body,
+            [((px, 18 * CF), BF16), ((px, 512), BF16), ((8, LN), F32), ((px, 512), F32), ((n, 4, LN), F32, "far")],
+            [pltpu.VMEM((px, 1024), F32), pltpu.VMEM((4, LN), F32)],
+            ints, recv, counts, h2, h2_other, w, xf, par, wlat, pa, wa,
             **kw,
         )
 
@@ -492,13 +553,11 @@
 
         return call(body, [((px, 512), F32), ((px, 2048), F32)], [], xs, wa, wp, smem=0, **kw)
 
-    def slow_join(self, ints, part, lat, w, params, alone=True, **kw):
-        px, grid, n = self.px, self.grid, self.n
+    def slow_join(self, ints, part, lat, w, params, **kw):
+        px, grid = self.px, self.grid
         width = params * LN
-        rows = max(2 * params, 4)
-
-        def body(int_ref, part_ref, lat_ref, w_ref, out_ref, pay_ref, *refs):
-            row_ref = refs[0] if alone else pay_ref
+
+        def body(int_ref, part_ref, lat_ref, w_ref, out_ref, row_ref):
             side = int_ref[0]
             for t in range(2):
                 at = slice(t * width, (t + 1) * width)
@@ -506,15 +565,9 @@
             moments(
                 out_ref, row_ref, 0, 2 * params, params, False, region(side, px, grid), side_sq(side, TS // 2)
             )
-            if alone:
-                send(pay_ref, row_ref)
-
-        return call(
-            body,
-            [((px, 2 * width), F32), ((n, rows, LN) if alone else (rows, LN), F32, "far")],
-            [pltpu.VMEM((rows, LN), F32)] if alone else [],
-            ints, part, lat, w,
-            **kw,
+
+        return call(
+            body, [((px, 2 * width), F32), ((2 * params, LN), F32)], [], ints, part, lat, w, **kw
         )
 
     def slow_top(self, ints, recv3, recvp, counts, h2, w, sp, gs, parc, parp, **kw):
@@ -526,8 +579,8 @@
         ):
             half_mask = 0.5 * region(int_ref[0], px, grid)
             count = n_ref[:, 2:3, :] * float(TS // 2)
-            combine(r3_ref[...], 0, 8, count, cc_ref)
-            combine(rp_ref[...], 4, 8, count, cp_ref)
+            combine_coded(r3_ref[...], 0, 8, count, cc_ref)
+            combine_coded(rp_ref[...], 8, 8, count, cp_ref)
             k_ref[0:8, :] = pc_ref[0:8, :] * cc_ref[8:16, :]
             k_ref[8:16, :] = pp_ref[0:8, :] * cp_ref[8:16, :]
             k_ref[16:24, :] = pc_ref[8:16, :] + pp_ref[8:16, :]
@@ -791,17 +844,12 @@
 
         return call(body, ((px, 2048), BF16, "far"), [], da, dp, wa, wp, smem=0, **kw)
 
-    def fast_first_back(self, ints, counts, recv, dn_lo, dn_hi, fa_lo, fa_hi, cst, par, xf, bc, bc_other, **kw):
-        px, grid, ndp = self.px, self.grid, self.ndp
-        rows = bc.shape[0]
-
-        def body(
-            int_ref, n_ref, recv_ref, dl_ref, dh_ref, xl_ref, xh_ref, cst_ref, par_ref, x_ref, b0_ref, b1_ref,
-            da_ref, sum_ref, pay_ref, row_ref,
-        ):
+    def fast_first_back(self, ints, counts, recv, dn_lo, dn_hi, fa_lo, fa_hi, cst, par, **kw):
+        px, grid = self.px, self.grid
+
+        def body(int_ref, n_ref, recv_ref, dl_ref, dh_ref, xl_ref, xh_ref, cst_ref, par_ref, da_ref, sum_ref):
             sums = recv_ref[...].sum(axis=0)
             sum_ref[...] = sums
-            row_ref[...] = b0_ref[...] + b1_ref[...]
 
             @pl.when(int_ref[1] == 1)
             def _():
@@ -816,6 +864,25 @@
                         e = (h_ref[:, lanes(b)] - mean) * c0
                         e = (dn_ref[:, lanes(b)] * a - b0 - e) * mask
                         da_ref[:, lanes(base + b)] = e.astype(BF16)
+
+        return call(
+            body,
+            [((px, 1024), BF16), ((4, LN), F32, "far")],
+            [],
+            ints, counts, recv, dn_lo, dn_hi, fa_lo, fa_hi, cst, par,
+            **kw,
+        )
+
+    def fast_small(self, ints, da, xf, bc, bc_other, **kw):
+        first = 3 * CF_MID
+        rows = first + bc.shape[0]
+
+        def body(int_ref, da_ref, x_ref, b0_ref, b1_ref, out_ref, row_ref, scratch):
+            row_ref[0:first, :] = jnp.zeros((first, LN), F32)
+            row_ref[first:rows, :] = b0_ref[...] + b1_ref[...]
+
+            @pl.when(int_ref[1] == 1)
+            def _():
                 accs = [None] * 3
                 for g in range(4):
                     lo, hi = max(8 * g - 1, 0), min(8 * g + 9, TF)
@@ -828,15 +895,16 @@
                                 part = d[i * CF_MID : (i + 1) * CF_MID, j * CF : (j + 1) * CF]
                                 accs[k] = part if accs[k] is None else accs[k] + part
                 for k in range(3):
-                    row_ref[k * CF_MID : (k + 1) * CF_MID, :] = accs[k]
-
-            send(pay_ref, row_ref)
-
-        return call(
-            body,
-            [((px, 1024), BF16), ((4, LN), F32, "far"), ((ndp, rows, LN), BF16, "far")],
-            [pltpu.VMEM((rows, LN), F32)],
-            ints, counts, recv, dn_lo, dn_hi, fa_lo, fa_hi, cst, par, xf, bc, bc_other,
+                    tiled = jnp.concatenate([accs[k]] * 4, axis=0).T
+                    row_ref[k * CF_MID : (k + 1) * CF_MID, :] = tiled_rows(scratch, tiled)
+
+            out_ref[...] = row_ref[...].astype(BF16)
+
+        return call(
+            body,
+            ((rows, LN), BF16, "far"),
+            [pltpu.VMEM((rows, LN), F32), pltpu.VMEM((LN, LN), F32)],
+            ints, da, xf, bc, bc_other,
             **kw,
         )
 
@@ -954,7 +1022,7 @@
     def fast_grads_bc(self, h1, db, h2, dc, **kw):
         px, grid = self.px, self.grid
 
-        def body(h1_ref, db_ref, h2_ref, dc_ref, gb_ref, gc_ref, pad):
+        def body(h1_ref, db_ref, h2_ref, dc_ref, out_ref, pad, scratch):
             clear_edges(pad, px, grid)
             for b in range(4):
                 h = h1_ref[:, lanes(b)].astype(F32)
@@ -973,7 +1041,8 @@
                             db_ref[:, g * 256 : (g + 1) * 256],
                         )
                     acc = jnp.where(same, acc, 0.0).reshape(8, CF_MID, 256).sum(axis=0)
-                    gb_ref[3 * i + s] = fold32(acc)
+                    at = (3 * i + s) * 8
+                    out_ref[at : at + 8, :] = tiled_rows(scratch, fold32(acc))
             acc = jnp.zeros((256, 1024), F32)
             for g in range(2):
                 acc = acc + dot(h2_ref[:, g * 256 : (g + 1) * 256].T, dc_ref[:, g * 1024 : (g + 1) * 1024])
@@ -981,12 +1050,13 @@
             for i in range(8):
                 part = acc[i * CF_MID : (i + 1) * CF_MID, i * CF : (i + 1) * CF]
                 out = part if out is None else out + part
-            gc_ref[...] = out
-
-        return call(
-            body,
-            [((9, CF_MID, CF_MID), F32, "far"), ((CF_MID, CF), F32, "far")],
-            [pltpu.VMEM((px + 2 * grid, 2 * 768), BF16)],
+            out_ref[72:104, :] = out
+            out_ref[104:, :] = jnp.zeros((8, LN), F32)
+
+        return call(
+            body,
+            ((112, LN), F32, "far"),
+            [pltpu.VMEM((px + 2 * grid, 2 * 768), BF16), pltpu.VMEM((CF_MID, LN), F32)],
             h1, db, h2, dc, smem=0,
             **kw,
         )
@@ -1172,15 +1242,18 @@
             **kw,
         )
 
-    def window(self, plan, ints, keep, came, vectors, small, tail, **kw):
+    def window(self, plan, ints, keep, came, small, small_other, vectors, tail, **kw):
         chunk, out_rows = plan.chunk, plan.out_rows
-        pad = small.shape[0] + 8
-
-        def body(int_ref, keep_ref, came_ref, vec_ref, small_ref, tail_ref, out_ref, a_ref):
+        extra = small.shape[0]
+        pad = extra + 8
+
+        def body(int_ref, keep_ref, came_ref, s0_ref, s1_ref, vec_ref, tail_ref, out_ref, a_ref, small_ref):
             r0 = int_ref[2]
             row = int_ref[3]
             lane = int_ref[4]
             a_ref[...] = jnp.zeros_like(a_ref)
+            total = s0_ref[...].astype(F32) + s1_ref[...].astype(F32)
+            small_ref[...] = jnp.where(int_ref[1] == 1, total, 0.0)
             for ref, start, n in (
                 (vec_ref, ROW_SG, 2 * SLOW_VEC), (small_ref, ROW_FA, ROW_LAT - ROW_FA), (tail_ref, ROW_FG, 3)
             ):
@@ -1198,8 +1271,8 @@
         return call(
             body,
             ((out_rows, LN), F32, "far"),
-            [pltpu.VMEM((chunk + 2 * pad + 8, LN), F32)],
-            ints, keep, came, vectors, small, tail,
+            [pltpu.VMEM((chunk + 2 * pad + 8, LN), F32), pltpu.VMEM((extra, LN), F32)],
+            ints, keep, came, small, small_other, vectors, tail,
             **kw,
         )
 
@@ -1220,7 +1293,7 @@
         self.out_rows = -(-self.share // LN)
         self.bits = ndp.bit_length() - 1
         one = list(range(self.bits))
-        two = [b ^ 1 if (b ^ 1) < self.bits else b for b in one]
+        two = one if self.bits < 3 else [1, 2, 0] + one[3:]
         self.order = [one, two]
 
     def place(self, path, j):
@@ -1308,12 +1381,11 @@
     fh2_other = swap(fh2_edge)
     (pa, pp), tok = net.slow_start(xs, w_slow_a, w_slow_proj, us=3.5, after=[pay], token=True)
     r = exchange(pay)
-    yf, lat, fc3 = net.fast_finish(
-        ints, r, r1, fh2, fh2_other, fc_w, xf, f3, wlat, us=3.0, after=[tok]
+    yf, lat, fc3, sa, pay = net.fast_finish(
+        ints, r, r1, fh2, fh2_other, fc_w, xf, f3, wlat, pa, wa_lat, us=5.0, after=[tok]
     )
 
-    sa, pay = net.slow_join(ints, pa, lat, wa_lat, 2, us=2.0)
-    (sp, sp_rows), tok = net.slow_join(ints, pp, lat, wp_lat, 8, False, us=3.0, after=[pay], token=True)
+    (sp, sp_rows), tok = net.slow_join(ints, pp, lat, wp_lat, 8, us=3.0, after=[pay], token=True)
     r = exchange(pay)
     sh1, sb, sc1, pay = net.conv_stage(
         ints, r, r1, sa, s1, wb3, 2, TS // 2, more=sp_rows, us=3.0, after=[tok]
@@ -1345,55 +1417,58 @@
         ints, r1, r, dn, sa, sc1, s1, dp, wa_lat, wp_lat, us=3.0, after=[tok], through=[conv]
     )
     dl_other = swap(dl0)
-
-    (fds, pay), (conv_out,) = net.fast_top(
-        ints, dl0, dl1, dl_other, wlat, gf, gp, fh2, fc_w, fc3, us=4.0, through=[conv_out]
+    (late, late_out), tok = net.grads_late(ints, xs, lat, da, yf, dl0, dl1, us=4.0, token=True)
+
+    (fds, pay), (conv_out, late_out) = net.fast_top(
+        ints, dl0, dl1, dl_other, wlat, gf, gp, fh2, fc_w, fc3, us=4.0, through=[conv_out, late_out]
     )
     conv_in = swap(conv_out)
+    late_in = swap(late_out)
     fds_lo = swap(fds)
-    (late, late_out), tok = net.grads_late(ints, xs, lat, da, yf, dl0, dl1, us=4.0, after=[pay], token=True)
-    dxs, tok2 = net.slow_input_grad(da, dp, w_slow_a, w_slow_proj, us=4.0, after=[tok], token=True)
-    r = exchange(pay)
-    (fdc, dn, u3, pay), (late_out, dxs_out) = net.expand_back(
-        ints, r1, r, fds, fh2, fc_w, fc3, f3, fb, fc2, f2, 1, 1, half,
-        us=4.0, after=[tok2], through=[late_out, dxs],
-    )
-    late_in = swap(late_out)
     (keep, there), tok = net.windows(
-        plan, ints, (Far(early), Far(early_in)), (Far(conv_out), Far(conv_in)), (Far(late), late_in),
+        plan, ints, (Far(early), early_in), (Far(conv_out), conv_in), (Far(late), late_in),
         us=6.0, after=[pay], token=True,
     )
     r = exchange(pay)
-    (fdb, dn, u2, pay), (there, dxs_out) = net.conv_back(
+    (fdc, dn, u3, pay), (there,) = net.expand_back(
+        ints, r1, r, fds, fh2, fc_w, fc3, f3, fb, fc2, f2, 1, 1, half,
+        us=5.0, after=[tok], through=[there],
+    )
+    here = lax.ppermute(there, ("path", "dp"), plan.pairs(0))
+    dxs, tok = net.slow_input_grad(da, dp, w_slow_a, w_slow_proj, us=4.0, after=[pay], token=True)
+    r = exchange(pay)
+    (fdb, dn, u2, pay), (dxs_out,) = net.conv_back(
         ints, r1, r, dn, fb, fc2, f2, fbt_w, fa_hi, fc1, f1, 1, half, fa_other,
-        us=3.5, after=[tok], through=[there, dxs_out],
+        us=4.0, after=[tok], through=[dxs],
     )
     dn_lo = swap(dn)
-    here = lax.ppermute(there, ("path", "dp"), plan.pairs(0))
-    gb, gc = net.fast_grads_bc(fh1, fdb, fh2, fdc, us=3.5, after=[pay])
-    bc = jnp.concatenate([gb.reshape(-1, LN), gc], axis=0)
-    bc = jnp.pad(bc, ((0, -bc.shape[0] % 16), (0, 0)))
+    bc, tok = net.fast_grads_bc(fh1, fdb, fh2, fdc, us=4.0, after=[pay], token=True)
+    got, tok = net.halve(plan, ints, 1, keep, here, us=3.0, after=[tok], token=True)
+    r = exchange(pay)
+    (fda, u1), (bc, *there) = net.fast_first_back(
+        ints, r1, r, dn_lo, dn, Far(fa_lo), fa_hi, fc1, f1, us=2.5, after=[tok], through=[bc] + got[1:]
+    )
     bc_other = swap(bc)
-    r = exchange(pay)
-    fda, u1, pay = net.fast_first_back(
-        ints, r1, r, dn_lo, dn, Far(fa_lo), fa_hi, fc1, f1, x, bc, bc_other, us=3.5
-    )
+    small = net.fast_small(ints, fda, x, bc, bc_other, us=3.0)
     dxs_other = swap(dxs_out)
-    dx = net.last(ints, fda, Far(fds_lo), fds, band, dxs_out, dxs_other, us=4.5, after=[pay])
-
-    out = net.out_join(ints, ys, yf, theirs, us=3.0)
-
-    for step in range(1, plan.bits):
-        keep, there = net.halve(plan, ints, step, keep, here, us=1.5)
+    keep = got[0]
+    first = small
+    for step in range(plan.bits):
+        small_other = lax.ppermute(small, ("path", "dp"), plan.pairs(step))
+        if step < plan.bits - 1:
+            small = (small.astype(F32) + small_other.astype(F32)).astype(BF16)
+    here = lax.ppermute(there[0], ("path", "dp"), plan.pairs(1))
+    for step in range(2, plan.bits):
+        keep, there = net.halve(plan, ints, step, keep, here, us=2.5, after=[first])
         here = lax.ppermute(there, ("path", "dp"), plan.pairs(step))
-    small = lax.all_to_all(pay, "dp", 0, 0).astype(F32).sum(axis=0)
-    bc = swap(small)
-    ga = small[: 3 * CF_MID].reshape(3, CF_MID, CF).transpose(0, 2, 1).reshape(-1, LN)
-    small = jnp.where(core0, 0.0, jnp.concatenate([ga, bc], axis=0))
+    dx = net.last(ints, fda, Far(fds_lo), fds, band, dxs_out, dxs_other, us=4.5, after=[first])
+
+    out = net.out_join(ints, ys, yf, theirs, us=3.0, after=[first])
+
     vectors = jnp.concatenate([t1[2:4], t2[2:4], t3[8:24], t1[0:2], t2[0:2], t3[0:8], t3[0:8]], axis=0)
     tail = jnp.concatenate([u1[1, :32], u2[1, :32], u3[1], u1[0, :32], u2[0, :32], u3[0]]).reshape(3, LN)
     tail = jnp.pad(tail, ((0, 5), (0, 0)))
-    flat = net.window(plan, ints, keep, here, vectors, small, tail).reshape(-1)[: plan.share]
+    flat = net.window(plan, ints, keep, here, small, small_other, vectors, tail).reshape(-1)[: plan.share]
     return (out.reshape(acts.shape), dx.reshape(acts.shape), flat)
 
 

time: 267 us -> 258 us (0.966)
  starting transfers between devices: 67.5 us -> 58.2 us
  waiting for transfers between devices: 58.2 us -> 61.3 us
    ppermute x0 -> x5, starting transfers between devices: none -> 7.53 us  [the longest x4 6.63 us: local(): small_other = lax.ppermute(small, ('path', 'dp'), plan.pairs(step))]
    ppermute x3 -> x2, starting transfers between devices: 8.5 us -> 1.1 us  [local(): here = lax.ppermute(there, ('path', 'dp'), plan.pairs(step))]
    all_to_all x1 -> x0, waiting for transfers between devices: 6.85 us -> none  [local(): small = lax.all_to_all(pay, 'dp', 0, 0).astype(F32).sum(axis=0)]
    ppermute x1, waiting for transfers between devices: 6.5 us -> 0.01 us  [local(): here = lax.ppermute(there, ('path', 'dp'), plan.pairs(0))]
    all_to_all x12, waiting for transfers between devices: 42.2 us -> 48.5 us  [exchange(): return lax.all_to_all(x, ('path', 'dp'), 0, 0)]
    ppermute x0 -> x5, waiting for transfers between devices: none -> 5.8 us  [the longest x4 5.79 us: local(): small_other = lax.ppermute(small, ('path', 'dp'), plan.pairs(step))]
    all_to_all x1 -> x0, starting transfers between devices: 5.68 us -> none  [local(): small = lax.all_to_all(pay, 'dp', 0, 0).astype(F32).sum(axis=0)]
    all_to_all x12, starting transfers between devices: 48.7 us -> 43.6 us  [exchange(): return lax.all_to_all(x, ('path', 'dp'), 0, 0)]
  transfers between devices with their start and end apart: 31 -> 33, of which waited for: 14 -> 16; matrix products, arithmetic and copies ran while one was open for 1% -> 1% of each run, Pallas kernels for 33% -> 36%
where the time goes in v3:
time: 258 us; the launch traced here: 257 us
  Pallas kernels  125 us (48%)
  waiting for transfers between devices  61.3 us (24%)
  starting transfers between devices  58.2 us (23%)
  local copies, waits for them, and re-layouts  9.28 us (4%)
    pallas_call x33, Pallas kernels, call(): pl.pallas_call(wrapped, out_shape=shapes, grid=(1,) if cut else (), in_sp...  125 us
    all_to_all x12, waiting for transfers between devices, exchange(): return lax.all_to_all(x, ('path', 'dp'), 0, 0)  48.5 us
    all_to_all x12, starting transfers between devices, exchange(): return lax.all_to_all(x, ('path', 'dp'), 0, 0)  43.6 us
    unnamed x59, local copies, waits for them, and re-layouts  7.8 us
    ppermute x4, starting transfers between devices, local(): small_other = lax.ppermute(small, ('path', 'dp'), plan.pairs(step))  6.63 us
    ppermute x4, waiting for transfers between devices, local(): small_other = lax.ppermute(small, ('path', 'dp'), plan.pairs(step))  5.79 us
    ppermute x2, waiting for transfers between devices, local(): here = lax.ppermute(there, ('path', 'dp'), plan.pairs(step))  5.57 us
    ppermute x13, starting transfers between devices, swap(): return lax.ppermute(x, 'path', SWAP)  5.22 us
  transfers between devices with their start and end apart: 33, of which 16 were waited for; matrix products, arithmetic and copies ran while one was open for 1% of the time, Pallas kernels for 36%

profile of v3, /device:TPU:0, one launch (start us, length us, event | category | flops | bytes accessed | tf_op | source)
XLA Modules:
  0.0 256.6 jit_solution(6496436729556080380)
XLA Ops:
  8.7 6.9 %all-to-all-start = ((f32[32,4,128]{2,1,0:T(4,128)}), f32[32,4,128]{2,1,0:T(4,128)S(1)}, u32[]{:S(2)}, u32[]{:S(2)}) async-start(f32[32,4,128]{2,1,0:T(4,128)} %get-tuple-element.107.refs_3_), calls=%async_computation | async-start | bytes 131072 | tf_op jit(solution)/shard_map/all_to_all | solution.py:1314
  18.3 4.7 %all-to-all-done.refs_1_.refs_2_ = f32[32,4,128]{2,1,0:T(4,128)S(1)} async-done(((f32[32,4,128]{2,1,0:T(4,128)}), f32[32,4,128]{2,1,0:T(4,128)S(1)}, u32[]{:S(2)}, u32[]{:S(2)}) %all-to-all-start) | async-done | bytes 65568 | tf_op jit(solution)/shard_map/all_to_all | solution.py:1314
  29.4 4.8 %shard_map.169 = (bf16[256,2048]{1,0:T(8,128)(2,1)}, bf16[256,2304]{1,0:T(8,128)(2,1)}, bf16[256,2048]{1,0:T(8,128)(2,1)}, bf16[256,2048]{1,0:T(8,128)(2,1)}, f32[8,128]{1,0:T(8,128)}) custom-call(s32[9]{0:T(128)S(1)} %stack.63.refs_0_, bf16[256,4096]{1,0:T(8,128)(2,1)} %bitcast.66, bf16[256,4096]{1,0:T(8,128)(2,1)} %collective-permute-done.1.refs_2_, ...), custom_call_target="tpu_custom_call" | custom-call | flops 2500000000 | tf_op jit(solution)/shard_map/pallas_call | solution.py:112
  36.7 4.0 %shard_map.170 = (bf16[256,512]{1,0:T(8,128)(2,1)}, f32[8,128]{1,0:T(8,128)}, f32[32,4,128]{2,1,0:T(4,128)}, bf16[256,128]{1,0:T(8,128)(2,1)}) custom-call(s32[9]{0:T(128)S(1)} %stack.63.refs_0_, f32[32,4,128]{2,1,0:T(4,128)S(1)} %all-to-all-done.1.refs_1_, f32[32,4,128]{2,1,0:T(4,128)} %get-tuple-element.113.refs_2_.refs_3_.refs_1_, ...), custom_call_target="tpu_custom_call" | custom-call | flops 2600000000 | tf_op jit(solution)/shard_map/pallas_call | solution.py:112
  46.0 4.2 %shard_map.171 = (f32[256,512]{1,0:T(8,128)}, f32[256,2048]{1,0:T(8,128)}, f32[8,128]{1,0:T(8,128)}) custom-call(bf16[256,2048]{1,0:T(8,128)(2,1)} %get-tuple-element.121.refs_0_.refs_1_, bf16[1280,256]{1,0:T(8,128)(2,1)S(1)} %copy-done.6, bf16[1280,1024]{1,0:T(8,128)(2,1)S(1)} %copy-done.2, f32[32,4,128]{2,1,0:T(4,128)} %get-tuple-element.117.refs_3_), custom_call_target="tpu_custom_call" | custom-call | flops 3500000000 | tf_op jit(solution)/shard_map/pallas_call | solution.py:112
  51.5 5.6 %shard_map.172 = (bf16[256,2304]{1,0:T(8,128)(2,1)}, bf16[256,512]{1,0:T(8,128)(2,1)}, f32[8,128]{1,0:T(8,128)}, f32[256,512]{1,0:T(8,128)}, f32[32,4,128]{2,1,0:T(4,128)}) custom-call(s32[9]{0:T(128)S(1)} %stack.63.refs_0_, f32[32,4,128]{2,1,0:T(4,128)S(1)} %all-to-all-done.2.refs_1_, f32[32,4,128]{2,1,0:T(4,128)} %get-tuple-element.113.refs_2_.refs_3_.refs_1_, ...), custom_call_target="tpu_custom_call" | custom-call | flops 5000000000 | tf_op jit(solution)/shard_map/pallas_call | solution.py:112
  57.1 4.4 %all-to-all-start.3 = ((f32[32,4,128]{2,1,0:T(4,128)}), f32[32,4,128]{2,1,0:T(4,128)S(1)}, u32[]{:S(2)}, u32[]{:S(2)}) async-start(f32[32,4,128]{2,1,0:T(4,128)} %get-tuple-element.124.refs_4_), calls=%async_computation.3 | async-start | bytes 131072 | tf_op jit(solution)/shard_map/all_to_all | solution.py:1314
  61.6 4.0 %shard_map.173 = (f32[256,2048]{1,0:T(8,128)}, f32[16,128]{1,0:T(8,128)}, f32[8,128]{1,0:T(8,128)}) custom-call(s32[9]{0:T(128)S(1)} %stack.63.refs_0_, f32[256,2048]{1,0:T(8,128)} %get-tuple-element.126.refs_1_, bf16[256,512]{1,0:T(8,128)(2,1)} %get-tuple-element.127.refs_2_, bf16[1280,1024]{1,0:T(8,128)(2,1)} %refs_3_.3, ...), custom_call_target="tpu_custom_call" | custom-call | flops 3000000000 | tf_op jit(solution)/shard_map/pallas_call | solution.py:112
  74.7 5.1 %shard_map.175 = (f32[256,2048]{1,0:T(8,128)}, f32[8,128]{1,0:T(8,128)}) custom-call(s32[9]{0:T(128)S(1)} %stack.63.refs_0_, bf16[256,512]{1,0:T(8,128)(2,1)} %get-tuple-element.118.refs_3_.refs_1_.refs_7_.refs_4_.refs_2_, bf16[256,1024]{1,0:T(8,128)(2,1)} %get-tuple-element.115.refs_5_.refs_2_.refs_8_, ...), custom_call_target="tpu_custom_call" | custom-call | flops 4000000000 | tf_op jit(solution)/shard_map/pallas_call | solution.py:112
  79.8 6.1 %all-to-all-done.4.refs_1_.refs_2_ = bf16[32,32,128]{2,1,0:T(8,128)(2,1)S(1)} async-done(((bf16[32,32,128]{2,1,0:T(8,128)(2,1)}), bf16[32,32,128]{2,1,0:T(8,128)(2,1)S(1)}, u32[]{:S(2)}, u32[]{:S(2)}) %all-to-all-start.4) | async-done | bytes 262176 | tf_op jit(solution)/shard_map/all_to_all | solution.py:1314
  91.7 9.6 %all-to-all-done.5.refs_1_ = bf16[32,24,128]{2,1,0:T(8,128)(2,1)S(1)} async-done(((bf16[32,24,128]{2,1,0:T(8,128)(2,1)}), bf16[32,24,128]{2,1,0:T(8,128)(2,1)S(1)}, u32[]{:S(2)}, u32[]{:S(2)}) %all-to-all-start.5) | async-done | bytes 196640 | tf_op jit(solution)/shard_map/all_to_all | solution.py:1314
  101.3 6.8 %shard_map.177 = (bf16[256,2048]{1,0:T(8,128)(2,1)}, f32[256,2048]{1,0:T(8,128)}, f32[16,128]{1,0:T(8,128)}, f32[16,128]{1,0:T(8,128)}, bf16[32,24,128]{2,1,0:T(8,128)(2,1)}) custom-call(s32[9]{0:T(128)S(1)} %stack.63.refs_0_, bf16[32,24,128]{2,1,0:T(8,128)(2,1)S(1)} %all-to-all-done.5.refs_1_, bf16[32,32,128]{2,1,0:T(8,128)(2,1)S(1)} %all-to-all-done.4.refs_1_.refs_2_, ...), custom_call_target="tpu_custom_call" | custom-call | flops 6000000000 | tf_op jit(solution)/shard_map/pallas_call | solution.py:112
  114.1 6.4 %all-to-all-done.6.refs_2_ = bf16[32,24,128]{2,1,0:T(8,128)(2,1)S(1)} async-done(((bf16[32,24,128]{2,1,0:T(8,128)(2,1)}), bf16[32,24,128]{2,1,0:T(8,128)(2,1)S(1)}, u32[]{:S(2)}, u32[]{:S(2)}) %all-to-all-start.6) | async-done | bytes 196640 | tf_op jit(solution)/shard_map/all_to_all | solution.py:1314
  120.5 6.2 %shard_map.179 = (bf16[256,2048]{1,0:T(8,128)(2,1)}, bf16[256,2048]{1,0:T(8,128)(2,1)}, f32[256,512]{1,0:T(8,128)}, f32[24,128]{1,0:T(8,128)}, f32[32,4,128]{2,1,0:T(4,128)}, /*index=5*/bf16[256,2048]{1,0:T(8,128)(2,1)}) custom-call(s32[9]{0:T(128)S(1)} %stack.63.refs_0_, ...), custom_call_target="tpu_custom_call", output_to_operand_aliasing={{5}: (15, {})} | custom-call | flops 6000000000 | tf_op jit(solution)/shard_map/pallas_call | solution.py:112
  129.2 7.1 %shard_map.180 = (bf16[8976,128]{1,0:T(8,128)(2,1)}, bf16[8976,128]{1,0:T(8,128)(2,1)}, f32[8,128]{1,0:T(8,128)}) custom-call(s32[9]{0:T(128)S(1)} %stack.63.refs_0_, bf16[256,2048]{1,0:T(8,128)(2,1)} %get-tuple-element.121.refs_0_.refs_1_, bf16[256,512]{1,0:T(8,128)(2,1)} %get-tuple-element.127.refs_2_, ...), custom_call_target="tpu_custom_call" | custom-call | flops 6000000000 | tf_op jit(solution)/shard_map/pallas_call | solution.py:112
  140.0 5.6 %all-to-all-start.8 = ((f32[32,4,128]{2,1,0:T(4,128)}), f32[32,4,128]{2,1,0:T(4,128)S(1)}, u32[]{:S(2)}, u32[]{:S(2)}) async-start(f32[32,4,128]{2,1,0:T(4,128)} %get-tuple-element.155.refs_2_), calls=%async_computation.8 | async-start | bytes 131072 | tf_op jit(solution)/shard_map/all_to_all | solution.py:1314
  156.0 4.1 %shard_map.184 = (bf16[2560,128]{1,0:T(8,128)(2,1)}, bf16[2560,128]{1,0:T(8,128)(2,1)}, f32[8,128]{1,0:T(8,128)}) custom-call(s32[9]{0:T(128)S(1)} %stack.63.refs_0_, bf16[256,2048]{1,0:T(8,128)(2,1)} %get-tuple-element.121.refs_0_.refs_1_, bf16[256,512]{1,0:T(8,128)(2,1)} %get-tuple-element.127.refs_2_, ...), custom_call_target="tpu_custom_call" | custom-call | flops 4000000000 | tf_op jit(solution)/shard_map/pallas_call | solution.py:112
  160.2 4.2 %shard_map.185 = (f32[256,2048]{1,0:T(8,128)}, f32[32,4,128]{2,1,0:T(4,128)}, bf16[4608,128]{1,0:T(8,128)(2,1)}, bf16[2560,128]{1,0:T(8,128)(2,1)}) custom-call(s32[9]{0:T(128)S(1)} %stack.63.refs_0_, bf16[256,256]{1,0:T(8,128)(2,1)} %get-tuple-element.161.refs_5_.refs_1_, ...), custom_call_target="tpu_custom_call", output_to_operand_aliasing={{2}: (10, {}), {3}: (11, {})} | custom-call | flops 4000000000 | tf_op jit(solution)/shard_map/pallas_call | solution.py:112
  169.3 5.3 %shard_map.186 = (bf16[8,672,128]{2,1,0:T(8,128)(2,1)}, bf16[8,672,128]{2,1,0:T(8,128)(2,1)}, f32[8,128]{1,0:T(8,128)}) custom-call(s32[9]{0:T(128)S(1)} %stack.63.refs_0_, bf16[8976,128]{1,0:T(8,128)(2,1)} %get-tuple-element.171.refs_1_, bf16[8976,128]{1,0:T(8,128)(2,1)S(1)} %collective-permute-done.6.refs_2_, ...), custom_call_target="tpu_custom_call" | custom-call | flops 6000000000 | tf_op jit(solution)/shard_map/pallas_call | solution.py:112
  175.3 5.0 %shard_map.187 = (bf16[256,2048]{1,0:T(8,128)(2,1)}, f32[256,512]{1,0:T(8,128)}, f32[4,128]{1,0:T(4,128)}, f32[32,4,128]{2,1,0:T(4,128)}, bf16[8,672,128]{2,1,0:T(8,128)(2,1)}) custom-call(s32[9]{0:T(128)S(1)} %stack.63.refs_0_, f32[32,4,128]{2,1,0:T(4,128)} %get-tuple-element.113.refs_2_.refs_3_.refs_1_, ...), custom_call_target="tpu_custom_call", output_to_operand_aliasing={{4}: (12, {})} | custom-call | flops 5000000000 | tf_op jit(solution)/shard_map/pallas_call | solution.py:112
  186.9 3.9 %shard_map.188 = (bf16[256,2048]{1,0:T(8,128)(2,1)}, f32[8,128]{1,0:T(8,128)}) custom-call(bf16[256,512]{1,0:T(8,128)(2,1)} %get-tuple-element.166.refs_3_.refs_0_, bf16[256,2048]{1,0:T(8,128)(2,1)} %get-tuple-element.151.refs_3_.refs_7_.refs_1_, bf16[1280,256]{1,0:T(8,128)(2,1)S(1)} %copy-done.7, bf16[1280,1024]{1,0:T(8,128)(2,1)S(1)} %copy-done.3, ...), custom_call_target="tpu_custom_call" | custom-call | flops 4000000000 | tf_op jit(solution)/shard_map/pallas_call | solution.py:112
  190.8 8.9 %all-to-all-done.10.refs_2_ = f32[32,4,128]{2,1,0:T(4,128)S(1)} async-done(((f32[32,4,128]{2,1,0:T(4,128)}), f32[32,4,128]{2,1,0:T(4,128)S(1)}, u32[]{:S(2)}, u32[]{:S(2)}) %all-to-all-start.10) | async-done | bytes 65568 | tf_op jit(solution)/shard_map/all_to_all | solution.py:1314
  235.8 5.4 %shard_map.195 = bf16[256,4096]{1,0:T(8,128)(2,1)} custom-call(s32[9]{0:T(128)S(1)} %stack.63.refs_0_, bf16[256,1024]{1,0:T(8,128)(2,1)} %get-tuple-element.195.refs_1_, f32[256,2048]{1,0:T(8,128)} %collective-permute-done.12.refs_2_, f32[256,2048]{1,0:T(8,128)} %get-tuple-element.169.refs_3_, bf16[1280,256]{1,0:T(8,128)(2,1)} %get-tuple-element.197.refs_4_, ...), custom_call_target="tpu_custom_call" | custom-call | flops 4499999744 | tf_op jit(solution)/shard_map/pallas_call | solution.py:112
  249.4 5.6 %collective-permute-done.16.refs_2_ = bf16[1,672,128]{2,1,0:T(8,128)(2,1)S(1)} collective-permute-done((bf16[1,672,128]{2,1,0:T(8,128)(2,1)}, bf16[1,672,128]{2,1,0:T(8,128)(2,1)S(1)}, u32[]{:S(2)}, u32[]{:S(2)}) %collective-permute-start.16) | collective-permute-done | bytes 172064 | tf_op jit(solution)/shard_map/ppermute | solution.py:1463
  (164 shorter events, 120.9 us)
Async XLA Ops:
  0.6 28.7 %collective-permute-start.1 = (bf16[256,4096]{1,0:T(8,128)(2,1)}, bf16[256,4096]{1,0:T(8,128)(2,1)}, u32[]{:S(2)}, u32[]{:S(2)}) collective-permute-start(bf16[256,4096]{1,0:T(8,128)(2,1)} %bitcast.65), channel_id=1, source_target_pairs={{0,16},{16,0},{1,17},{17,1},{2,18},{18,2},{3,19},{19,3},{4,20},{20... | collective-permute-start | bytes 6291464 | tf_op jit(solution)/shard_map/ppermute | solution.py:1319
  1.1 28.2 %collective-permute-start.2 = (bf16[256,4096]{1,0:T(8,128)(2,1)}, bf16[256,4096]{1,0:T(8,128)(2,1)}, u32[]{:S(2)}, u32[]{:S(2)}) collective-permute-start(bf16[256,4096]{1,0:T(8,128)(2,1)} %bitcast.73), channel_id=1, source_target_pairs={{0,16},{16,0},{1,17},{17,1},{2,18},{18,2},{3,19},{19,3},{4,20},{20... | collective-permute-start | bytes 6291464 | tf_op jit(solution)/shard_map/ppermute | solution.py:1319
  6.1 16.8 %collective-permute-start = (f32[256,512]{1,0:T(8,128)}, f32[256,512]{1,0:T(8,128)S(1)}, u32[]{:S(2)}, u32[]{:S(2)}) collective-permute-start(f32[256,512]{1,0:T(8,128)} %get-tuple-element.110.refs_5_), channel_id=1, source_target_pairs={{0,16},{16,0},{1,17},{17,1},{2,18},{18,2},{3,19},{19,3},{4,20},{20... | collective-permute-start | bytes 1572872 | tf_op jit(solution)/shard_map/ppermute | solution.py:1319
  8.7 14.3 %all-to-all-start = ((f32[32,4,128]{2,1,0:T(4,128)}), f32[32,4,128]{2,1,0:T(4,128)S(1)}, u32[]{:S(2)}, u32[]{:S(2)}) async-start(f32[32,4,128]{2,1,0:T(4,128)} %get-tuple-element.107.refs_3_), calls=%async_computation | async-start | bytes 131072 | tf_op jit(solution)/shard_map/all_to_all | solution.py:1314
  26.8 9.9 %all-to-all-start.1 = ((f32[32,4,128]{2,1,0:T(4,128)}), f32[32,4,128]{2,1,0:T(4,128)S(1)}, u32[]{:S(2)}, u32[]{:S(2)}) async-start(f32[32,4,128]{2,1,0:T(4,128)} %get-tuple-element.112.refs_5_), calls=%async_computation.1 | async-start | bytes 131072 | tf_op jit(solution)/shard_map/all_to_all | solution.py:1314
  40.7 10.8 %all-to-all-start.2 = ((f32[32,4,128]{2,1,0:T(4,128)}), f32[32,4,128]{2,1,0:T(4,128)S(1)}, u32[]{:S(2)}, u32[]{:S(2)}) async-start(f32[32,4,128]{2,1,0:T(4,128)} %get-tuple-element.117.refs_3_), calls=%async_computation.2 | async-start | bytes 131072 | tf_op jit(solution)/shard_map/all_to_all | solution.py:1314
  57.1 11.8 %all-to-all-start.3 = ((f32[32,4,128]{2,1,0:T(4,128)}), f32[32,4,128]{2,1,0:T(4,128)S(1)}, u32[]{:S(2)}, u32[]{:S(2)}) async-start(f32[32,4,128]{2,1,0:T(4,128)} %get-tuple-element.124.refs_4_), calls=%async_computation.3 | async-start | bytes 131072 | tf_op jit(solution)/shard_map/all_to_all | solution.py:1314
  72.1 13.8 %all-to-all-start.4 = ((bf16[32,32,128]{2,1,0:T(8,128)(2,1)}), bf16[32,32,128]{2,1,0:T(8,128)(2,1)S(1)}, u32[]{:S(2)}, u32[]{:S(2)}) async-start(bf16[32,32,128]{2,1,0:T(8,128)(2,1)} %get-tuple-element.130.refs_6_), calls=%async_computation.4 | async-start | bytes 524288 | tf_op jit(solution)/shard_map/all_to_all | solution.py:1314
  88.9 12.4 %all-to-all-start.5 = ((bf16[32,24,128]{2,1,0:T(8,128)(2,1)}), bf16[32,24,128]{2,1,0:T(8,128)(2,1)S(1)}, u32[]{:S(2)}, u32[]{:S(2)}) async-start(bf16[32,24,128]{2,1,0:T(8,128)(2,1)} %get-tuple-element.134), calls=%async_computation.5 | async-start | bytes 393216 | tf_op jit(solution)/shard_map/all_to_all | solution.py:1314
  108.1 12.4 %all-to-all-start.6 = ((bf16[32,24,128]{2,1,0:T(8,128)(2,1)}), bf16[32,24,128]{2,1,0:T(8,128)(2,1)S(1)}, u32[]{:S(2)}, u32[]{:S(2)}) async-start(bf16[32,24,128]{2,1,0:T(8,128)(2,1)} %get-tuple-element.140.refs_3_), calls=%async_computation.6 | async-start | bytes 393216 | tf_op jit(solution)/shard_map/all_to_all | solution.py:1314
  126.7 9.9 %all-to-all-start.7 = ((f32[32,4,128]{2,1,0:T(4,128)}), f32[32,4,128]{2,1,0:T(4,128)S(1)}, u32[]{:S(2)}, u32[]{:S(2)}) async-start(f32[32,4,128]{2,1,0:T(4,128)} %get-tuple-element.148.refs_6_), calls=%async_computation.7 | async-start | bytes 131072 | tf_op jit(solution)/shard_map/all_to_all | solution.py:1314
  140.0 12.9 %all-to-all-start.8 = ((f32[32,4,128]{2,1,0:T(4,128)}), f32[32,4,128]{2,1,0:T(4,128)S(1)}, u32[]{:S(2)}, u32[]{:S(2)}) async-start(f32[32,4,128]{2,1,0:T(4,128)} %get-tuple-element.155.refs_2_), calls=%async_computation.8 | async-start | bytes 131072 | tf_op jit(solution)/shard_map/all_to_all | solution.py:1314
  145.7 23.7 %collective-permute-start.6 = (bf16[8976,128]{1,0:T(8,128)(2,1)}, bf16[8976,128]{1,0:T(8,128)(2,1)S(1)}, u32[]{:S(2)}, u32[]{:S(2)}) collective-permute-start(bf16[8976,128]{1,0:T(8,128)(2,1)} %get-tuple-element.172), channel_id=1, source_target_pairs={{0,16},{16,0},{1,17},{17,1},{2,18},{18,2},{3,19},{19,3},{4,20},{20... | collective-permute-start | bytes 6893576 | tf_op jit(solution)/shard_map/ppermute | solution.py:1319
  164.9 81.1 %collective-permute-start.4 = (bf16[256,2048]{1,0:T(8,128)(2,1)}, bf16[256,2048]{1,0:T(8,128)(2,1)}, u32[]{:S(2)}, u32[]{:S(2)}) collective-permute-start(bf16[256,2048]{1,0:T(8,128)(2,1)} %get-tuple-element.147), channel_id=1, source_target_pairs={{0,16},{16,0},{1,17},{17,1},{2,18},{18,2},{3,19},{19,3},{4,20},{20... | collective-permute-start | bytes 3145736 | tf_op jit(solution)/shard_map/ppermute | solution.py:1319
  165.4 9.9 %all-to-all-start.9 = ((f32[32,4,128]{2,1,0:T(4,128)}), f32[32,4,128]{2,1,0:T(4,128)S(1)}, u32[]{:S(2)}, u32[]{:S(2)}) async-start(f32[32,4,128]{2,1,0:T(4,128)} %get-tuple-element.168.refs_7_), calls=%async_computation.9 | async-start | bytes 131072 | tf_op jit(solution)/shard_map/all_to_all | solution.py:1314
  180.3 30.8 %collective-permute-start.10 = (bf16[8,672,128]{2,1,0:T(8,128)(2,1)}, bf16[8,672,128]{2,1,0:T(8,128)(2,1)S(1)}, u32[]{:S(2)}, u32[]{:S(2)}) collective-permute-start(bf16[8,672,128]{2,1,0:T(8,128)(2,1)} %get-tuple-element.187), channel_id=1, source_target_pairs={{0,1},{1,0},{2,3},{3,2},{4,5},{5,4},{6,7},{7,6},{8,9},{9,8},{10,11... | collective-permute-start | bytes 4128776 | tf_op jit(solution)/shard_map/ppermute | solution.py:1437
  181.3 53.6 %collective-permute-start.12 = (f32[256,2048]{1,0:T(8,128)}, f32[256,2048]{1,0:T(8,128)}, u32[]{:S(2)}, u32[]{:S(2)}) collective-permute-start(f32[256,2048]{1,0:T(8,128)} %get-tuple-element.169.refs_3_), channel_id=1, source_target_pairs={{0,16},{16,0},{1,17},{17,1},{2,18},{18,2},{3,19},{19,3},{4,20},{20... | collective-permute-start | bytes 6291464 | tf_op jit(solution)/shard_map/ppermute | solution.py:1319
  181.3 18.4 %all-to-all-start.10 = ((f32[32,4,128]{2,1,0:T(4,128)}), f32[32,4,128]{2,1,0:T(4,128)S(1)}, u32[]{:S(2)}, u32[]{:S(2)}) async-start(f32[32,4,128]{2,1,0:T(4,128)} %get-tuple-element.178.refs_4_), calls=%async_computation.10 | async-start | bytes 131072 | tf_op jit(solution)/shard_map/all_to_all | solution.py:1314
  203.6 11.2 %collective-permute-start.9 = (f32[256,512]{1,0:T(8,128)}, f32[256,512]{1,0:T(8,128)S(1)}, u32[]{:S(2)}, u32[]{:S(2)}) collective-permute-start(f32[256,512]{1,0:T(8,128)} %get-tuple-element.185.refs_4_), channel_id=1, source_target_pairs={{0,16},{16,0},{1,17},{17,1},{2,18},{18,2},{3,19},{19,3},{4,20},{20... | collective-permute-start | bytes 1572872 | tf_op jit(solution)/shard_map/ppermute | solution.py:1319
  203.8 11.0 %all-to-all-start.11 = ((f32[32,4,128]{2,1,0:T(4,128)}), f32[32,4,128]{2,1,0:T(4,128)S(1)}, u32[]{:S(2)}, u32[]{:S(2)}) async-start(f32[32,4,128]{2,1,0:T(4,128)} %get-tuple-element.184.refs_4_), calls=%async_computation.11 | async-start | bytes 131072 | tf_op jit(solution)/shard_map/all_to_all | solution.py:1314
  217.2 17.6 %collective-permute-start.13 = (bf16[256,2048]{1,0:T(8,128)(2,1)S(1)}, bf16[256,2048]{1,0:T(8,128)(2,1)S(1)}, u32[]{:S(2)}, u32[]{:S(2)}) collective-permute-start(bf16[256,2048]{1,0:T(8,128)(2,1)S(1)} %copy-done.28), channel_id=1, source_target_pairs={{0,16},{16,0},{1,17},{17,1},{2,18},{18,2},{3,19},{19,3},{4,20},{20... | collective-permute-start | bytes 3145736 | tf_op jit(solution)/shard_map/ppermute | solution.py:1319
  217.8 14.4 %collective-permute-start.14 = (bf16[4,672,128]{2,1,0:T(8,128)(2,1)}, bf16[4,672,128]{2,1,0:T(8,128)(2,1)S(1)}, u32[]{:S(2)}, u32[]{:S(2)}) collective-permute-start(bf16[4,672,128]{2,1,0:T(8,128)(2,1)} %get-tuple-element.200), channel_id=1, source_target_pairs={{0,2},{1,3},{2,0},{3,1},{4,6},{5,7},{6,4},{7,5},{8,10},{9,11},{10,... | collective-permute-start | bytes 2064392 | tf_op jit(solution)/shard_map/ppermute | solution.py:1460
  230.6 10.6 %collective-permute-start.19 = (bf16[208,128]{1,0:T(8,128)(2,1)S(1)}, bf16[208,128]{1,0:T(8,128)(2,1)S(1)}, u32[]{:S(2)}, u32[]{:S(2)}) collective-permute-start(bf16[208,128]{1,0:T(8,128)(2,1)S(1)} %add_convert_fusion.1), channel_id=1, source_target_pairs={{0,4},{1,5},{2,6},{3,7},{4,0},{5,1},{6,2},{7,3},{8,12},{9,13},{10,... | collective-permute-start | bytes 159752 | tf_op jit(solution)/shard_map/ppermute | solution.py:1457
  245.5 9.5 %collective-permute-start.16 = (bf16[1,672,128]{2,1,0:T(8,128)(2,1)}, bf16[1,672,128]{2,1,0:T(8,128)(2,1)S(1)}, u32[]{:S(2)}, u32[]{:S(2)}) collective-permute-start(bf16[1,672,128]{2,1,0:T(8,128)(2,1)} %get-tuple-element.204), channel_id=1, source_target_pairs={{0,8},{1,9},{2,10},{3,11},{4,12},{5,13},{6,14},{7,15},{8,0},{9,1},... | collective-permute-start | bytes 516104 | tf_op jit(solution)/shard_map/ppermute | solution.py:1463
  (38 other events, 235.6 us)

commit v4 on v3

--- a/solution.py
+++ b/solution.py
@@ -917,16 +917,16 @@
                 return pltpu.make_async_copy(out_ref.at[:, at], dx_ref.at[:, at], sem.at[g])
 
             def half(ref, g):
-                return pltpu.make_async_copy(ref, out_ref.at[:, g * 2048 : (g + 1) * 2048], sem.at[g])
+                return pltpu.make_async_copy(ref, out_ref.at[:, g * 2048 : (g + 1) * 2048], sem.at[4 + g])
 
             @pl.when(int_ref[1] == 0)
             def _():
                 half(x0_ref, 0).start()
                 half(x1_ref, 1).start()
-                half(x0_ref, 0).wait()
-                half(x1_ref, 1).wait()
-                for g in range(4):
-                    part(g).start()
+                for g in range(2):
+                    half(x0_ref if g == 0 else x1_ref, g).wait()
+                    part(2 * g).start()
+                    part(2 * g + 1).start()
                 for g in range(4):
                     part(g).wait()
 
@@ -951,7 +951,7 @@
         return call(
             body,
             ((px, 4096), BF16, "manual"),
-            [pltpu.VMEM((px, 34 * CF), F32), pltpu.VMEM((px, 4096), BF16), pltpu.SemaphoreType.DMA((4,))],
+            [pltpu.VMEM((px, 34 * CF), F32), pltpu.VMEM((px, 4096), BF16), pltpu.SemaphoreType.DMA((6,))],
             ints, da, ds_lo, ds_hi, band, Manual(dxs0), Manual(dxs1),
             **kw,
         )
@@ -1242,17 +1242,24 @@
             **kw,
         )
 
-    def window(self, plan, ints, keep, came, small, small_other, vectors, tail, **kw):
+    def add(self, parts, **kw):
+        def body(*refs):
+            refs[-1][...] = sum(r[...].astype(F32) for r in refs[:-1]).astype(BF16)
+
+        return call(body, (parts[0].shape, BF16, "far"), [], Far(parts[0]), *parts[1:], smem=0, **kw)
+
+    def window(self, plan, ints, keep, came, parts, vectors, tail, **kw):
         chunk, out_rows = plan.chunk, plan.out_rows
-        extra = small.shape[0]
+        extra, count = parts[0].shape[0], len(parts)
         pad = extra + 8
 
-        def body(int_ref, keep_ref, came_ref, s0_ref, s1_ref, vec_ref, tail_ref, out_ref, a_ref, small_ref):
+        def body(int_ref, keep_ref, came_ref, vec_ref, tail_ref, *refs):
+            out_ref, a_ref, small_ref = refs[count:]
             r0 = int_ref[2]
             row = int_ref[3]
             lane = int_ref[4]
             a_ref[...] = jnp.zeros_like(a_ref)
-            total = s0_ref[...].astype(F32) + s1_ref[...].astype(F32)
+            total = sum(r[...].astype(F32) for r in refs[:count])
             small_ref[...] = jnp.where(int_ref[1] == 1, total, 0.0)
             for ref, start, n in (
                 (vec_ref, ROW_SG, 2 * SLOW_VEC), (small_ref, ROW_FA, ROW_LAT - ROW_FA), (tail_ref, ROW_FG, 3)
@@ -1272,7 +1279,7 @@
             body,
             ((out_rows, LN), F32, "far"),
             [pltpu.VMEM((chunk + 2 * pad + 8, LN), F32), pltpu.VMEM((extra, LN), F32)],
-            ints, keep, came, small, small_other, vectors, tail,
+            ints, keep, came, vectors, tail, *parts,
             **kw,
         )
 
@@ -1293,14 +1300,20 @@
         self.out_rows = -(-self.share // LN)
         self.bits = ndp.bit_length() - 1
         one = list(range(self.bits))
-        two = one if self.bits < 3 else [1, 2, 0] + one[3:]
+        two = one[1:] + one[:1]
         self.order = [one, two]
+        self.stages = [
+            [m << b for m in range(1, 1 << min(2, self.bits - b))] for b in range(0, self.bits, 2)
+        ]
 
     def place(self, path, j):
         at = 0
         for b in self.order[path]:
             at = 2 * at + ((j >> b) & 1)
         return at
+
+    def route(self, mask):
+        return [(q * self.ndp + j, q * self.ndp + (j ^ mask)) for q in range(2) for j in range(self.ndp)]
 
     def pairs(self, step):
         out = []
@@ -1412,6 +1425,7 @@
     )
     early_in = swap(early_out)
     conv, tok = net.grads_conv(sh1, db, us=3.0, after=[pay], token=True)
+    out, tok = net.out_join(ints, ys, yf, theirs, us=3.0, after=[tok], token=True)
     r = exchange(pay)
     (da, dl0, dl1, t1), (conv_out,) = net.slow_last(
         ints, r1, r, dn, sa, sc1, s1, dp, wa_lat, wp_lat, us=3.0, after=[tok], through=[conv]
@@ -1436,39 +1450,37 @@
     )
     here = lax.ppermute(there, ("path", "dp"), plan.pairs(0))
     dxs, tok = net.slow_input_grad(da, dp, w_slow_a, w_slow_proj, us=4.0, after=[pay], token=True)
+    (keep, there), tok = net.halve(plan, ints, 1, keep, here, us=3.0, after=[tok], token=True)
     r = exchange(pay)
-    (fdb, dn, u2, pay), (dxs_out,) = net.conv_back(
+    (fdb, dn, u2, pay), (dxs_out, there) = net.conv_back(
         ints, r1, r, dn, fb, fc2, f2, fbt_w, fa_hi, fc1, f1, 1, half, fa_other,
-        us=4.0, after=[tok], through=[dxs],
+        us=4.0, after=[tok], through=[dxs, there],
     )
     dn_lo = swap(dn)
+    here = lax.ppermute(there, ("path", "dp"), plan.pairs(1))
     bc, tok = net.fast_grads_bc(fh1, fdb, fh2, fdc, us=4.0, after=[pay], token=True)
-    got, tok = net.halve(plan, ints, 1, keep, here, us=3.0, after=[tok], token=True)
+    (keep, there), tok = net.halve(plan, ints, 2, keep, here, us=2.5, after=[tok], token=True)
     r = exchange(pay)
-    (fda, u1), (bc, *there) = net.fast_first_back(
-        ints, r1, r, dn_lo, dn, Far(fa_lo), fa_hi, fc1, f1, us=2.5, after=[tok], through=[bc] + got[1:]
+    (fda, u1), (bc, there) = net.fast_first_back(
+        ints, r1, r, dn_lo, dn, Far(fa_lo), fa_hi, fc1, f1, us=2.5, after=[tok], through=[bc, there]
     )
     bc_other = swap(bc)
+    dxs_other = swap(dxs_out)
     small = net.fast_small(ints, fda, x, bc, bc_other, us=3.0)
-    dxs_other = swap(dxs_out)
-    keep = got[0]
-    first = small
-    for step in range(plan.bits):
-        small_other = lax.ppermute(small, ("path", "dp"), plan.pairs(step))
-        if step < plan.bits - 1:
-            small = (small.astype(F32) + small_other.astype(F32)).astype(BF16)
-    here = lax.ppermute(there[0], ("path", "dp"), plan.pairs(1))
-    for step in range(2, plan.bits):
-        keep, there = net.halve(plan, ints, step, keep, here, us=2.5, after=[first])
+    here = lax.ppermute(there, ("path", "dp"), plan.pairs(2))
+    for step in range(3, plan.bits):
+        keep, there = net.halve(plan, ints, step, keep, here, us=2.5, after=[small])
         here = lax.ppermute(there, ("path", "dp"), plan.pairs(step))
-    dx = net.last(ints, fda, Far(fds_lo), fds, band, dxs_out, dxs_other, us=4.5, after=[first])
-
-    out = net.out_join(ints, ys, yf, theirs, us=3.0, after=[first])
+    for k, masks in enumerate(plan.stages):
+        parts = [small] + [lax.ppermute(small, ("path", "dp"), plan.route(m)) for m in masks]
+        if k < len(plan.stages) - 1:
+            small = net.add(parts, us=1.0, after=[keep, dxs_other, fds_lo] if k == 0 else [])
+    dx = net.last(ints, fda, Far(fds_lo), fds, band, dxs_out, dxs_other, us=4.5, after=[small])
 
     vectors = jnp.concatenate([t1[2:4], t2[2:4], t3[8:24], t1[0:2], t2[0:2], t3[0:8], t3[0:8]], axis=0)
     tail = jnp.concatenate([u1[1, :32], u2[1, :32], u3[1], u1[0, :32], u2[0, :32], u3[0]]).reshape(3, LN)
     tail = jnp.pad(tail, ((0, 5), (0, 0)))
-    flat = net.window(plan, ints, keep, here, small, small_other, vectors, tail).reshape(-1)[: plan.share]
+    flat = net.window(plan, ints, keep, here, parts, vectors, tail).reshape(-1)[: plan.share]
     return (out.reshape(acts.shape), dx.reshape(acts.shape), flat)
 
 

time: 258 us -> 255 us (0.988)
  waiting for transfers between devices: 61.3 us -> 53.4 us
  starting transfers between devices: 58.2 us -> 62.5 us
    all_to_all x12, waiting for transfers between devices: 48.5 us -> 36 us  [exchange(): return lax.all_to_all(x, ('path', 'dp'), 0, 0)]
    ppermute x1, waiting for transfers between devices: 0.01 us -> 8.82 us  [local(): here = lax.ppermute(there, ('path', 'dp'), plan.pairs(0))]
    ppermute x2 -> x1, waiting for transfers between devices: 5.57 us -> 0.01 us  [local(): here = lax.ppermute(there, ('path', 'dp'), plan.pairs(step))]
    all_to_all x12, starting transfers between devices: 43.6 us -> 48.8 us  [exchange(): return lax.all_to_all(x, ('path', 'dp'), 0, 0)]
    ppermute x5 -> x8, waiting for transfers between devices: 5.8 us -> 8.61 us  [the longest x1 4.6 us: local(): here = lax.ppermute(there, ('path', 'dp'), plan.pairs(2))]
    pallas_call x33 -> x34, Pallas kernels: 125 us -> 126 us  [call(): pl.pallas_call(wrapped, out_shape=shapes, grid=(1,) if cut else (), in_sp...]
    unnamed x59 -> x55, local copies, waits for them, and re-layouts: 7.8 us -> 6.82 us
    ppermute x5 -> x8, starting transfers between devices: 7.53 us -> 8.3 us  [the longest x6 6.67 us: local(): lax.ppermute(small, ('path', 'dp'), plan.route(m))]
  transfers between devices with their start and end apart: 33 -> 35, of which waited for: 16 -> 14; matrix products, arithmetic and copies ran while one was open for 1% -> 1% of each run, Pallas kernels for 36% -> 36%
where the time goes in v4:
time: 255 us; the launch traced here: 253 us
  Pallas kernels  126 us (49%)
  starting transfers between devices  62.5 us (25%)
  waiting for transfers between devices  53.4 us (21%)
  local copies, waits for them, and re-layouts  9.04 us (4%)
    pallas_call x34, Pallas kernels, call(): pl.pallas_call(wrapped, out_shape=shapes, grid=(1,) if cut else (), in_sp...  126 us
    all_to_all x12, starting transfers between devices, exchange(): return lax.all_to_all(x, ('path', 'dp'), 0, 0)  48.8 us
    all_to_all x12, waiting for transfers between devices, exchange(): return lax.all_to_all(x, ('path', 'dp'), 0, 0)  36 us
    ppermute x1, waiting for transfers between devices, local(): here = lax.ppermute(there, ('path', 'dp'), plan.pairs(0))  8.82 us
    unnamed x55, local copies, waits for them, and re-layouts  6.82 us
    ppermute x6, starting transfers between devices, local(): lax.ppermute(small, ('path', 'dp'), plan.route(m))  6.67 us
  transfers between devices with their start and end apart: 35, of which 14 were waited for; matrix products, arithmetic and copies ran while one was open for 1% of the time, Pallas kernels for 36%

profile of v4, /device:TPU:0, one launch (start us, length us, event | category | flops | bytes accessed | tf_op | source)
XLA Modules:
  0.0 253.0 jit_solution(12179124930512803489)
XLA Ops:
  6.1 9.1 %all-to-all-start = ((f32[32,4,128]{2,1,0:T(4,128)}), f32[32,4,128]{2,1,0:T(4,128)S(1)}, u32[]{:S(2)}, u32[]{:S(2)}) async-start(f32[32,4,128]{2,1,0:T(4,128)} %get-tuple-element.111.refs_3_), calls=%async_computation | async-start | bytes 131072 | tf_op jit(solution)/shard_map/all_to_all | solution.py:1327
  18.1 4.4 %all-to-all-done.refs_1_.refs_2_ = f32[32,4,128]{2,1,0:T(4,128)S(1)} async-done(((f32[32,4,128]{2,1,0:T(4,128)}), f32[32,4,128]{2,1,0:T(4,128)S(1)}, u32[]{:S(2)}, u32[]{:S(2)}) %all-to-all-start) | async-done | bytes 65568 | tf_op jit(solution)/shard_map/all_to_all | solution.py:1327
  29.0 4.9 %shard_map.169 = (bf16[256,2048]{1,0:T(8,128)(2,1)}, bf16[256,2304]{1,0:T(8,128)(2,1)}, bf16[256,2048]{1,0:T(8,128)(2,1)}, bf16[256,2048]{1,0:T(8,128)(2,1)}, f32[8,128]{1,0:T(8,128)}) custom-call(s32[9]{0:T(128)S(1)} %stack.63.refs_0_, bf16[256,4096]{1,0:T(8,128)(2,1)} %bitcast.66, bf16[256,4096]{1,0:T(8,128)(2,1)} %collective-permute-done.1.refs_2_, ...), custom_call_target="tpu_custom_call" | custom-call | flops 2500000000 | tf_op jit(solution)/shard_map/pallas_call | solution.py:112
  36.3 4.0 %shard_map.170 = (bf16[256,512]{1,0:T(8,128)(2,1)}, f32[8,128]{1,0:T(8,128)}, f32[32,4,128]{2,1,0:T(4,128)}, bf16[256,128]{1,0:T(8,128)(2,1)}) custom-call(s32[9]{0:T(128)S(1)} %stack.63.refs_0_, f32[32,4,128]{2,1,0:T(4,128)S(1)} %all-to-all-done.1.refs_1_, f32[32,4,128]{2,1,0:T(4,128)} %get-tuple-element.117.refs_2_.refs_3_.refs_1_, ...), custom_call_target="tpu_custom_call" | custom-call | flops 2600000000 | tf_op jit(solution)/shard_map/pallas_call | solution.py:112
  45.8 4.1 %shard_map.171 = (f32[256,512]{1,0:T(8,128)}, f32[256,2048]{1,0:T(8,128)}, f32[8,128]{1,0:T(8,128)}) custom-call(bf16[256,2048]{1,0:T(8,128)(2,1)} %get-tuple-element.125.refs_0_.refs_1_, bf16[1280,256]{1,0:T(8,128)(2,1)S(1)} %copy-done.6, bf16[1280,1024]{1,0:T(8,128)(2,1)S(1)} %copy-done.2, f32[32,4,128]{2,1,0:T(4,128)} %get-tuple-element.121.refs_3_), custom_call_target="tpu_custom_call" | custom-call | flops 3500000000 | tf_op jit(solution)/shard_map/pallas_call | solution.py:112
  51.1 5.6 %shard_map.172 = (bf16[256,2304]{1,0:T(8,128)(2,1)}, bf16[256,512]{1,0:T(8,128)(2,1)}, f32[8,128]{1,0:T(8,128)}, f32[256,512]{1,0:T(8,128)}, f32[32,4,128]{2,1,0:T(4,128)}) custom-call(s32[9]{0:T(128)S(1)} %stack.63.refs_0_, f32[32,4,128]{2,1,0:T(4,128)S(1)} %all-to-all-done.2.refs_1_, f32[32,4,128]{2,1,0:T(4,128)} %get-tuple-element.117.refs_2_.refs_3_.refs_1_, ...), custom_call_target="tpu_custom_call" | custom-call | flops 5000000000 | tf_op jit(solution)/shard_map/pallas_call | solution.py:112
  56.7 4.6 %all-to-all-start.3 = ((f32[32,4,128]{2,1,0:T(4,128)}), f32[32,4,128]{2,1,0:T(4,128)S(1)}, u32[]{:S(2)}, u32[]{:S(2)}) async-start(f32[32,4,128]{2,1,0:T(4,128)} %get-tuple-element.128.refs_4_), calls=%async_computation.3 | async-start | bytes 131072 | tf_op jit(solution)/shard_map/all_to_all | solution.py:1327
  61.3 4.0 %shard_map.173 = (f32[256,2048]{1,0:T(8,128)}, f32[16,128]{1,0:T(8,128)}, f32[8,128]{1,0:T(8,128)}) custom-call(s32[9]{0:T(128)S(1)} %stack.63.refs_0_, f32[256,2048]{1,0:T(8,128)} %get-tuple-element.130.refs_1_, bf16[256,512]{1,0:T(8,128)(2,1)} %get-tuple-element.131.refs_2_, bf16[1280,1024]{1,0:T(8,128)(2,1)} %refs_3_.3, ...), custom_call_target="tpu_custom_call" | custom-call | flops 3000000000 | tf_op jit(solution)/shard_map/pallas_call | solution.py:112
  74.5 5.1 %shard_map.175 = (f32[256,2048]{1,0:T(8,128)}, f32[8,128]{1,0:T(8,128)}) custom-call(s32[9]{0:T(128)S(1)} %stack.63.refs_0_, bf16[256,512]{1,0:T(8,128)(2,1)} %get-tuple-element.122.refs_3_.refs_1_.refs_7_.refs_4_.refs_2_, bf16[256,1024]{1,0:T(8,128)(2,1)} %get-tuple-element.119.refs_5_.refs_2_.refs_8_, ...), custom_call_target="tpu_custom_call" | custom-call | flops 4000000000 | tf_op jit(solution)/shard_map/pallas_call | solution.py:112
  79.5 6.1 %all-to-all-done.4.refs_1_.refs_2_ = bf16[32,32,128]{2,1,0:T(8,128)(2,1)S(1)} async-done(((bf16[32,32,128]{2,1,0:T(8,128)(2,1)}), bf16[32,32,128]{2,1,0:T(8,128)(2,1)S(1)}, u32[]{:S(2)}, u32[]{:S(2)}) %all-to-all-start.4) | async-done | bytes 262176 | tf_op jit(solution)/shard_map/all_to_all | solution.py:1327
  91.4 9.6 %all-to-all-done.5.refs_1_ = bf16[32,24,128]{2,1,0:T(8,128)(2,1)S(1)} async-done(((bf16[32,24,128]{2,1,0:T(8,128)(2,1)}), bf16[32,24,128]{2,1,0:T(8,128)(2,1)S(1)}, u32[]{:S(2)}, u32[]{:S(2)}) %all-to-all-start.5) | async-done | bytes 196640 | tf_op jit(solution)/shard_map/all_to_all | solution.py:1327
  101.0 6.7 %shard_map.177 = (bf16[256,2048]{1,0:T(8,128)(2,1)}, f32[256,2048]{1,0:T(8,128)}, f32[16,128]{1,0:T(8,128)}, f32[16,128]{1,0:T(8,128)}, bf16[32,24,128]{2,1,0:T(8,128)(2,1)}) custom-call(s32[9]{0:T(128)S(1)} %stack.63.refs_0_, bf16[32,24,128]{2,1,0:T(8,128)(2,1)S(1)} %all-to-all-done.5.refs_1_, bf16[32,32,128]{2,1,0:T(8,128)(2,1)S(1)} %all-to-all-done.4.refs_1_.refs_2_, ...), custom_call_target="tpu_custom_call" | custom-call | flops 6000000000 | tf_op jit(solution)/shard_map/pallas_call | solution.py:112
  113.7 6.4 %all-to-all-done.6.refs_2_ = bf16[32,24,128]{2,1,0:T(8,128)(2,1)S(1)} async-done(((bf16[32,24,128]{2,1,0:T(8,128)(2,1)}), bf16[32,24,128]{2,1,0:T(8,128)(2,1)S(1)}, u32[]{:S(2)}, u32[]{:S(2)}) %all-to-all-start.6) | async-done | bytes 196640 | tf_op jit(solution)/shard_map/all_to_all | solution.py:1327
  120.1 6.2 %shard_map.179 = (bf16[256,2048]{1,0:T(8,128)(2,1)}, bf16[256,2048]{1,0:T(8,128)(2,1)}, f32[256,512]{1,0:T(8,128)}, f32[24,128]{1,0:T(8,128)}, f32[32,4,128]{2,1,0:T(4,128)}, /*index=5*/bf16[256,2048]{1,0:T(8,128)(2,1)}) custom-call(s32[9]{0:T(128)S(1)} %stack.63.refs_0_, ...), custom_call_target="tpu_custom_call", output_to_operand_aliasing={{5}: (15, {})} | custom-call | flops 6000000000 | tf_op jit(solution)/shard_map/pallas_call | solution.py:112
  129.1 7.1 %shard_map.180 = (bf16[8976,128]{1,0:T(8,128)(2,1)}, bf16[8976,128]{1,0:T(8,128)(2,1)}, f32[8,128]{1,0:T(8,128)}) custom-call(s32[9]{0:T(128)S(1)} %stack.63.refs_0_, bf16[256,2048]{1,0:T(8,128)(2,1)} %get-tuple-element.125.refs_0_.refs_1_, bf16[256,512]{1,0:T(8,128)(2,1)} %get-tuple-element.131.refs_2_, ...), custom_call_target="tpu_custom_call" | custom-call | flops 6000000000 | tf_op jit(solution)/shard_map/pallas_call | solution.py:112
  139.7 5.8 %all-to-all-start.8 = ((f32[32,4,128]{2,1,0:T(4,128)}), f32[32,4,128]{2,1,0:T(4,128)S(1)}, u32[]{:S(2)}, u32[]{:S(2)}) async-start(f32[32,4,128]{2,1,0:T(4,128)} %get-tuple-element.161.refs_2_), calls=%async_computation.8 | async-start | bytes 131072 | tf_op jit(solution)/shard_map/all_to_all | solution.py:1327
  156.0 4.1 %shard_map.185 = (bf16[2560,128]{1,0:T(8,128)(2,1)}, bf16[2560,128]{1,0:T(8,128)(2,1)}, f32[8,128]{1,0:T(8,128)}) custom-call(s32[9]{0:T(128)S(1)} %stack.63.refs_0_, bf16[256,2048]{1,0:T(8,128)(2,1)} %get-tuple-element.125.refs_0_.refs_1_, bf16[256,512]{1,0:T(8,128)(2,1)} %get-tuple-element.131.refs_2_, ...), custom_call_target="tpu_custom_call" | custom-call | flops 4000000000 | tf_op jit(solution)/shard_map/pallas_call | solution.py:112
  160.1 4.3 %shard_map.186 = (f32[256,2048]{1,0:T(8,128)}, f32[32,4,128]{2,1,0:T(4,128)}, bf16[4608,128]{1,0:T(8,128)(2,1)}, bf16[2560,128]{1,0:T(8,128)(2,1)}) custom-call(s32[9]{0:T(128)S(1)} %stack.63.refs_0_, bf16[256,256]{1,0:T(8,128)(2,1)} %get-tuple-element.167.refs_5_.refs_1_, ...), custom_call_target="tpu_custom_call", output_to_operand_aliasing={{2}: (10, {}), {3}: (11, {})} | custom-call | flops 4000000000 | tf_op jit(solution)/shard_map/pallas_call | solution.py:112
  164.8 5.6 %all-to-all-start.9 = ((f32[32,4,128]{2,1,0:T(4,128)}), f32[32,4,128]{2,1,0:T(4,128)S(1)}, u32[]{:S(2)}, u32[]{:S(2)}) async-start(f32[32,4,128]{2,1,0:T(4,128)} %get-tuple-element.174.refs_7_), calls=%async_computation.9 | async-start | bytes 131072 | tf_op jit(solution)/shard_map/all_to_all | solution.py:1327
  170.5 5.2 %shard_map.187 = (bf16[8,672,128]{2,1,0:T(8,128)(2,1)}, bf16[8,672,128]{2,1,0:T(8,128)(2,1)}, f32[8,128]{1,0:T(8,128)}) custom-call(s32[9]{0:T(128)S(1)} %stack.63.refs_0_, bf16[8976,128]{1,0:T(8,128)(2,1)} %get-tuple-element.177.refs_1_, bf16[8976,128]{1,0:T(8,128)(2,1)S(1)} %collective-permute-done.6.refs_2_, ...), custom_call_target="tpu_custom_call" | custom-call | flops 6000000000 | tf_op jit(solution)/shard_map/pallas_call | solution.py:112
  177.8 5.0 %shard_map.188 = (bf16[256,2048]{1,0:T(8,128)(2,1)}, f32[256,512]{1,0:T(8,128)}, f32[4,128]{1,0:T(4,128)}, f32[32,4,128]{2,1,0:T(4,128)}, bf16[8,672,128]{2,1,0:T(8,128)(2,1)}) custom-call(s32[9]{0:T(128)S(1)} %stack.63.refs_0_, f32[32,4,128]{2,1,0:T(4,128)} %get-tuple-element.117.refs_2_.refs_3_.refs_1_, ...), custom_call_target="tpu_custom_call", output_to_operand_aliasing={{4}: (12, {})} | custom-call | flops 5000000000 | tf_op jit(solution)/shard_map/pallas_call | solution.py:112
  193.1 8.8 %collective-permute-done.9.refs_2_ = bf16[8,672,128]{2,1,0:T(8,128)(2,1)S(1)} collective-permute-done((bf16[8,672,128]{2,1,0:T(8,128)(2,1)}, bf16[8,672,128]{2,1,0:T(8,128)(2,1)S(1)}, u32[]{:S(2)}, u32[]{:S(2)}) %collective-permute-start.9) | collective-permute-done | bytes 1376288 | tf_op jit(solution)/shard_map/ppermute | solution.py:1451
  231.0 4.6 %collective-permute-done.18.refs_2_ = bf16[2,672,128]{2,1,0:T(8,128)(2,1)S(1)} collective-permute-done((bf16[2,672,128]{2,1,0:T(8,128)(2,1)}, bf16[2,672,128]{2,1,0:T(8,128)(2,1)S(1)}, u32[]{:S(2)}, u32[]{:S(2)}) %collective-permute-start.18) | collective-permute-done | bytes 344096 | tf_op jit(solution)/shard_map/ppermute | solution.py:1470
  246.1 5.1 %shard_map.198 = bf16[256,4096]{1,0:T(8,128)(2,1)} custom-call(s32[9]{0:T(128)S(1)} %stack.63.refs_0_, bf16[256,1024]{1,0:T(8,128)(2,1)} %get-tuple-element.205.refs_1_, f32[256,2048]{1,0:T(8,128)} %collective-permute-done.12.refs_6_.refs_2_, f32[256,2048]{1,0:T(8,128)} %get-tuple-element.175.refs_3_, bf16[1280,256]{1,0:T(8,128)(2,1)} %get-tuple-element.206.refs_4_, ...), custom_call_target="tpu_custom_call" | custom-call | flops 4499999744 | tf_op jit(solution)/shard_map/pallas_call | solution.py:112
  (162 shorter events, 114.7 us)
Async XLA Ops:
  0.6 28.3 %collective-permute-start.1 = (bf16[256,4096]{1,0:T(8,128)(2,1)}, bf16[256,4096]{1,0:T(8,128)(2,1)}, u32[]{:S(2)}, u32[]{:S(2)}) collective-permute-start(bf16[256,4096]{1,0:T(8,128)(2,1)} %bitcast.65), channel_id=1, source_target_pairs={{0,16},{16,0},{1,17},{17,1},{2,18},{18,2},{3,19},{19,3},{4,20},{20... | collective-permute-start | bytes 6291464 | tf_op jit(solution)/shard_map/ppermute | solution.py:1332
  1.1 27.8 %collective-permute-start.2 = (bf16[256,4096]{1,0:T(8,128)(2,1)}, bf16[256,4096]{1,0:T(8,128)(2,1)}, u32[]{:S(2)}, u32[]{:S(2)}) collective-permute-start(bf16[256,4096]{1,0:T(8,128)(2,1)} %bitcast.73), channel_id=1, source_target_pairs={{0,16},{16,0},{1,17},{17,1},{2,18},{18,2},{3,19},{19,3},{4,20},{20... | collective-permute-start | bytes 6291464 | tf_op jit(solution)/shard_map/ppermute | solution.py:1332
  6.1 16.4 %all-to-all-start = ((f32[32,4,128]{2,1,0:T(4,128)}), f32[32,4,128]{2,1,0:T(4,128)S(1)}, u32[]{:S(2)}, u32[]{:S(2)}) async-start(f32[32,4,128]{2,1,0:T(4,128)} %get-tuple-element.111.refs_3_), calls=%async_computation | async-start | bytes 131072 | tf_op jit(solution)/shard_map/all_to_all | solution.py:1327
  26.4 9.9 %all-to-all-start.1 = ((f32[32,4,128]{2,1,0:T(4,128)}), f32[32,4,128]{2,1,0:T(4,128)S(1)}, u32[]{:S(2)}, u32[]{:S(2)}) async-start(f32[32,4,128]{2,1,0:T(4,128)} %get-tuple-element.116.refs_5_), calls=%async_computation.1 | async-start | bytes 131072 | tf_op jit(solution)/shard_map/all_to_all | solution.py:1327
  40.3 10.8 %all-to-all-start.2 = ((f32[32,4,128]{2,1,0:T(4,128)}), f32[32,4,128]{2,1,0:T(4,128)S(1)}, u32[]{:S(2)}, u32[]{:S(2)}) async-start(f32[32,4,128]{2,1,0:T(4,128)} %get-tuple-element.121.refs_3_), calls=%async_computation.2 | async-start | bytes 131072 | tf_op jit(solution)/shard_map/all_to_all | solution.py:1327
  56.7 12.0 %all-to-all-start.3 = ((f32[32,4,128]{2,1,0:T(4,128)}), f32[32,4,128]{2,1,0:T(4,128)S(1)}, u32[]{:S(2)}, u32[]{:S(2)}) async-start(f32[32,4,128]{2,1,0:T(4,128)} %get-tuple-element.128.refs_4_), calls=%async_computation.3 | async-start | bytes 131072 | tf_op jit(solution)/shard_map/all_to_all | solution.py:1327
  71.8 13.8 %all-to-all-start.4 = ((bf16[32,32,128]{2,1,0:T(8,128)(2,1)}), bf16[32,32,128]{2,1,0:T(8,128)(2,1)S(1)}, u32[]{:S(2)}, u32[]{:S(2)}) async-start(bf16[32,32,128]{2,1,0:T(8,128)(2,1)} %get-tuple-element.134.refs_6_), calls=%async_computation.4 | async-start | bytes 524288 | tf_op jit(solution)/shard_map/all_to_all | solution.py:1327
  88.6 12.4 %all-to-all-start.5 = ((bf16[32,24,128]{2,1,0:T(8,128)(2,1)}), bf16[32,24,128]{2,1,0:T(8,128)(2,1)S(1)}, u32[]{:S(2)}, u32[]{:S(2)}) async-start(bf16[32,24,128]{2,1,0:T(8,128)(2,1)} %get-tuple-element.138), calls=%async_computation.5 | async-start | bytes 393216 | tf_op jit(solution)/shard_map/all_to_all | solution.py:1327
  107.7 12.4 %all-to-all-start.6 = ((bf16[32,24,128]{2,1,0:T(8,128)(2,1)}), bf16[32,24,128]{2,1,0:T(8,128)(2,1)S(1)}, u32[]{:S(2)}, u32[]{:S(2)}) async-start(bf16[32,24,128]{2,1,0:T(8,128)(2,1)} %get-tuple-element.144.refs_3_), calls=%async_computation.6 | async-start | bytes 393216 | tf_op jit(solution)/shard_map/all_to_all | solution.py:1327
  126.4 9.9 %all-to-all-start.7 = ((f32[32,4,128]{2,1,0:T(4,128)}), f32[32,4,128]{2,1,0:T(4,128)S(1)}, u32[]{:S(2)}, u32[]{:S(2)}) async-start(f32[32,4,128]{2,1,0:T(4,128)} %get-tuple-element.153.refs_6_), calls=%async_computation.7 | async-start | bytes 131072 | tf_op jit(solution)/shard_map/all_to_all | solution.py:1327
  128.9 20.1 %collective-permute-start.4 = (bf16[256,2048]{1,0:T(8,128)(2,1)}, bf16[256,2048]{1,0:T(8,128)(2,1)}, u32[]{:S(2)}, u32[]{:S(2)}) collective-permute-start(bf16[256,2048]{1,0:T(8,128)(2,1)} %get-tuple-element.151), channel_id=1, source_target_pairs={{0,16},{16,0},{1,17},{17,1},{2,18},{18,2},{3,19},{19,3},{4,20},{20... | collective-permute-start | bytes 3145736 | tf_op jit(solution)/shard_map/ppermute | solution.py:1332
  139.7 13.2 %all-to-all-start.8 = ((f32[32,4,128]{2,1,0:T(4,128)}), f32[32,4,128]{2,1,0:T(4,128)S(1)}, u32[]{:S(2)}, u32[]{:S(2)}) async-start(f32[32,4,128]{2,1,0:T(4,128)} %get-tuple-element.161.refs_2_), calls=%async_computation.8 | async-start | bytes 131072 | tf_op jit(solution)/shard_map/all_to_all | solution.py:1327
  145.6 24.9 %collective-permute-start.6 = (bf16[8976,128]{1,0:T(8,128)(2,1)}, bf16[8976,128]{1,0:T(8,128)(2,1)S(1)}, u32[]{:S(2)}, u32[]{:S(2)}) collective-permute-start(bf16[8976,128]{1,0:T(8,128)(2,1)} %get-tuple-element.178), channel_id=1, source_target_pairs={{0,16},{16,0},{1,17},{17,1},{2,18},{18,2},{3,19},{19,3},{4,20},{20... | collective-permute-start | bytes 6893576 | tf_op jit(solution)/shard_map/ppermute | solution.py:1332
  164.8 12.9 %all-to-all-start.9 = ((f32[32,4,128]{2,1,0:T(4,128)}), f32[32,4,128]{2,1,0:T(4,128)S(1)}, u32[]{:S(2)}, u32[]{:S(2)}) async-start(f32[32,4,128]{2,1,0:T(4,128)} %get-tuple-element.174.refs_7_), calls=%async_computation.9 | async-start | bytes 131072 | tf_op jit(solution)/shard_map/all_to_all | solution.py:1327
  182.8 19.1 %collective-permute-start.9 = (bf16[8,672,128]{2,1,0:T(8,128)(2,1)}, bf16[8,672,128]{2,1,0:T(8,128)(2,1)S(1)}, u32[]{:S(2)}, u32[]{:S(2)}) collective-permute-start(bf16[8,672,128]{2,1,0:T(8,128)(2,1)} %get-tuple-element.189), channel_id=1, source_target_pairs={{0,1},{1,0},{2,3},{3,2},{4,5},{5,4},{6,7},{7,6},{8,9},{9,8},{10,11... | collective-permute-start | bytes 4128776 | tf_op jit(solution)/shard_map/ppermute | solution.py:1451
  183.8 53.9 %collective-permute-start.12 = (f32[256,2048]{1,0:T(8,128)}, f32[256,2048]{1,0:T(8,128)}, u32[]{:S(2)}, u32[]{:S(2)}) collective-permute-start(f32[256,2048]{1,0:T(8,128)} %get-tuple-element.175.refs_3_), channel_id=1, source_target_pairs={{0,16},{16,0},{1,17},{17,1},{2,18},{18,2},{3,19},{19,3},{4,20},{20... | collective-permute-start | bytes 6291464 | tf_op jit(solution)/shard_map/ppermute | solution.py:1332
  183.9 20.9 %all-to-all-start.10 = ((f32[32,4,128]{2,1,0:T(4,128)}), f32[32,4,128]{2,1,0:T(4,128)S(1)}, u32[]{:S(2)}, u32[]{:S(2)}) async-start(f32[32,4,128]{2,1,0:T(4,128)} %get-tuple-element.184.refs_4_), calls=%async_computation.10 | async-start | bytes 131072 | tf_op jit(solution)/shard_map/all_to_all | solution.py:1327
  208.6 11.8 %collective-permute-start.11 = (bf16[4,672,128]{2,1,0:T(8,128)(2,1)}, bf16[4,672,128]{2,1,0:T(8,128)(2,1)S(1)}, u32[]{:S(2)}, u32[]{:S(2)}) collective-permute-start(bf16[4,672,128]{2,1,0:T(8,128)(2,1)} %get-tuple-element.197), channel_id=1, source_target_pairs={{0,2},{1,3},{2,0},{3,1},{4,6},{5,7},{6,4},{7,5},{8,10},{9,11},{10,... | collective-permute-start | bytes 2064392 | tf_op jit(solution)/shard_map/ppermute | solution.py:1460
  209.4 13.1 %all-to-all-start.11 = ((f32[32,4,128]{2,1,0:T(4,128)}), f32[32,4,128]{2,1,0:T(4,128)S(1)}, u32[]{:S(2)}, u32[]{:S(2)}) async-start(f32[32,4,128]{2,1,0:T(4,128)} %get-tuple-element.194.refs_4_), calls=%async_computation.11 | async-start | bytes 131072 | tf_op jit(solution)/shard_map/all_to_all | solution.py:1327
  213.0 9.5 %collective-permute-start.10 = (f32[256,512]{1,0:T(8,128)}, f32[256,512]{1,0:T(8,128)S(1)}, u32[]{:S(2)}, u32[]{:S(2)}) collective-permute-start(f32[256,512]{1,0:T(8,128)} %get-tuple-element.195.refs_4_), channel_id=1, source_target_pairs={{0,16},{16,0},{1,17},{17,1},{2,18},{18,2},{3,19},{19,3},{4,20},{20... | collective-permute-start | bytes 1572872 | tf_op jit(solution)/shard_map/ppermute | solution.py:1332
  213.3 27.0 %collective-permute-start.13 = (bf16[256,2048]{1,0:T(8,128)(2,1)}, bf16[256,2048]{1,0:T(8,128)(2,1)}, u32[]{:S(2)}, u32[]{:S(2)}) collective-permute-start(bf16[256,2048]{1,0:T(8,128)(2,1)} %get-tuple-element.207.refs_5_), channel_id=1, source_target_pairs={{0,16},{16,0},{1,17},{17,1},{2,18},{18,2},{3,19},{19,3},{4,20},{20... | collective-permute-start | bytes 3145736 | tf_op jit(solution)/shard_map/ppermute | solution.py:1332
  224.9 10.7 %collective-permute-start.18 = (bf16[2,672,128]{2,1,0:T(8,128)(2,1)}, bf16[2,672,128]{2,1,0:T(8,128)(2,1)S(1)}, u32[]{:S(2)}, u32[]{:S(2)}) collective-permute-start(bf16[2,672,128]{2,1,0:T(8,128)(2,1)} %get-tuple-element.210), channel_id=1, source_target_pairs={{0,4},{1,5},{2,6},{3,7},{4,0},{5,1},{6,2},{7,3},{8,12},{9,13},{10,... | collective-permute-start | bytes 1032200 | tf_op jit(solution)/shard_map/ppermute | solution.py:1470
  229.1 10.4 %collective-permute-start.17 = (bf16[208,128]{1,0:T(8,128)(2,1)}, bf16[208,128]{1,0:T(8,128)(2,1)S(1)}, u32[]{:S(2)}, u32[]{:S(2)}) collective-permute-start(bf16[208,128]{1,0:T(8,128)(2,1)} %shard_map.195.refs_3_.refs_0_), channel_id=1, source_target_pairs={{0,3},{1,2},{2,1},{3,0},{4,7},{5,6},{6,5},{7,4},{8,11},{9,10},{10,... | collective-permute-start | bytes 159752 | tf_op jit(solution)/shard_map/ppermute | solution.py:1475
  237.7 13.6 %collective-permute-start.19 = (bf16[1,672,128]{2,1,0:T(8,128)(2,1)}, bf16[1,672,128]{2,1,0:T(8,128)(2,1)S(1)}, u32[]{:S(2)}, u32[]{:S(2)}) collective-permute-start(bf16[1,672,128]{2,1,0:T(8,128)(2,1)} %get-tuple-element.212), channel_id=1, source_target_pairs={{0,8},{1,9},{2,10},{3,11},{4,12},{5,13},{6,14},{7,15},{8,0},{9,1},... | collective-permute-start | bytes 516104 | tf_op jit(solution)/shard_map/ppermute | solution.py:1473
  (38 other events, 237.8 us)

commit v5 on v4

--- a/solution.py
+++ b/solution.py
@@ -1377,7 +1377,7 @@
     x_other = swap(x)
     cot_other = swap(cot)
 
-    fa_lo, fa_hi, band, pay = net.fast_first(ints, x, w_fast_a.transpose(0, 2, 1), us=3.5)
+    fa_lo, fa_hi, band, pay = net.fast_first(ints, Far(x), Far(w_fast_a.transpose(0, 2, 1)), us=3.5)
     (fb_w, fbt_w, fc_w), tok = net.fast_weights(
         w_fast_b, w_fast_b.transpose(0, 2, 1), w_fast_c, us=1.0, after=[pay], token=True
     )
@@ -1392,7 +1392,7 @@
         ints, r, r1, fb, f2, fc_w, 1, 1, half, True, us=2.6, after=[tok]
     )
     fh2_other = swap(fh2_edge)
-    (pa, pp), tok = net.slow_start(xs, w_slow_a, w_slow_proj, us=3.5, after=[pay], token=True)
+    (pa, pp), tok = net.slow_start(xs, Far(w_slow_a), Far(w_slow_proj), us=3.5, after=[pay], token=True)
     r = exchange(pay)
     yf, lat, fc3, sa, pay = net.fast_finish(
         ints, r, r1, fh2, fh2_other, fc_w, xf, f3, wlat, pa, wa_lat, us=5.0, after=[tok]
@@ -1449,7 +1449,7 @@
         us=5.0, after=[tok], through=[there],
     )
     here = lax.ppermute(there, ("path", "dp"), plan.pairs(0))
-    dxs, tok = net.slow_input_grad(da, dp, w_slow_a, w_slow_proj, us=4.0, after=[pay], token=True)
+    dxs, tok = net.slow_input_grad(da, dp, Far(w_slow_a), Far(w_slow_proj), us=4.0, after=[pay], token=True)
     (keep, there), tok = net.halve(plan, ints, 1, keep, here, us=3.0, after=[tok], token=True)
     r = exchange(pay)
     (fdb, dn, u2, pay), (dxs_out, there) = net.conv_back(
@@ -1466,7 +1466,7 @@
     )
     bc_other = swap(bc)
     dxs_other = swap(dxs_out)
-    small = net.fast_small(ints, fda, x, bc, bc_other, us=3.0)
+    small = net.fast_small(ints, fda, Far(x), bc, bc_other, us=3.0, after=[fds_lo])
     here = lax.ppermute(there, ("path", "dp"), plan.pairs(2))
     for step in range(3, plan.bits):
         keep, there = net.halve(plan, ints, step, keep, here, us=2.5, after=[small])
@@ -1474,7 +1474,7 @@
     for k, masks in enumerate(plan.stages):
         parts = [small] + [lax.ppermute(small, ("path", "dp"), plan.route(m)) for m in masks]
         if k < len(plan.stages) - 1:
-            small = net.add(parts, us=1.0, after=[keep, dxs_other, fds_lo] if k == 0 else [])
+            small = net.add(parts, us=1.0, after=[keep] if k == 0 else [])
     dx = net.last(ints, fda, Far(fds_lo), fds, band, dxs_out, dxs_other, us=4.5, after=[small])
 
     vectors = jnp.concatenate([t1[2:4], t2[2:4], t3[8:24], t1[0:2], t2[0:2], t3[0:8], t3[0:8]], axis=0)

time: 255 us -> 252 us (0.988)
  local copies, waits for them, and re-layouts: 9.04 us -> 4.29 us
  Pallas kernels: 126 us -> 130 us
    unnamed x55 -> x43, local copies, waits for them, and re-layouts: 6.82 us -> 2.07 us
    pallas_call x34, Pallas kernels: 126 us -> 130 us  [call(): pl.pallas_call(wrapped, out_shape=shapes, grid=(1,) if cut else (), in_sp...]
  transfers between devices with their start and end apart: 35 -> 35, of which waited for: 14 -> 13; matrix products, arithmetic and copies ran while one was open for 1% -> 1% of each run, Pallas kernels for 36% -> 38%
where the time goes in v5:
time: 252 us; the launch traced here: 251 us
  Pallas kernels  130 us (52%)
  starting transfers between devices  61.6 us (24%)
  waiting for transfers between devices  53.2 us (21%)
  local copies, waits for them, and re-layouts  4.29 us (2%)
    pallas_call x34, Pallas kernels, call(): pl.pallas_call(wrapped, out_shape=shapes, grid=(1,) if cut else (), in_sp...  130 us
    all_to_all x12, starting transfers between devices, exchange(): return lax.all_to_all(x, ('path', 'dp'), 0, 0)  48.1 us
    all_to_all x12, waiting for transfers between devices, exchange(): return lax.all_to_all(x, ('path', 'dp'), 0, 0)  36.7 us
    ppermute x1, waiting for transfers between devices, local(): here = lax.ppermute(there, ('path', 'dp'), plan.pairs(0))  9.54 us
    ppermute x6, starting transfers between devices, local(): lax.ppermute(small, ('path', 'dp'), plan.route(m))  7.88 us
  transfers between devices with their start and end apart: 35, of which 13 were waited for; matrix products, arithmetic and copies ran while one was open for 1% of the time, Pallas kernels for 38%

profile of v5, /device:TPU:0, one launch (start us, length us, event | category | flops | bytes accessed | tf_op | source)
XLA Modules:
  0.0 250.9 jit_solution(4068979316075423106)
XLA Ops:
  4.9 9.1 %all-to-all-start = ((f32[32,4,128]{2,1,0:T(4,128)}), f32[32,4,128]{2,1,0:T(4,128)S(1)}, u32[]{:S(2)}, u32[]{:S(2)}) async-start(f32[32,4,128]{2,1,0:T(4,128)} %get-tuple-element.111.refs_3_), calls=%async_computation | async-start | bytes 131072 | tf_op jit(solution)/shard_map/all_to_all | solution.py:1327
  16.9 4.4 %all-to-all-done.refs_1_.refs_2_ = f32[32,4,128]{2,1,0:T(4,128)S(1)} async-done(((f32[32,4,128]{2,1,0:T(4,128)}), f32[32,4,128]{2,1,0:T(4,128)S(1)}, u32[]{:S(2)}, u32[]{:S(2)}) %all-to-all-start) | async-done | bytes 65568 | tf_op jit(solution)/shard_map/all_to_all | solution.py:1327
  27.8 4.9 %shard_map.169 = (bf16[256,2048]{1,0:T(8,128)(2,1)}, bf16[256,2304]{1,0:T(8,128)(2,1)}, bf16[256,2048]{1,0:T(8,128)(2,1)}, bf16[256,2048]{1,0:T(8,128)(2,1)}, f32[8,128]{1,0:T(8,128)}) custom-call(s32[9]{0:T(128)S(1)} %stack.63.refs_0_, bf16[256,4096]{1,0:T(8,128)(2,1)} %bitcast.72, bf16[256,4096]{1,0:T(8,128)(2,1)} %collective-permute-done.1.refs_2_, ...), custom_call_target="tpu_custom_call" | custom-call | flops 2500000000 | tf_op jit(solution)/shard_map/pallas_call | solution.py:112
  35.1 4.0 %shard_map.170 = (bf16[256,512]{1,0:T(8,128)(2,1)}, f32[8,128]{1,0:T(8,128)}, f32[32,4,128]{2,1,0:T(4,128)}, bf16[256,128]{1,0:T(8,128)(2,1)}) custom-call(s32[9]{0:T(128)S(1)} %stack.63.refs_0_, f32[32,4,128]{2,1,0:T(4,128)S(1)} %all-to-all-done.1.refs_1_, f32[32,4,128]{2,1,0:T(4,128)} %get-tuple-element.117.refs_2_.refs_3_.refs_1_, ...), custom_call_target="tpu_custom_call" | custom-call | flops 2600000000 | tf_op jit(solution)/shard_map/pallas_call | solution.py:112
  42.8 5.2 %shard_map.171 = (f32[256,512]{1,0:T(8,128)}, f32[256,2048]{1,0:T(8,128)}, f32[8,128]{1,0:T(8,128)}) custom-call(bf16[256,2048]{1,0:T(8,128)(2,1)} %get-tuple-element.125.refs_0_.refs_1_, bf16[1280,256]{1,0:T(8,128)(2,1)} %refs_2_.5, bf16[1280,1024]{1,0:T(8,128)(2,1)} %refs_3_.3, f32[32,4,128]{2,1,0:T(4,128)} %get-tuple-element.121.refs_3_), custom_call_target="tpu_custom_call" | custom-call | flops 3500000000 | tf_op jit(solution)/shard_map/pallas_call | solution.py:112
  49.8 5.6 %shard_map.172 = (bf16[256,2304]{1,0:T(8,128)(2,1)}, bf16[256,512]{1,0:T(8,128)(2,1)}, f32[8,128]{1,0:T(8,128)}, f32[256,512]{1,0:T(8,128)}, f32[32,4,128]{2,1,0:T(4,128)}) custom-call(s32[9]{0:T(128)S(1)} %stack.63.refs_0_, f32[32,4,128]{2,1,0:T(4,128)S(1)} %all-to-all-done.2.refs_1_, f32[32,4,128]{2,1,0:T(4,128)} %get-tuple-element.117.refs_2_.refs_3_.refs_1_, ...), custom_call_target="tpu_custom_call" | custom-call | flops 5000000000 | tf_op jit(solution)/shard_map/pallas_call | solution.py:112
  55.4 3.9 %all-to-all-start.3 = ((f32[32,4,128]{2,1,0:T(4,128)}), f32[32,4,128]{2,1,0:T(4,128)S(1)}, u32[]{:S(2)}, u32[]{:S(2)}) async-start(f32[32,4,128]{2,1,0:T(4,128)} %get-tuple-element.128.refs_4_), calls=%async_computation.3 | async-start | bytes 131072 | tf_op jit(solution)/shard_map/all_to_all | solution.py:1327
  59.3 4.0 %shard_map.173 = (f32[256,2048]{1,0:T(8,128)}, f32[16,128]{1,0:T(8,128)}, f32[8,128]{1,0:T(8,128)}) custom-call(s32[9]{0:T(128)S(1)} %stack.63.refs_0_, f32[256,2048]{1,0:T(8,128)} %get-tuple-element.130.refs_1_, bf16[256,512]{1,0:T(8,128)(2,1)} %get-tuple-element.131.refs_2_, bf16[1280,1024]{1,0:T(8,128)(2,1)} %refs_3_.3, ...), custom_call_target="tpu_custom_call" | custom-call | flops 3000000000 | tf_op jit(solution)/shard_map/pallas_call | solution.py:112
  72.5 5.1 %shard_map.175 = (f32[256,2048]{1,0:T(8,128)}, f32[8,128]{1,0:T(8,128)}) custom-call(s32[9]{0:T(128)S(1)} %stack.63.refs_0_, bf16[256,512]{1,0:T(8,128)(2,1)} %get-tuple-element.122.refs_3_.refs_1_.refs_7_.refs_4_.refs_2_, bf16[256,1024]{1,0:T(8,128)(2,1)} %get-tuple-element.119.refs_5_.refs_2_.refs_8_, ...), custom_call_target="tpu_custom_call" | custom-call | flops 4000000000 | tf_op jit(solution)/shard_map/pallas_call | solution.py:112
  77.6 6.1 %all-to-all-done.4.refs_1_.refs_2_ = bf16[32,32,128]{2,1,0:T(8,128)(2,1)S(1)} async-done(((bf16[32,32,128]{2,1,0:T(8,128)(2,1)}), bf16[32,32,128]{2,1,0:T(8,128)(2,1)S(1)}, u32[]{:S(2)}, u32[]{:S(2)}) %all-to-all-start.4) | async-done | bytes 262176 | tf_op jit(solution)/shard_map/all_to_all | solution.py:1327
  89.5 9.6 %all-to-all-done.5.refs_1_ = bf16[32,24,128]{2,1,0:T(8,128)(2,1)S(1)} async-done(((bf16[32,24,128]{2,1,0:T(8,128)(2,1)}), bf16[32,24,128]{2,1,0:T(8,128)(2,1)S(1)}, u32[]{:S(2)}, u32[]{:S(2)}) %all-to-all-start.5) | async-done | bytes 196640 | tf_op jit(solution)/shard_map/all_to_all | solution.py:1327
  99.1 6.8 %shard_map.177 = (bf16[256,2048]{1,0:T(8,128)(2,1)}, f32[256,2048]{1,0:T(8,128)}, f32[16,128]{1,0:T(8,128)}, f32[16,128]{1,0:T(8,128)}, bf16[32,24,128]{2,1,0:T(8,128)(2,1)}) custom-call(s32[9]{0:T(128)S(1)} %stack.63.refs_0_, bf16[32,24,128]{2,1,0:T(8,128)(2,1)S(1)} %all-to-all-done.5.refs_1_, bf16[32,32,128]{2,1,0:T(8,128)(2,1)S(1)} %all-to-all-done.4.refs_1_.refs_2_, ...), custom_call_target="tpu_custom_call" | custom-call | flops 6000000000 | tf_op jit(solution)/shard_map/pallas_call | solution.py:112
  111.8 6.4 %all-to-all-done.6.refs_2_ = bf16[32,24,128]{2,1,0:T(8,128)(2,1)S(1)} async-done(((bf16[32,24,128]{2,1,0:T(8,128)(2,1)}), bf16[32,24,128]{2,1,0:T(8,128)(2,1)S(1)}, u32[]{:S(2)}, u32[]{:S(2)}) %all-to-all-start.6) | async-done | bytes 196640 | tf_op jit(solution)/shard_map/all_to_all | solution.py:1327
  118.2 6.2 %shard_map.179 = (bf16[256,2048]{1,0:T(8,128)(2,1)}, bf16[256,2048]{1,0:T(8,128)(2,1)}, f32[256,512]{1,0:T(8,128)}, f32[24,128]{1,0:T(8,128)}, f32[32,4,128]{2,1,0:T(4,128)}, /*index=5*/bf16[256,2048]{1,0:T(8,128)(2,1)}) custom-call(s32[9]{0:T(128)S(1)} %stack.63.refs_0_, ...), custom_call_target="tpu_custom_call", output_to_operand_aliasing={{5}: (15, {})} | custom-call | flops 6000000000 | tf_op jit(solution)/shard_map/pallas_call | solution.py:112
  127.1 7.1 %shard_map.180 = (bf16[8976,128]{1,0:T(8,128)(2,1)}, bf16[8976,128]{1,0:T(8,128)(2,1)}, f32[8,128]{1,0:T(8,128)}) custom-call(s32[9]{0:T(128)S(1)} %stack.63.refs_0_, bf16[256,2048]{1,0:T(8,128)(2,1)} %get-tuple-element.125.refs_0_.refs_1_, bf16[256,512]{1,0:T(8,128)(2,1)} %get-tuple-element.131.refs_2_, ...), custom_call_target="tpu_custom_call" | custom-call | flops 6000000000 | tf_op jit(solution)/shard_map/pallas_call | solution.py:112
  137.8 5.8 %all-to-all-start.8 = ((f32[32,4,128]{2,1,0:T(4,128)}), f32[32,4,128]{2,1,0:T(4,128)S(1)}, u32[]{:S(2)}, u32[]{:S(2)}) async-start(f32[32,4,128]{2,1,0:T(4,128)} %get-tuple-element.161.refs_2_), calls=%async_computation.8 | async-start | bytes 131072 | tf_op jit(solution)/shard_map/all_to_all | solution.py:1327
  154.0 4.1 %shard_map.185 = (bf16[2560,128]{1,0:T(8,128)(2,1)}, bf16[2560,128]{1,0:T(8,128)(2,1)}, f32[8,128]{1,0:T(8,128)}) custom-call(s32[9]{0:T(128)S(1)} %stack.63.refs_0_, bf16[256,2048]{1,0:T(8,128)(2,1)} %get-tuple-element.125.refs_0_.refs_1_, bf16[256,512]{1,0:T(8,128)(2,1)} %get-tuple-element.131.refs_2_, ...), custom_call_target="tpu_custom_call" | custom-call | flops 4000000000 | tf_op jit(solution)/shard_map/pallas_call | solution.py:112
  158.1 4.3 %shard_map.186 = (f32[256,2048]{1,0:T(8,128)}, f32[32,4,128]{2,1,0:T(4,128)}, bf16[4608,128]{1,0:T(8,128)(2,1)}, bf16[2560,128]{1,0:T(8,128)(2,1)}) custom-call(s32[9]{0:T(128)S(1)} %stack.63.refs_0_, bf16[256,256]{1,0:T(8,128)(2,1)} %get-tuple-element.167.refs_5_.refs_1_, ...), custom_call_target="tpu_custom_call", output_to_operand_aliasing={{2}: (10, {}), {3}: (11, {})} | custom-call | flops 4000000000 | tf_op jit(solution)/shard_map/pallas_call | solution.py:112
  162.9 5.6 %all-to-all-start.9 = ((f32[32,4,128]{2,1,0:T(4,128)}), f32[32,4,128]{2,1,0:T(4,128)S(1)}, u32[]{:S(2)}, u32[]{:S(2)}) async-start(f32[32,4,128]{2,1,0:T(4,128)} %get-tuple-element.174.refs_7_), calls=%async_computation.9 | async-start | bytes 131072 | tf_op jit(solution)/shard_map/all_to_all | solution.py:1327
  168.5 5.2 %shard_map.187 = (bf16[8,672,128]{2,1,0:T(8,128)(2,1)}, bf16[8,672,128]{2,1,0:T(8,128)(2,1)}, f32[8,128]{1,0:T(8,128)}) custom-call(s32[9]{0:T(128)S(1)} %stack.63.refs_0_, bf16[8976,128]{1,0:T(8,128)(2,1)} %get-tuple-element.177.refs_1_, bf16[8976,128]{1,0:T(8,128)(2,1)S(1)} %collective-permute-done.6.refs_2_, ...), custom_call_target="tpu_custom_call" | custom-call | flops 6000000000 | tf_op jit(solution)/shard_map/pallas_call | solution.py:112
  175.8 5.0 %shard_map.188 = (bf16[256,2048]{1,0:T(8,128)(2,1)}, f32[256,512]{1,0:T(8,128)}, f32[4,128]{1,0:T(4,128)}, f32[32,4,128]{2,1,0:T(4,128)}, bf16[8,672,128]{2,1,0:T(8,128)(2,1)}) custom-call(s32[9]{0:T(128)S(1)} %stack.63.refs_0_, f32[32,4,128]{2,1,0:T(4,128)} %get-tuple-element.117.refs_2_.refs_3_.refs_1_, ...), custom_call_target="tpu_custom_call", output_to_operand_aliasing={{4}: (12, {})} | custom-call | flops 5000000000 | tf_op jit(solution)/shard_map/pallas_call | solution.py:112
  185.5 4.9 %shard_map.189 = (bf16[256,2048]{1,0:T(8,128)(2,1)}, f32[8,128]{1,0:T(8,128)}) custom-call(bf16[256,512]{1,0:T(8,128)(2,1)} %get-tuple-element.172.refs_3_.refs_0_, bf16[256,2048]{1,0:T(8,128)(2,1)} %get-tuple-element.156.refs_3_.refs_7_.refs_1_, bf16[1280,256]{1,0:T(8,128)(2,1)} %refs_2_.5, bf16[1280,1024]{1,0:T(8,128)(2,1)} %refs_3_.3, ...), custom_call_target="tpu_custom_call" | custom-call | flops 4000000000 | tf_op jit(solution)/shard_map/pallas_call | solution.py:112
  190.4 9.5 %collective-permute-done.9.refs_2_ = bf16[8,672,128]{2,1,0:T(8,128)(2,1)S(1)} collective-permute-done((bf16[8,672,128]{2,1,0:T(8,128)(2,1)}, bf16[8,672,128]{2,1,0:T(8,128)(2,1)S(1)}, u32[]{:S(2)}, u32[]{:S(2)}) %collective-permute-start.9) | collective-permute-done | bytes 1376288 | tf_op jit(solution)/shard_map/ppermute | solution.py:1451
  242.6 5.1 %shard_map.198 = bf16[256,4096]{1,0:T(8,128)(2,1)} custom-call(s32[9]{0:T(128)S(1)} %stack.63.refs_0_, bf16[256,1024]{1,0:T(8,128)(2,1)} %get-tuple-element.205.refs_1_, f32[256,2048]{1,0:T(8,128)} %collective-permute-done.12.refs_5_.refs_2_, f32[256,2048]{1,0:T(8,128)} %get-tuple-element.175.refs_3_, bf16[1280,256]{1,0:T(8,128)(2,1)} %get-tuple-element.206.refs_4_, ...), custom_call_target="tpu_custom_call" | custom-call | flops 4499999744 | tf_op jit(solution)/shard_map/pallas_call | solution.py:112
  (150 shorter events, 111.3 us)
Async XLA Ops:
  0.6 27.1 %collective-permute-start.1 = (bf16[256,4096]{1,0:T(8,128)(2,1)}, bf16[256,4096]{1,0:T(8,128)(2,1)}, u32[]{:S(2)}, u32[]{:S(2)}) collective-permute-start(bf16[256,4096]{1,0:T(8,128)(2,1)} %bitcast.70), channel_id=1, source_target_pairs={{0,16},{16,0},{1,17},{17,1},{2,18},{18,2},{3,19},{19,3},{4,20},{20... | collective-permute-start | bytes 6291464 | tf_op jit(solution)/shard_map/ppermute | solution.py:1332
  1.1 26.6 %collective-permute-start.2 = (bf16[256,4096]{1,0:T(8,128)(2,1)}, bf16[256,4096]{1,0:T(8,128)(2,1)}, u32[]{:S(2)}, u32[]{:S(2)}) collective-permute-start(bf16[256,4096]{1,0:T(8,128)(2,1)} %bitcast.68), channel_id=1, source_target_pairs={{0,16},{16,0},{1,17},{17,1},{2,18},{18,2},{3,19},{19,3},{4,20},{20... | collective-permute-start | bytes 6291464 | tf_op jit(solution)/shard_map/ppermute | solution.py:1332
  4.9 16.4 %all-to-all-start = ((f32[32,4,128]{2,1,0:T(4,128)}), f32[32,4,128]{2,1,0:T(4,128)S(1)}, u32[]{:S(2)}, u32[]{:S(2)}) async-start(f32[32,4,128]{2,1,0:T(4,128)} %get-tuple-element.111.refs_3_), calls=%async_computation | async-start | bytes 131072 | tf_op jit(solution)/shard_map/all_to_all | solution.py:1327
  25.2 9.9 %all-to-all-start.1 = ((f32[32,4,128]{2,1,0:T(4,128)}), f32[32,4,128]{2,1,0:T(4,128)S(1)}, u32[]{:S(2)}, u32[]{:S(2)}) async-start(f32[32,4,128]{2,1,0:T(4,128)} %get-tuple-element.116.refs_5_), calls=%async_computation.1 | async-start | bytes 131072 | tf_op jit(solution)/shard_map/all_to_all | solution.py:1327
  39.0 10.8 %all-to-all-start.2 = ((f32[32,4,128]{2,1,0:T(4,128)}), f32[32,4,128]{2,1,0:T(4,128)S(1)}, u32[]{:S(2)}, u32[]{:S(2)}) async-start(f32[32,4,128]{2,1,0:T(4,128)} %get-tuple-element.121.refs_3_), calls=%async_computation.2 | async-start | bytes 131072 | tf_op jit(solution)/shard_map/all_to_all | solution.py:1327
  55.4 11.2 %all-to-all-start.3 = ((f32[32,4,128]{2,1,0:T(4,128)}), f32[32,4,128]{2,1,0:T(4,128)S(1)}, u32[]{:S(2)}, u32[]{:S(2)}) async-start(f32[32,4,128]{2,1,0:T(4,128)} %get-tuple-element.128.refs_4_), calls=%async_computation.3 | async-start | bytes 131072 | tf_op jit(solution)/shard_map/all_to_all | solution.py:1327
  69.9 13.8 %all-to-all-start.4 = ((bf16[32,32,128]{2,1,0:T(8,128)(2,1)}), bf16[32,32,128]{2,1,0:T(8,128)(2,1)S(1)}, u32[]{:S(2)}, u32[]{:S(2)}) async-start(bf16[32,32,128]{2,1,0:T(8,128)(2,1)} %get-tuple-element.134.refs_6_), calls=%async_computation.4 | async-start | bytes 524288 | tf_op jit(solution)/shard_map/all_to_all | solution.py:1327
  86.7 12.4 %all-to-all-start.5 = ((bf16[32,24,128]{2,1,0:T(8,128)(2,1)}), bf16[32,24,128]{2,1,0:T(8,128)(2,1)S(1)}, u32[]{:S(2)}, u32[]{:S(2)}) async-start(bf16[32,24,128]{2,1,0:T(8,128)(2,1)} %get-tuple-element.138), calls=%async_computation.5 | async-start | bytes 393216 | tf_op jit(solution)/shard_map/all_to_all | solution.py:1327
  105.8 12.4 %all-to-all-start.6 = ((bf16[32,24,128]{2,1,0:T(8,128)(2,1)}), bf16[32,24,128]{2,1,0:T(8,128)(2,1)S(1)}, u32[]{:S(2)}, u32[]{:S(2)}) async-start(bf16[32,24,128]{2,1,0:T(8,128)(2,1)} %get-tuple-element.144.refs_3_), calls=%async_computation.6 | async-start | bytes 393216 | tf_op jit(solution)/shard_map/all_to_all | solution.py:1327
  124.4 9.9 %all-to-all-start.7 = ((f32[32,4,128]{2,1,0:T(4,128)}), f32[32,4,128]{2,1,0:T(4,128)S(1)}, u32[]{:S(2)}, u32[]{:S(2)}) async-start(f32[32,4,128]{2,1,0:T(4,128)} %get-tuple-element.153.refs_6_), calls=%async_computation.7 | async-start | bytes 131072 | tf_op jit(solution)/shard_map/all_to_all | solution.py:1327
  127.0 20.1 %collective-permute-start.4 = (bf16[256,2048]{1,0:T(8,128)(2,1)}, bf16[256,2048]{1,0:T(8,128)(2,1)}, u32[]{:S(2)}, u32[]{:S(2)}) collective-permute-start(bf16[256,2048]{1,0:T(8,128)(2,1)} %get-tuple-element.151), channel_id=1, source_target_pairs={{0,16},{16,0},{1,17},{17,1},{2,18},{18,2},{3,19},{19,3},{4,20},{20... | collective-permute-start | bytes 3145736 | tf_op jit(solution)/shard_map/ppermute | solution.py:1332
  137.8 13.2 %all-to-all-start.8 = ((f32[32,4,128]{2,1,0:T(4,128)}), f32[32,4,128]{2,1,0:T(4,128)S(1)}, u32[]{:S(2)}, u32[]{:S(2)}) async-start(f32[32,4,128]{2,1,0:T(4,128)} %get-tuple-element.161.refs_2_), calls=%async_computation.8 | async-start | bytes 131072 | tf_op jit(solution)/shard_map/all_to_all | solution.py:1327
  143.6 24.9 %collective-permute-start.6 = (bf16[8976,128]{1,0:T(8,128)(2,1)}, bf16[8976,128]{1,0:T(8,128)(2,1)S(1)}, u32[]{:S(2)}, u32[]{:S(2)}) collective-permute-start(bf16[8976,128]{1,0:T(8,128)(2,1)} %get-tuple-element.178), channel_id=1, source_target_pairs={{0,16},{16,0},{1,17},{17,1},{2,18},{18,2},{3,19},{19,3},{4,20},{20... | collective-permute-start | bytes 6893576 | tf_op jit(solution)/shard_map/ppermute | solution.py:1332
  162.9 12.9 %all-to-all-start.9 = ((f32[32,4,128]{2,1,0:T(4,128)}), f32[32,4,128]{2,1,0:T(4,128)S(1)}, u32[]{:S(2)}, u32[]{:S(2)}) async-start(f32[32,4,128]{2,1,0:T(4,128)} %get-tuple-element.174.refs_7_), calls=%async_computation.9 | async-start | bytes 131072 | tf_op jit(solution)/shard_map/all_to_all | solution.py:1327
  180.8 19.1 %collective-permute-start.9 = (bf16[8,672,128]{2,1,0:T(8,128)(2,1)}, bf16[8,672,128]{2,1,0:T(8,128)(2,1)S(1)}, u32[]{:S(2)}, u32[]{:S(2)}) collective-permute-start(bf16[8,672,128]{2,1,0:T(8,128)(2,1)} %get-tuple-element.189), channel_id=1, source_target_pairs={{0,1},{1,0},{2,3},{3,2},{4,5},{5,4},{6,7},{7,6},{8,9},{9,8},{10,11... | collective-permute-start | bytes 4128776 | tf_op jit(solution)/shard_map/ppermute | solution.py:1451
  181.8 42.7 %collective-permute-start.12 = (f32[256,2048]{1,0:T(8,128)}, f32[256,2048]{1,0:T(8,128)}, u32[]{:S(2)}, u32[]{:S(2)}) collective-permute-start(f32[256,2048]{1,0:T(8,128)} %get-tuple-element.175.refs_3_), channel_id=1, source_target_pairs={{0,16},{16,0},{1,17},{17,1},{2,18},{18,2},{3,19},{19,3},{4,20},{20... | collective-permute-start | bytes 6291464 | tf_op jit(solution)/shard_map/ppermute | solution.py:1332
  181.9 20.9 %all-to-all-start.10 = ((f32[32,4,128]{2,1,0:T(4,128)}), f32[32,4,128]{2,1,0:T(4,128)S(1)}, u32[]{:S(2)}, u32[]{:S(2)}) async-start(f32[32,4,128]{2,1,0:T(4,128)} %get-tuple-element.184.refs_4_), calls=%async_computation.10 | async-start | bytes 131072 | tf_op jit(solution)/shard_map/all_to_all | solution.py:1327
  206.6 11.8 %collective-permute-start.11 = (bf16[4,672,128]{2,1,0:T(8,128)(2,1)}, bf16[4,672,128]{2,1,0:T(8,128)(2,1)S(1)}, u32[]{:S(2)}, u32[]{:S(2)}) collective-permute-start(bf16[4,672,128]{2,1,0:T(8,128)(2,1)} %get-tuple-element.197), channel_id=1, source_target_pairs={{0,2},{1,3},{2,0},{3,1},{4,6},{5,7},{6,4},{7,5},{8,10},{9,11},{10,... | collective-permute-start | bytes 2064392 | tf_op jit(solution)/shard_map/ppermute | solution.py:1460
  207.5 13.1 %all-to-all-start.11 = ((f32[32,4,128]{2,1,0:T(4,128)}), f32[32,4,128]{2,1,0:T(4,128)S(1)}, u32[]{:S(2)}, u32[]{:S(2)}) async-start(f32[32,4,128]{2,1,0:T(4,128)} %get-tuple-element.194.refs_4_), calls=%async_computation.11 | async-start | bytes 131072 | tf_op jit(solution)/shard_map/all_to_all | solution.py:1327
  211.0 9.6 %collective-permute-start.10 = (f32[256,512]{1,0:T(8,128)}, f32[256,512]{1,0:T(8,128)S(1)}, u32[]{:S(2)}, u32[]{:S(2)}) collective-permute-start(f32[256,512]{1,0:T(8,128)} %get-tuple-element.195.refs_4_), channel_id=1, source_target_pairs={{0,16},{16,0},{1,17},{17,1},{2,18},{18,2},{3,19},{19,3},{4,20},{20... | collective-permute-start | bytes 1572872 | tf_op jit(solution)/shard_map/ppermute | solution.py:1332
  211.3 30.3 %collective-permute-start.13 = (bf16[256,2048]{1,0:T(8,128)(2,1)}, bf16[256,2048]{1,0:T(8,128)(2,1)S(1)}, u32[]{:S(2)}, u32[]{:S(2)}) collective-permute-start(bf16[256,2048]{1,0:T(8,128)(2,1)} %get-tuple-element.207.refs_5_), channel_id=1, source_target_pairs={{0,16},{16,0},{1,17},{17,1},{2,18},{18,2},{3,19},{19,3},{4,20},{20... | collective-permute-start | bytes 3145736 | tf_op jit(solution)/shard_map/ppermute | solution.py:1332
  222.8 10.7 %collective-permute-start.18 = (bf16[2,672,128]{2,1,0:T(8,128)(2,1)}, bf16[2,672,128]{2,1,0:T(8,128)(2,1)S(1)}, u32[]{:S(2)}, u32[]{:S(2)}) collective-permute-start(bf16[2,672,128]{2,1,0:T(8,128)(2,1)} %get-tuple-element.210), channel_id=1, source_target_pairs={{0,4},{1,5},{2,6},{3,7},{4,0},{5,1},{6,2},{7,3},{8,12},{9,13},{10,... | collective-permute-start | bytes 1032200 | tf_op jit(solution)/shard_map/ppermute | solution.py:1470
  236.8 11.0 %collective-permute-start.22 = (bf16[208,128]{1,0:T(8,128)(2,1)}, bf16[208,128]{1,0:T(8,128)(2,1)S(1)}, u32[]{:S(2)}, u32[]{:S(2)}) collective-permute-start(bf16[208,128]{1,0:T(8,128)(2,1)} %shard_map.197.refs_7_.refs_5_), channel_id=1, source_target_pairs={{0,12},{1,13},{2,14},{3,15},{4,8},{5,9},{6,10},{7,11},{8,4},{9,5},... | collective-permute-start | bytes 159752 | tf_op jit(solution)/shard_map/ppermute | solution.py:1475
  238.2 9.6 %collective-permute-start.21 = (bf16[208,128]{1,0:T(8,128)(2,1)}, bf16[208,128]{1,0:T(8,128)(2,1)S(1)}, u32[]{:S(2)}, u32[]{:S(2)}) collective-permute-start(bf16[208,128]{1,0:T(8,128)(2,1)} %shard_map.197.refs_7_.refs_5_), channel_id=1, source_target_pairs={{0,8},{1,9},{2,10},{3,11},{4,12},{5,13},{6,14},{7,15},{8,0},{9,1},... | collective-permute-start | bytes 159752 | tf_op jit(solution)/shard_map/ppermute | solution.py:1475
  (32 other events, 221.2 us)

commit v6 on v5

--- a/solution.py
+++ b/solution.py
@@ -1420,17 +1420,16 @@
         plan, ints, xs, lat, dp, sh2, dc, us=6.0, after=[pay], token=True
     )
     r = exchange(pay)
-    (db, dn, t2, pay), (early_out,) = net.conv_back(
-        ints, r1, r, dn, sb, sc2, s2, wbt3, sa, sc1, s1, 2, TS // 2, us=3.0, after=[tok], through=[early_out]
+    db, dn, t2, pay = net.conv_back(
+        ints, r1, r, dn, sb, sc2, s2, wbt3, sa, sc1, s1, 2, TS // 2, us=3.0, after=[tok]
     )
-    early_in = swap(early_out)
     conv, tok = net.grads_conv(sh1, db, us=3.0, after=[pay], token=True)
-    out, tok = net.out_join(ints, ys, yf, theirs, us=3.0, after=[tok], token=True)
     r = exchange(pay)
-    (da, dl0, dl1, t1), (conv_out,) = net.slow_last(
-        ints, r1, r, dn, sa, sc1, s1, dp, wa_lat, wp_lat, us=3.0, after=[tok], through=[conv]
+    (da, dl0, dl1, t1), (conv_out, early_out) = net.slow_last(
+        ints, r1, r, dn, sa, sc1, s1, dp, wa_lat, wp_lat, us=3.0, after=[tok], through=[conv, early_out]
     )
     dl_other = swap(dl0)
+    early_in = swap(early_out)
     (late, late_out), tok = net.grads_late(ints, xs, lat, da, yf, dl0, dl1, us=4.0, token=True)
 
     (fds, pay), (conv_out, late_out) = net.fast_top(
@@ -1450,6 +1449,7 @@
     )
     here = lax.ppermute(there, ("path", "dp"), plan.pairs(0))
     dxs, tok = net.slow_input_grad(da, dp, Far(w_slow_a), Far(w_slow_proj), us=4.0, after=[pay], token=True)
+    out, tok = net.out_join(ints, ys, yf, theirs, us=3.0, after=[tok], token=True)
     (keep, there), tok = net.halve(plan, ints, 1, keep, here, us=3.0, after=[tok], token=True)
     r = exchange(pay)
     (fdb, dn, u2, pay), (dxs_out, there) = net.conv_back(

time: 252 us -> 251 us (level)
  starting transfers between devices: 61.6 us -> 59 us
    all_to_all x12, starting transfers between devices: 48.1 us -> 42.7 us  [exchange(): return lax.all_to_all(x, ('path', 'dp'), 0, 0)]
    ppermute x1, waiting for transfers between devices: 9.54 us -> 4.77 us  [local(): here = lax.ppermute(there, ('path', 'dp'), plan.pairs(0))]
    all_to_all x12, waiting for transfers between devices: 36.7 us -> 40.3 us  [exchange(): return lax.all_to_all(x, ('path', 'dp'), 0, 0)]
  transfers between devices with their start and end apart: 35 -> 35, of which waited for: 13 -> 16; matrix products, arithmetic and copies ran while one was open for 1% -> 1% of each run, Pallas kernels for 38% -> 35%
where the time goes in v6:
time: 251 us; the launch traced here: 249 us
  Pallas kernels  130 us (52%)
  starting transfers between devices  59 us (24%)
  waiting for transfers between devices  53.5 us (21%)
  local copies, waits for them, and re-layouts  5.2 us (2%)
    pallas_call x34, Pallas kernels, call(): pl.pallas_call(wrapped, out_shape=shapes, grid=(1,) if cut else (), in_sp...  130 us
    all_to_all x12, starting transfers between devices, exchange(): return lax.all_to_all(x, ('path', 'dp'), 0, 0)  42.7 us
    all_to_all x12, waiting for transfers between devices, exchange(): return lax.all_to_all(x, ('path', 'dp'), 0, 0)  40.3 us
    ppermute x6, starting transfers between devices, local(): lax.ppermute(small, ('path', 'dp'), plan.route(m))  7.87 us
    ppermute x13, starting transfers between devices, swap(): return lax.ppermute(x, 'path', SWAP)  5.04 us
  transfers between devices with their start and end apart: 35, of which 16 were waited for; matrix products, arithmetic and copies ran while one was open for 1% of the time, Pallas kernels for 35%

profile of v6, /device:TPU:0, one launch (start us, length us, event | category | flops | bytes accessed | tf_op | source)
XLA Modules:
  0.0 249.3 jit_solution(3322226371334433384)
XLA Ops:
  7.4 6.9 %all-to-all-start = ((f32[32,4,128]{2,1,0:T(4,128)}), f32[32,4,128]{2,1,0:T(4,128)S(1)}, u32[]{:S(2)}, u32[]{:S(2)}) async-start(f32[32,4,128]{2,1,0:T(4,128)} %get-tuple-element.111.refs_3_), calls=%async_computation | async-start | bytes 131072 | tf_op jit(solution)/shard_map/all_to_all | solution.py:1327
  17.0 4.7 %all-to-all-done.refs_1_.refs_2_ = f32[32,4,128]{2,1,0:T(4,128)S(1)} async-done(((f32[32,4,128]{2,1,0:T(4,128)}), f32[32,4,128]{2,1,0:T(4,128)S(1)}, u32[]{:S(2)}, u32[]{:S(2)}) %all-to-all-start) | async-done | bytes 65568 | tf_op jit(solution)/shard_map/all_to_all | solution.py:1327
  28.1 4.8 %shard_map.169 = (bf16[256,2048]{1,0:T(8,128)(2,1)}, bf16[256,2304]{1,0:T(8,128)(2,1)}, bf16[256,2048]{1,0:T(8,128)(2,1)}, bf16[256,2048]{1,0:T(8,128)(2,1)}, f32[8,128]{1,0:T(8,128)}) custom-call(s32[9]{0:T(128)S(1)} %stack.63.refs_0_, bf16[256,4096]{1,0:T(8,128)(2,1)} %bitcast.72, bf16[256,4096]{1,0:T(8,128)(2,1)} %collective-permute-done.1.refs_2_, ...), custom_call_target="tpu_custom_call" | custom-call | flops 2500000000 | tf_op jit(solution)/shard_map/pallas_call | solution.py:112
  35.4 4.0 %shard_map.170 = (bf16[256,512]{1,0:T(8,128)(2,1)}, f32[8,128]{1,0:T(8,128)}, f32[32,4,128]{2,1,0:T(4,128)}, bf16[256,128]{1,0:T(8,128)(2,1)}) custom-call(s32[9]{0:T(128)S(1)} %stack.63.refs_0_, f32[32,4,128]{2,1,0:T(4,128)S(1)} %all-to-all-done.1.refs_1_, f32[32,4,128]{2,1,0:T(4,128)} %get-tuple-element.117.refs_2_.refs_3_.refs_1_, ...), custom_call_target="tpu_custom_call" | custom-call | flops 2600000000 | tf_op jit(solution)/shard_map/pallas_call | solution.py:112
  43.0 5.2 %shard_map.171 = (f32[256,512]{1,0:T(8,128)}, f32[256,2048]{1,0:T(8,128)}, f32[8,128]{1,0:T(8,128)}) custom-call(bf16[256,2048]{1,0:T(8,128)(2,1)} %get-tuple-element.125.refs_0_.refs_1_, bf16[1280,256]{1,0:T(8,128)(2,1)} %refs_2_.5, bf16[1280,1024]{1,0:T(8,128)(2,1)} %refs_3_.3, f32[32,4,128]{2,1,0:T(4,128)} %get-tuple-element.121.refs_3_), custom_call_target="tpu_custom_call" | custom-call | flops 3500000000 | tf_op jit(solution)/shard_map/pallas_call | solution.py:112
  50.3 5.6 %shard_map.172 = (bf16[256,2304]{1,0:T(8,128)(2,1)}, bf16[256,512]{1,0:T(8,128)(2,1)}, f32[8,128]{1,0:T(8,128)}, f32[256,512]{1,0:T(8,128)}, f32[32,4,128]{2,1,0:T(4,128)}) custom-call(s32[9]{0:T(128)S(1)} %stack.63.refs_0_, f32[32,4,128]{2,1,0:T(4,128)S(1)} %all-to-all-done.2.refs_1_, f32[32,4,128]{2,1,0:T(4,128)} %get-tuple-element.117.refs_2_.refs_3_.refs_1_, ...), custom_call_target="tpu_custom_call" | custom-call | flops 5000000000 | tf_op jit(solution)/shard_map/pallas_call | solution.py:112
  59.6 4.0 %shard_map.173 = (f32[256,2048]{1,0:T(8,128)}, f32[16,128]{1,0:T(8,128)}, f32[8,128]{1,0:T(8,128)}) custom-call(s32[9]{0:T(128)S(1)} %stack.63.refs_0_, f32[256,2048]{1,0:T(8,128)} %get-tuple-element.130.refs_1_, bf16[256,512]{1,0:T(8,128)(2,1)} %get-tuple-element.131.refs_2_, bf16[1280,1024]{1,0:T(8,128)(2,1)} %refs_3_.3, ...), custom_call_target="tpu_custom_call" | custom-call | flops 3000000000 | tf_op jit(solution)/shard_map/pallas_call | solution.py:112
  72.8 5.1 %shard_map.175 = (f32[256,2048]{1,0:T(8,128)}, f32[8,128]{1,0:T(8,128)}) custom-call(s32[9]{0:T(128)S(1)} %stack.63.refs_0_, bf16[256,512]{1,0:T(8,128)(2,1)} %get-tuple-element.122.refs_3_.refs_1_.refs_7_.refs_4_.refs_2_, bf16[256,1024]{1,0:T(8,128)(2,1)} %get-tuple-element.119.refs_5_.refs_2_.refs_8_, ...), custom_call_target="tpu_custom_call" | custom-call | flops 4000000000 | tf_op jit(solution)/shard_map/pallas_call | solution.py:112
  77.9 6.1 %all-to-all-done.4.refs_1_.refs_2_ = bf16[32,32,128]{2,1,0:T(8,128)(2,1)S(1)} async-done(((bf16[32,32,128]{2,1,0:T(8,128)(2,1)}), bf16[32,32,128]{2,1,0:T(8,128)(2,1)S(1)}, u32[]{:S(2)}, u32[]{:S(2)}) %all-to-all-start.4) | async-done | bytes 262176 | tf_op jit(solution)/shard_map/all_to_all | solution.py:1327
  89.7 9.6 %all-to-all-done.5.refs_1_ = bf16[32,24,128]{2,1,0:T(8,128)(2,1)S(1)} async-done(((bf16[32,24,128]{2,1,0:T(8,128)(2,1)}), bf16[32,24,128]{2,1,0:T(8,128)(2,1)S(1)}, u32[]{:S(2)}, u32[]{:S(2)}) %all-to-all-start.5) | async-done | bytes 196640 | tf_op jit(solution)/shard_map/all_to_all | solution.py:1327
  99.3 6.8 %shard_map.177 = (bf16[256,2048]{1,0:T(8,128)(2,1)}, f32[256,2048]{1,0:T(8,128)}, f32[16,128]{1,0:T(8,128)}, f32[16,128]{1,0:T(8,128)}, bf16[32,24,128]{2,1,0:T(8,128)(2,1)}) custom-call(s32[9]{0:T(128)S(1)} %stack.63.refs_0_, bf16[32,24,128]{2,1,0:T(8,128)(2,1)S(1)} %all-to-all-done.5.refs_1_, bf16[32,32,128]{2,1,0:T(8,128)(2,1)S(1)} %all-to-all-done.4.refs_1_.refs_2_, ...), custom_call_target="tpu_custom_call" | custom-call | flops 6000000000 | tf_op jit(solution)/shard_map/pallas_call | solution.py:112
  112.1 6.4 %all-to-all-done.6.refs_2_ = bf16[32,24,128]{2,1,0:T(8,128)(2,1)S(1)} async-done(((bf16[32,24,128]{2,1,0:T(8,128)(2,1)}), bf16[32,24,128]{2,1,0:T(8,128)(2,1)S(1)}, u32[]{:S(2)}, u32[]{:S(2)}) %all-to-all-start.6) | async-done | bytes 196640 | tf_op jit(solution)/shard_map/all_to_all | solution.py:1327
  118.5 6.2 %shard_map.179 = (bf16[256,2048]{1,0:T(8,128)(2,1)}, bf16[256,2048]{1,0:T(8,128)(2,1)}, f32[256,512]{1,0:T(8,128)}, f32[24,128]{1,0:T(8,128)}, f32[32,4,128]{2,1,0:T(4,128)}, /*index=5*/bf16[256,2048]{1,0:T(8,128)(2,1)}) custom-call(s32[9]{0:T(128)S(1)} %stack.63.refs_0_, ...), custom_call_target="tpu_custom_call", output_to_operand_aliasing={{5}: (15, {})} | custom-call | flops 6000000000 | tf_op jit(solution)/shard_map/pallas_call | solution.py:112
  127.3 7.1 %shard_map.180 = (bf16[8976,128]{1,0:T(8,128)(2,1)}, bf16[8976,128]{1,0:T(8,128)(2,1)}, f32[8,128]{1,0:T(8,128)}) custom-call(s32[9]{0:T(128)S(1)} %stack.63.refs_0_, bf16[256,2048]{1,0:T(8,128)(2,1)} %get-tuple-element.125.refs_0_.refs_1_, bf16[256,512]{1,0:T(8,128)(2,1)} %get-tuple-element.131.refs_2_, ...), custom_call_target="tpu_custom_call" | custom-call | flops 6000000000 | tf_op jit(solution)/shard_map/pallas_call | solution.py:112
  138.1 5.6 %all-to-all-start.8 = ((f32[32,4,128]{2,1,0:T(4,128)}), f32[32,4,128]{2,1,0:T(4,128)S(1)}, u32[]{:S(2)}, u32[]{:S(2)}) async-start(f32[32,4,128]{2,1,0:T(4,128)} %get-tuple-element.158.refs_2_), calls=%async_computation.8 | async-start | bytes 131072 | tf_op jit(solution)/shard_map/all_to_all | solution.py:1327
  146.8 4.2 %all-to-all-done.8.refs_2_ = f32[32,4,128]{2,1,0:T(4,128)S(1)} async-done(((f32[32,4,128]{2,1,0:T(4,128)}), f32[32,4,128]{2,1,0:T(4,128)S(1)}, u32[]{:S(2)}, u32[]{:S(2)}) %all-to-all-start.8) | async-done | bytes 65568 | tf_op jit(solution)/shard_map/all_to_all | solution.py:1327
  154.6 4.0 %shard_map.184 = (bf16[2560,128]{1,0:T(8,128)(2,1)}, bf16[2560,128]{1,0:T(8,128)(2,1)}, f32[8,128]{1,0:T(8,128)}) custom-call(s32[9]{0:T(128)S(1)} %stack.63.refs_0_, bf16[256,2048]{1,0:T(8,128)(2,1)} %get-tuple-element.125.refs_0_.refs_1_, bf16[256,512]{1,0:T(8,128)(2,1)} %get-tuple-element.131.refs_2_, ...), custom_call_target="tpu_custom_call" | custom-call | flops 4000000000 | tf_op jit(solution)/shard_map/pallas_call | solution.py:112
  158.9 4.3 %shard_map.185 = (f32[256,2048]{1,0:T(8,128)}, f32[32,4,128]{2,1,0:T(4,128)}, bf16[4608,128]{1,0:T(8,128)(2,1)}, bf16[2560,128]{1,0:T(8,128)(2,1)}) custom-call(s32[9]{0:T(128)S(1)} %stack.63.refs_0_, bf16[256,256]{1,0:T(8,128)(2,1)} %get-tuple-element.166.refs_5_.refs_1_, ...), custom_call_target="tpu_custom_call", output_to_operand_aliasing={{2}: (10, {}), {3}: (11, {})} | custom-call | flops 4000000000 | tf_op jit(solution)/shard_map/pallas_call | solution.py:112
  167.2 5.2 %shard_map.186 = (bf16[8,672,128]{2,1,0:T(8,128)(2,1)}, bf16[8,672,128]{2,1,0:T(8,128)(2,1)}, f32[8,128]{1,0:T(8,128)}) custom-call(s32[9]{0:T(128)S(1)} %stack.63.refs_0_, bf16[8976,128]{1,0:T(8,128)(2,1)} %get-tuple-element.175.refs_1_, bf16[8976,128]{1,0:T(8,128)(2,1)S(1)} %collective-permute-done.6.refs_2_, ...), custom_call_target="tpu_custom_call" | custom-call | flops 6000000000 | tf_op jit(solution)/shard_map/pallas_call | solution.py:112
  173.6 5.0 %shard_map.187 = (bf16[256,2048]{1,0:T(8,128)(2,1)}, f32[256,512]{1,0:T(8,128)}, f32[4,128]{1,0:T(4,128)}, f32[32,4,128]{2,1,0:T(4,128)}, bf16[8,672,128]{2,1,0:T(8,128)(2,1)}) custom-call(s32[9]{0:T(128)S(1)} %stack.63.refs_0_, f32[32,4,128]{2,1,0:T(4,128)} %get-tuple-element.117.refs_2_.refs_3_.refs_1_, ...), custom_call_target="tpu_custom_call", output_to_operand_aliasing={{4}: (12, {})} | custom-call | flops 5000000000 | tf_op jit(solution)/shard_map/pallas_call | solution.py:112
  183.7 4.9 %shard_map.188 = (bf16[256,2048]{1,0:T(8,128)(2,1)}, f32[8,128]{1,0:T(8,128)}) custom-call(bf16[256,512]{1,0:T(8,128)(2,1)} %get-tuple-element.165.refs_3_.refs_0_, bf16[256,2048]{1,0:T(8,128)(2,1)} %get-tuple-element.155.refs_3_.refs_7_.refs_1_, bf16[1280,256]{1,0:T(8,128)(2,1)} %refs_2_.5, bf16[1280,1024]{1,0:T(8,128)(2,1)} %refs_3_.3, ...), custom_call_target="tpu_custom_call" | custom-call | flops 4000000000 | tf_op jit(solution)/shard_map/pallas_call | solution.py:112
  192.9 4.8 %collective-permute-done.9.refs_2_ = bf16[8,672,128]{2,1,0:T(8,128)(2,1)S(1)} collective-permute-done((bf16[8,672,128]{2,1,0:T(8,128)(2,1)}, bf16[8,672,128]{2,1,0:T(8,128)(2,1)S(1)}, u32[]{:S(2)}, u32[]{:S(2)}) %collective-permute-start.9) | collective-permute-done | bytes 1376288 | tf_op jit(solution)/shard_map/ppermute | solution.py:1450
  200.5 3.8 %shard_map.191 = (bf16[256,512]{1,0:T(8,128)(2,1)}, f32[256,512]{1,0:T(8,128)}, f32[4,128]{1,0:T(4,128)}, f32[32,4,128]{2,1,0:T(4,128)}, bf16[256,2048]{1,0:T(8,128)(2,1)}, /*index=5*/bf16[4,672,128]{2,1,0:T(8,128)(2,1)}) custom-call(s32[9]{0:T(128)S(1)} %stack.63.refs_0_, ...), custom_call_target="tpu_custom_call", output_to_operand_aliasing={{4}: (13, {}), {5}: (14, {})} | custom-call | flops 4000000000 | tf_op jit(solution)/shard_map/pallas_call | solution.py:112
  240.9 5.1 %shard_map.198 = bf16[256,4096]{1,0:T(8,128)(2,1)} custom-call(s32[9]{0:T(128)S(1)} %stack.63.refs_0_, bf16[256,1024]{1,0:T(8,128)(2,1)} %get-tuple-element.205.refs_1_, f32[256,2048]{1,0:T(8,128)} %collective-permute-done.12.refs_5_.refs_2_, f32[256,2048]{1,0:T(8,128)} %get-tuple-element.173.refs_3_, bf16[1280,256]{1,0:T(8,128)(2,1)} %get-tuple-element.206.refs_4_, ...), custom_call_target="tpu_custom_call" | custom-call | flops 4499999744 | tf_op jit(solution)/shard_map/pallas_call | solution.py:112
  (152 shorter events, 118.2 us)
Async XLA Ops:
  0.6 27.5 %collective-permute-start.1 = (bf16[256,4096]{1,0:T(8,128)(2,1)}, bf16[256,4096]{1,0:T(8,128)(2,1)}, u32[]{:S(2)}, u32[]{:S(2)}) collective-permute-start(bf16[256,4096]{1,0:T(8,128)(2,1)} %bitcast.70), channel_id=1, source_target_pairs={{0,16},{16,0},{1,17},{17,1},{2,18},{18,2},{3,19},{19,3},{4,20},{20... | collective-permute-start | bytes 6291464 | tf_op jit(solution)/shard_map/ppermute | solution.py:1332
  1.1 27.0 %collective-permute-start.2 = (bf16[256,4096]{1,0:T(8,128)(2,1)}, bf16[256,4096]{1,0:T(8,128)(2,1)}, u32[]{:S(2)}, u32[]{:S(2)}) collective-permute-start(bf16[256,4096]{1,0:T(8,128)(2,1)} %bitcast.68), channel_id=1, source_target_pairs={{0,16},{16,0},{1,17},{17,1},{2,18},{18,2},{3,19},{19,3},{4,20},{20... | collective-permute-start | bytes 6291464 | tf_op jit(solution)/shard_map/ppermute | solution.py:1332
  4.9 16.8 %collective-permute-start = (f32[256,512]{1,0:T(8,128)}, f32[256,512]{1,0:T(8,128)S(1)}, u32[]{:S(2)}, u32[]{:S(2)}) collective-permute-start(f32[256,512]{1,0:T(8,128)} %get-tuple-element.114.refs_5_), channel_id=1, source_target_pairs={{0,16},{16,0},{1,17},{17,1},{2,18},{18,2},{3,19},{19,3},{4,20},{20... | collective-permute-start | bytes 1572872 | tf_op jit(solution)/shard_map/ppermute | solution.py:1332
  7.4 14.3 %all-to-all-start = ((f32[32,4,128]{2,1,0:T(4,128)}), f32[32,4,128]{2,1,0:T(4,128)S(1)}, u32[]{:S(2)}, u32[]{:S(2)}) async-start(f32[32,4,128]{2,1,0:T(4,128)} %get-tuple-element.111.refs_3_), calls=%async_computation | async-start | bytes 131072 | tf_op jit(solution)/shard_map/all_to_all | solution.py:1327
  25.5 9.9 %all-to-all-start.1 = ((f32[32,4,128]{2,1,0:T(4,128)}), f32[32,4,128]{2,1,0:T(4,128)S(1)}, u32[]{:S(2)}, u32[]{:S(2)}) async-start(f32[32,4,128]{2,1,0:T(4,128)} %get-tuple-element.116.refs_5_), calls=%async_computation.1 | async-start | bytes 131072 | tf_op jit(solution)/shard_map/all_to_all | solution.py:1327
  39.4 10.9 %all-to-all-start.2 = ((f32[32,4,128]{2,1,0:T(4,128)}), f32[32,4,128]{2,1,0:T(4,128)S(1)}, u32[]{:S(2)}, u32[]{:S(2)}) async-start(f32[32,4,128]{2,1,0:T(4,128)} %get-tuple-element.121.refs_3_), calls=%async_computation.2 | async-start | bytes 131072 | tf_op jit(solution)/shard_map/all_to_all | solution.py:1327
  55.9 11.0 %all-to-all-start.3 = ((f32[32,4,128]{2,1,0:T(4,128)}), f32[32,4,128]{2,1,0:T(4,128)S(1)}, u32[]{:S(2)}, u32[]{:S(2)}) async-start(f32[32,4,128]{2,1,0:T(4,128)} %get-tuple-element.128.refs_4_), calls=%async_computation.3 | async-start | bytes 131072 | tf_op jit(solution)/shard_map/all_to_all | solution.py:1327
  70.2 13.8 %all-to-all-start.4 = ((bf16[32,32,128]{2,1,0:T(8,128)(2,1)}), bf16[32,32,128]{2,1,0:T(8,128)(2,1)S(1)}, u32[]{:S(2)}, u32[]{:S(2)}) async-start(bf16[32,32,128]{2,1,0:T(8,128)(2,1)} %get-tuple-element.134.refs_6_), calls=%async_computation.4 | async-start | bytes 524288 | tf_op jit(solution)/shard_map/all_to_all | solution.py:1327
  86.9 12.4 %all-to-all-start.5 = ((bf16[32,24,128]{2,1,0:T(8,128)(2,1)}), bf16[32,24,128]{2,1,0:T(8,128)(2,1)S(1)}, u32[]{:S(2)}, u32[]{:S(2)}) async-start(bf16[32,24,128]{2,1,0:T(8,128)(2,1)} %get-tuple-element.138), calls=%async_computation.5 | async-start | bytes 393216 | tf_op jit(solution)/shard_map/all_to_all | solution.py:1327
  106.1 12.4 %all-to-all-start.6 = ((bf16[32,24,128]{2,1,0:T(8,128)(2,1)}), bf16[32,24,128]{2,1,0:T(8,128)(2,1)S(1)}, u32[]{:S(2)}, u32[]{:S(2)}) async-start(bf16[32,24,128]{2,1,0:T(8,128)(2,1)} %get-tuple-element.144.refs_3_), calls=%async_computation.6 | async-start | bytes 393216 | tf_op jit(solution)/shard_map/all_to_all | solution.py:1327
  124.7 9.9 %all-to-all-start.7 = ((f32[32,4,128]{2,1,0:T(4,128)}), f32[32,4,128]{2,1,0:T(4,128)S(1)}, u32[]{:S(2)}, u32[]{:S(2)}) async-start(f32[32,4,128]{2,1,0:T(4,128)} %get-tuple-element.152.refs_6_), calls=%async_computation.7 | async-start | bytes 131072 | tf_op jit(solution)/shard_map/all_to_all | solution.py:1327
  138.1 13.0 %all-to-all-start.8 = ((f32[32,4,128]{2,1,0:T(4,128)}), f32[32,4,128]{2,1,0:T(4,128)S(1)}, u32[]{:S(2)}, u32[]{:S(2)}) async-start(f32[32,4,128]{2,1,0:T(4,128)} %get-tuple-element.158.refs_2_), calls=%async_computation.8 | async-start | bytes 131072 | tf_op jit(solution)/shard_map/all_to_all | solution.py:1327
  154.1 13.1 %collective-permute-start.6 = (bf16[8976,128]{1,0:T(8,128)(2,1)}, bf16[8976,128]{1,0:T(8,128)(2,1)S(1)}, u32[]{:S(2)}, u32[]{:S(2)}) collective-permute-start(bf16[8976,128]{1,0:T(8,128)(2,1)} %get-tuple-element.176), channel_id=1, source_target_pairs={{0,16},{16,0},{1,17},{17,1},{2,18},{18,2},{3,19},{19,3},{4,20},{20... | collective-permute-start | bytes 6893576 | tf_op jit(solution)/shard_map/ppermute | solution.py:1332
  163.7 9.9 %all-to-all-start.9 = ((f32[32,4,128]{2,1,0:T(4,128)}), f32[32,4,128]{2,1,0:T(4,128)S(1)}, u32[]{:S(2)}, u32[]{:S(2)}) async-start(f32[32,4,128]{2,1,0:T(4,128)} %get-tuple-element.172.refs_7_), calls=%async_computation.9 | async-start | bytes 131072 | tf_op jit(solution)/shard_map/all_to_all | solution.py:1327
  178.5 19.1 %collective-permute-start.9 = (bf16[8,672,128]{2,1,0:T(8,128)(2,1)}, bf16[8,672,128]{2,1,0:T(8,128)(2,1)S(1)}, u32[]{:S(2)}, u32[]{:S(2)}) collective-permute-start(bf16[8,672,128]{2,1,0:T(8,128)(2,1)} %get-tuple-element.189), channel_id=1, source_target_pairs={{0,1},{1,0},{2,3},{3,2},{4,5},{5,4},{6,7},{7,6},{8,9},{9,8},{10,11... | collective-permute-start | bytes 4128776 | tf_op jit(solution)/shard_map/ppermute | solution.py:1450
  179.5 42.6 %collective-permute-start.12 = (f32[256,2048]{1,0:T(8,128)}, f32[256,2048]{1,0:T(8,128)}, u32[]{:S(2)}, u32[]{:S(2)}) collective-permute-start(f32[256,2048]{1,0:T(8,128)} %get-tuple-element.173.refs_3_), channel_id=1, source_target_pairs={{0,16},{16,0},{1,17},{17,1},{2,18},{18,2},{3,19},{19,3},{4,20},{20... | collective-permute-start | bytes 6291464 | tf_op jit(solution)/shard_map/ppermute | solution.py:1332
  180.1 20.4 %all-to-all-start.10 = ((f32[32,4,128]{2,1,0:T(4,128)}), f32[32,4,128]{2,1,0:T(4,128)S(1)}, u32[]{:S(2)}, u32[]{:S(2)}) async-start(f32[32,4,128]{2,1,0:T(4,128)} %get-tuple-element.182.refs_4_), calls=%async_computation.10 | async-start | bytes 131072 | tf_op jit(solution)/shard_map/all_to_all | solution.py:1327
  204.3 11.8 %collective-permute-start.11 = (bf16[4,672,128]{2,1,0:T(8,128)(2,1)}, bf16[4,672,128]{2,1,0:T(8,128)(2,1)S(1)}, u32[]{:S(2)}, u32[]{:S(2)}) collective-permute-start(bf16[4,672,128]{2,1,0:T(8,128)(2,1)} %get-tuple-element.197), channel_id=1, source_target_pairs={{0,2},{1,3},{2,0},{3,1},{4,6},{5,7},{6,4},{7,5},{8,10},{9,11},{10,... | collective-permute-start | bytes 2064392 | tf_op jit(solution)/shard_map/ppermute | solution.py:1460
  205.2 13.1 %collective-permute-start.10 = (f32[256,512]{1,0:T(8,128)}, f32[256,512]{1,0:T(8,128)S(1)}, u32[]{:S(2)}, u32[]{:S(2)}) collective-permute-start(f32[256,512]{1,0:T(8,128)} %get-tuple-element.195.refs_4_), channel_id=1, source_target_pairs={{0,16},{16,0},{1,17},{17,1},{2,18},{18,2},{3,19},{19,3},{4,20},{20... | collective-permute-start | bytes 1572872 | tf_op jit(solution)/shard_map/ppermute | solution.py:1332
  205.2 13.1 %all-to-all-start.11 = ((f32[32,4,128]{2,1,0:T(4,128)}), f32[32,4,128]{2,1,0:T(4,128)S(1)}, u32[]{:S(2)}, u32[]{:S(2)}) async-start(f32[32,4,128]{2,1,0:T(4,128)} %get-tuple-element.194.refs_4_), calls=%async_computation.11 | async-start | bytes 131072 | tf_op jit(solution)/shard_map/all_to_all | solution.py:1327
  208.8 31.1 %collective-permute-start.13 = (bf16[256,2048]{1,0:T(8,128)(2,1)}, bf16[256,2048]{1,0:T(8,128)(2,1)S(1)}, u32[]{:S(2)}, u32[]{:S(2)}) collective-permute-start(bf16[256,2048]{1,0:T(8,128)(2,1)} %get-tuple-element.207.refs_5_), channel_id=1, source_target_pairs={{0,16},{16,0},{1,17},{17,1},{2,18},{18,2},{3,19},{19,3},{4,20},{20... | collective-permute-start | bytes 3145736 | tf_op jit(solution)/shard_map/ppermute | solution.py:1332
  220.5 10.7 %collective-permute-start.18 = (bf16[2,672,128]{2,1,0:T(8,128)(2,1)}, bf16[2,672,128]{2,1,0:T(8,128)(2,1)S(1)}, u32[]{:S(2)}, u32[]{:S(2)}) collective-permute-start(bf16[2,672,128]{2,1,0:T(8,128)(2,1)} %get-tuple-element.210), channel_id=1, source_target_pairs={{0,4},{1,5},{2,6},{3,7},{4,0},{5,1},{6,2},{7,3},{8,12},{9,13},{10,... | collective-permute-start | bytes 1032200 | tf_op jit(solution)/shard_map/ppermute | solution.py:1470
  234.5 11.6 %collective-permute-start.20 = (bf16[208,128]{1,0:T(8,128)(2,1)}, bf16[208,128]{1,0:T(8,128)(2,1)S(1)}, u32[]{:S(2)}, u32[]{:S(2)}) collective-permute-start(bf16[208,128]{1,0:T(8,128)(2,1)} %shard_map.197.refs_7_.refs_5_), channel_id=1, source_target_pairs={{0,4},{1,5},{2,6},{3,7},{4,0},{5,1},{6,2},{7,3},{8,12},{9,13},{10,... | collective-permute-start | bytes 159752 | tf_op jit(solution)/shard_map/ppermute | solution.py:1475
  235.0 11.0 %collective-permute-start.21 = (bf16[208,128]{1,0:T(8,128)(2,1)}, bf16[208,128]{1,0:T(8,128)(2,1)S(1)}, u32[]{:S(2)}, u32[]{:S(2)}) collective-permute-start(bf16[208,128]{1,0:T(8,128)(2,1)} %shard_map.197.refs_7_.refs_5_), channel_id=1, source_target_pairs={{0,8},{1,9},{2,10},{3,11},{4,12},{5,13},{6,14},{7,15},{8,0},{9,1},... | collective-permute-start | bytes 159752 | tf_op jit(solution)/shard_map/ppermute | solution.py:1475
  (33 other events, 226.5 us)
